TPU v7x, 768 devices: a whole 4x8x12 slice. The times are simulated.
768 devices in a mesh: tx: 96 (over y, z), ty: 8 (over x, core).
Axes of the slice: x: 4, y: 8, z: 12, core: 2. Of those that a mesh axis runs over, the one named last changes fastest.
Arguments:
- state: bfloat16 [786432, 128], P(('tx', 'ty')), may hold values from -6 to 6
- departures: bfloat16 [147456, 256], P(('tx', 'ty')), may hold values from -6 to 6
- stencil: int32 [147456, 4], P(('tx', 'ty')), may hold values from 0 to 1023, as said below
- bilinear: bfloat16 [147456, 4], P(('tx', 'ty')), may hold values from 0 to 1, as said below
- counts: int32 [73728], P(('tx', 'ty')), may hold values from 0 to 2, as said below
- predictors: float32 [8, 147456], P(None, ('tx', 'ty')), may hold values from -6 to 6
- w_in: bfloat16 [128, 512], replicated, may hold values from -0.5 to 0.5
- b_in: float32 [512], replicated, may hold values from -3 to 3
- w_mid: bfloat16 [512, 512], replicated, may hold values from -0.25 to 0.25
- b_mid: float32 [512], replicated, may hold values from -3 to 3
- w_out: bfloat16 [512, 256], replicated, may hold values from -0.25 to 0.25
- b_out: float32 [256], replicated, may hold values from -4 to 4
Outputs:
- radiance: bfloat16 [147456, 256], P(('tx', 'ty'))
- state_grad: float32 [786432, 128], P(('tx', 'ty'))
- bias_grad: float32 [8, 256], replicated
Inputs may be any that keep to these rules, and one draw needn't show every extreme that they name: `stencil`: the four entries are c, c + 1, c + 32, c + 33 for a corner c of the owner's 32 x 32 tile. Nonnegative bilinear weights of two fractions; the four sum to one up to rounding. Only the first counts slots of each block of 2 are live. In every draw one tx index receives 2 live slots from every holder.
All inputs are finite; a program needn't handle non-finite values.
Results may differ from a plain program's by a relative error of at most 0.0075.
Values may be sent and summed in bfloat16 or wider, within the bound.
No kernel may reach another device: no remote copies, remote signals or barrier semaphores. Data moves between devices by JAX's collectives and lax.ppermute only.
A program may use at most 32 MiB of HBM per device.

v0:
```python
import math

import jax
import jax.numpy as jnp
from jax import lax
from jax.sharding import PartitionSpec as P


def interpolate(state, stencil, bilinear):
    profile = jnp.zeros((stencil.shape[0], state.shape[1]), jnp.float32)
    for k in range(4):
        rows = jnp.take(state, stencil[:, k], axis=0)
        profile = profile + bilinear[:, k : k + 1].astype(jnp.float32) * rows.astype(jnp.float32)
    return profile.astype(jnp.bfloat16)


def network_pass(profile, cotangent, w_in, b_in, w_mid, b_mid, w_out, b_out):
    h1 = jnp.tanh(jnp.dot(profile, w_in, preferred_element_type=jnp.float32) + b_in).astype(
        jnp.bfloat16
    )
    h2 = jnp.tanh(jnp.dot(h1, w_mid, preferred_element_type=jnp.float32) + b_mid).astype(
        jnp.bfloat16
    )
    radiance = (jnp.dot(h2, w_out, preferred_element_type=jnp.float32) + b_out).astype(jnp.bfloat16)
    h2f = h2.astype(jnp.float32)
    h1f = h1.astype(jnp.float32)
    back_dims = (((1,), (1,)), ((), ()))
    g2 = lax.dot_general(cotangent, w_out, back_dims, preferred_element_type=jnp.float32)
    g2 = (g2 * (1.0 - h2f * h2f)).astype(jnp.bfloat16)
    g1 = lax.dot_general(g2, w_mid, back_dims, preferred_element_type=jnp.float32)
    g1 = (g1 * (1.0 - h1f * h1f)).astype(jnp.bfloat16)
    dprofile = lax.dot_general(g1, w_in, back_dims, preferred_element_type=jnp.float32).astype(
        jnp.bfloat16
    )
    return (radiance, dprofile)


def accumulate(stencil, bilinear, dprofile, columns):
    places = jnp.arange(columns, dtype=jnp.int32)
    spread = jnp.zeros((stencil.shape[0], columns), jnp.float32)
    for k in range(4):
        spread = spread + jnp.where(
            stencil[:, k : k + 1] == places[None, :],
            bilinear[:, k : k + 1].astype(jnp.float32),
            0.0,
        )
    return lax.dot_general(
        spread,
        dprofile.astype(jnp.float32),
        (((0,), (0,)), ((), ())),
        precision=lax.Precision.HIGHEST,
    )


def on_device(
    state, departures, stencil, bilinear, counts, predictors, w_in, b_in, w_mid, b_mid, w_out, b_out
):
    slots = departures.shape[0]
    peers = lax.axis_size("tx")
    cap = slots // peers
    slot = jnp.arange(slots, dtype=jnp.int32)
    live = slot % cap < jnp.take(counts, slot // cap)
    dy = jnp.where(live[:, None], departures, jnp.zeros_like(departures))
    total_slots = slots * peers * lax.axis_size("ty")
    partial_terms = jnp.dot(predictors, dy.astype(jnp.float32), precision=lax.Precision.HIGHEST)
    bias_grad = lax.psum(partial_terms, ("tx", "ty")) * (1.0 / math.sqrt(total_slots))
    got_dy, got_stencil, got_weights = (
        lax.all_to_all(dy, "tx", split_axis=0, concat_axis=0, tiled=True),
        lax.all_to_all(stencil, "tx", split_axis=0, concat_axis=0, tiled=True),
        lax.all_to_all(bilinear, "tx", split_axis=0, concat_axis=0, tiled=True),
    )
    profile = interpolate(state, got_stencil, got_weights)
    computed, dprofile = network_pass(profile, got_dy, w_in, b_in, w_mid, b_mid, w_out, b_out)
    radiance = lax.all_to_all(computed, "tx", split_axis=0, concat_axis=0, tiled=True)
    state_grad = accumulate(got_stencil, got_weights, dprofile, state.shape[0])
    return (radiance, state_grad, bias_grad)


def solution(mesh):
    placed = (
        P(("tx", "ty"), None),
        P(("tx", "ty"), None),
        P(("tx", "ty"), None),
        P(("tx", "ty"), None),
        P(("tx", "ty")),
        P(None, ("tx", "ty")),
        P(),
        P(),
        P(),
        P(),
        P(),
        P(),
    )
    return jax.shard_map(
        on_device,
        mesh=mesh,
        in_specs=placed,
        out_specs=(P(("tx", "ty"), None), P(("tx", "ty"), None), P()),
        check_vma=False,
    )
```

profile of v0, /device:TPU:1, one launch (start us, length us, event | category | flops | bytes accessed | tf_op | source)
XLA Modules:
  0.0 205.9 jit_solution(13415737674991173348)
XLA Ops:
  0.6 0.0 copy-start
  0.6 1.5 copy.17
  2.1 22.5 %all-to-all-start = ((bf16[96,2,4]{2,1,0:T(2,128)(2,1)}), bf16[96,2,4]{2,1,0:T(2,128)(2,1)S(1)}, u32[]{:S(2)}, u32[]{:S(2)}) async-start(bf16[96,2,4]{2,1,0:T(2,128)(2,1)} %bitcast), calls=%async_computation | async-start | bytes 98304 | tf_op jit(solution)/shard_map/all_to_all | solution.py:70
  24.7 0.0 copy-start.1
  24.7 0.6 copy-done.1
  25.4 0.0 copy-start.4
  25.4 1.5 gather_fusion
  26.9 0.0 copy-done.4
  26.9 0.0 copy-start.5
  27.0 0.1 broadcast_select_fusion
  27.1 0.6 copy-done.5
  27.6 0.1 convolution_bitcast_fusion
  27.8 110.8 %psum.7 = f32[8,256]{1,0:T(8,128)S(1)} all-reduce(f32[8,256]{1,0:T(8,128)S(1)} %convolution_bitcast_fusion), channel_id=1, replica_groups=mesh['tx'=96,'ty'=8] {'tx','ty'}, use_global_device_ids=true, to_apply=%region_0.2 | all-reduce | flops 2048 | bytes 16384 | tf_op jit(solution)/shard_map/psum | solution.py:66
  138.5 0.6 broadcast_multiply_fusion
  139.1 0.0 copy-start.6
  139.1 0.7 all_to_all.41
  139.8 0.0 copy-done.6
  139.8 0.8 copy.18
  140.6 0.0 all-to-all-done
  140.6 9.5 %all-to-all-start.1 = ((s32[96,2,4]{2,1,0:T(2,128)}), s32[96,2,4]{2,1,0:T(2,128)S(1)}, u32[]{:S(2)}, u32[]{:S(2)}) async-start(s32[96,2,4]{2,1,0:T(2,128)} %bitcast.2), calls=%async_computation.1 | async-start | bytes 196608 | tf_op jit(solution)/shard_map/all_to_all | solution.py:69
  150.1 0.2 convert_reduce_fusion.3
  150.4 13.1 %all-to-all-done.1 = s32[96,2,4]{2,1,0:T(2,128)S(1)} async-done(((s32[96,2,4]{2,1,0:T(2,128)}), s32[96,2,4]{2,1,0:T(2,128)S(1)}, u32[]{:S(2)}, u32[]{:S(2)}) %all-to-all-start.1) | async-done | bytes 3104 | tf_op jit(solution)/shard_map/all_to_all | solution.py:69
  163.5 5.9 %all-to-all-start.3 = ((bf16[96,2,256]{2,1,0:T(2,128)(2,1)}), bf16[96,2,256]{2,1,0:T(2,128)(2,1)S(1)}, u32[]{:S(2)}, u32[]{:S(2)}) async-start(bf16[96,2,256]{2,1,0:T(2,128)(2,1)} %all_to_all.41), calls=%async_computation.3 | async-start | bytes 196608 | tf_op jit(solution)/shard_map/all_to_all | solution.py:68
  169.4 0.0 copy-start.2
  169.4 0.3 slice_reduce_fusion.3
  169.9 0.5 copy-done.2
  170.4 0.8 gather_fusion.1
  171.2 0.8 gather_fusion.3
  172.0 0.8 gather_fusion.2
  172.7 0.0 copy-start.9
  172.7 0.8 gather_fusion.4
  173.5 0.0 copy-start.10
  173.5 0.1 copy-done.9
  173.6 0.6 copy-done.10
  174.2 0.0 copy-start.7
  174.2 0.4 fusion.2
  174.6 0.0 copy-done
  174.6 0.3 copy-done.7
  174.9 0.0 copy-start.3
  174.9 0.0 copy-start.8
  174.9 0.3 fusion.4
  175.2 0.7 copy-done.3
  175.9 0.0 copy-done.8
  175.9 0.2 fusion.7
  176.1 0.7 all_to_all.38
  176.8 6.1 %all-to-all-done.3 = bf16[96,2,256]{2,1,0:T(2,128)(2,1)S(1)} async-done(((bf16[96,2,256]{2,1,0:T(2,128)(2,1)}), bf16[96,2,256]{2,1,0:T(2,128)(2,1)S(1)}, u32[]{:S(2)}, u32[]{:S(2)}) %all-to-all-start.3) | async-done | bytes 98336 | tf_op jit(solution)/shard_map/all_to_all | solution.py:68
  182.8 9.0 %all-to-all-start.2 = ((bf16[96,2,256]{2,1,0:T(2,128)(2,1)}), bf16[96,2,256]{2,1,0:T(2,128)(2,1)S(1)}, u32[]{:S(2)}, u32[]{:S(2)}) async-start(bf16[96,2,256]{2,1,0:T(2,128)(2,1)} %all_to_all.38), calls=%async_computation.2 | async-start | bytes 196608 | tf_op jit(solution)/shard_map/all_to_all | solution.py:74
  191.9 0.2 fusion.3
  192.1 0.4 fusion.8
  192.6 2.1 %fusion.9 = f32[1024,128]{1,0:T(8,128)} fusion(bf16[192,128]{1,0:T(8,128)(2,1)S(1)} %fusion.8, f32[192]{0:T(256)S(1)} %get-tuple-element.9, s32[192]{0:T(256)S(1)} %get-tuple-element.5, f32[192]{0:T(256)S(1)} %get-tuple-element.10, s32[192]{0:T(256)S(1)} %get-tuple-element.6, f32[192]{0:T(256)S(1)} %get-tuple-element.11, s32[192]{0:T(256)S(1)} %get-tuple-element.7, ...), kind=kOutput, calls=%fused_computation.20 | convolution fusion | flops 304152576 | bytes 579584 | tf_op jit(solution)/shard_map/dot_general | solution.py:47
  194.7 10.5 %all-to-all-done.2 = bf16[96,2,256]{2,1,0:T(2,128)(2,1)S(1)} async-done(((bf16[96,2,256]{2,1,0:T(2,128)(2,1)}), bf16[96,2,256]{2,1,0:T(2,128)(2,1)S(1)}, u32[]{:S(2)}, u32[]{:S(2)}) %all-to-all-start.2) | async-done | bytes 98336 | tf_op jit(solution)/shard_map/all_to_all | solution.py:74
  205.2 0.7 all_to_all.40
  (12 shorter events, 0.1 us)
Async XLA Ops:
  0.6 174.0 %copy-start = (bf16[512,512]{1,0:T(8,128)(2,1)S(1)}, bf16[512,512]{1,0:T(8,128)(2,1)}, u32[]{:S(2)}) copy-start(bf16[512,512]{1,0:T(8,128)(2,1)} %param.22) | copy-start | bytes 1572868
  2.1 138.5 %all-to-all-start = ((bf16[96,2,4]{2,1,0:T(2,128)(2,1)}), bf16[96,2,4]{2,1,0:T(2,128)(2,1)S(1)}, u32[]{:S(2)}, u32[]{:S(2)}) async-start(bf16[96,2,4]{2,1,0:T(2,128)(2,1)} %bitcast), calls=%async_computation | async-start | bytes 98304 | tf_op jit(solution)/shard_map/all_to_all | solution.py:70
  24.7 0.7 copy-start.1
  25.4 1.6 copy-start.4
  26.9 0.7 copy-start.5
  139.1 0.7 copy-start.6
  140.6 22.9 %all-to-all-start.1 = ((s32[96,2,4]{2,1,0:T(2,128)}), s32[96,2,4]{2,1,0:T(2,128)S(1)}, u32[]{:S(2)}, u32[]{:S(2)}) async-start(s32[96,2,4]{2,1,0:T(2,128)} %bitcast.2), calls=%async_computation.1 | async-start | bytes 196608 | tf_op jit(solution)/shard_map/all_to_all | solution.py:69
  163.5 19.4 %all-to-all-start.3 = ((bf16[96,2,256]{2,1,0:T(2,128)(2,1)}), bf16[96,2,256]{2,1,0:T(2,128)(2,1)S(1)}, u32[]{:S(2)}, u32[]{:S(2)}) async-start(bf16[96,2,256]{2,1,0:T(2,128)(2,1)} %all_to_all.41), calls=%async_computation.3 | async-start | bytes 196608 | tf_op jit(solution)/shard_map/all_to_all | solution.py:68
  169.4 1.0 copy-start.2
  172.7 0.9 copy-start.9
  173.5 0.7 copy-start.10
  174.2 0.7 copy-start.7
  174.9 0.9 copy-start.3
  174.9 1.0 copy-start.8
  182.8 22.4 %all-to-all-start.2 = ((bf16[96,2,256]{2,1,0:T(2,128)(2,1)}), bf16[96,2,256]{2,1,0:T(2,128)(2,1)S(1)}, u32[]{:S(2)}, u32[]{:S(2)}) async-start(bf16[96,2,256]{2,1,0:T(2,128)(2,1)} %all_to_all.38), calls=%async_computation.2 | async-start | bytes 196608 | tf_op jit(solution)/shard_map/all_to_all | solution.py:74
where the time goes:
time: 208 us; the launch traced here: 206 us
  blocking collectives  111 us (53%)
  starting transfers between devices  47 us (23%)
  waiting for transfers between devices  29.7 us (14%)
  local copies, waits for them, and re-layouts  12.7 us (6%)
  matrix products  3.82 us (2%)
    psum x1, blocking collectives, on_device(): lax.psum(partial_terms, ('tx', 'ty')) * (1.0 / math.sqrt(total_slots))  111 us
    all_to_all x1, starting transfers between devices, on_device(): lax.all_to_all(bilinear, 'tx', split_axis=0, concat_axis=0, tiled=True)  22.5 us
    all_to_all x1, waiting for transfers between devices, on_device(): lax.all_to_all(stencil, 'tx', split_axis=0, concat_axis=0, tiled=True)  13.1 us
    all_to_all x1, waiting for transfers between devices, on_device(): lax.all_to_all(computed, 'tx', split_axis=0, concat_axis=0, tiled=True)  10.5 us
    all_to_all x1, starting transfers between devices, on_device(): lax.all_to_all(stencil, 'tx', split_axis=0, concat_axis=0, tiled=True)  9.51 us
    all_to_all x1, starting transfers between devices, on_device(): lax.all_to_all(computed, 'tx', split_axis=0, concat_axis=0, tiled=True)  8.98 us
    all_to_all x1, waiting for transfers between devices, on_device(): lax.all_to_all(dy, 'tx', split_axis=0, concat_axis=0, tiled=True)  6.07 us
    all_to_all x1, starting transfers between devices, on_device(): lax.all_to_all(dy, 'tx', split_axis=0, concat_axis=0, tiled=True)  5.94 us
  transfers between devices with their start and end apart: 4, of which 3 were waited for; matrix products, arithmetic and copies ran while one was open for 5% of the time, Pallas kernels for 0%

commit v1 on v0

v1 whole, which is shorter than its diff:
```python
import math

import jax
import jax.numpy as jnp
from jax import lax
from jax.sharding import PartitionSpec as P

F32, BF16 = jnp.float32, jnp.bfloat16


def exchange(block, axis):
    return lax.all_to_all(block, axis, split_axis=0, concat_axis=0, tiled=True)


def split_pair(x):
    high = lax.reduce_precision(x, exponent_bits=8, mantissa_bits=7)
    return high.astype(BF16), (x - high).astype(BF16)


def forward(profile, w_in, b_in, w_mid, b_mid):
    h1 = jnp.tanh(jnp.dot(profile, w_in, preferred_element_type=F32) + b_in).astype(BF16)
    h2 = jnp.tanh(jnp.dot(h1, w_mid, preferred_element_type=F32) + b_mid).astype(BF16)
    return h1, h2


def backward(cotangent, h1, h2, w_in, w_mid, w_out):
    back_dims = (((1,), (1,)), ((), ()))
    h2f, h1f = h2.astype(F32), h1.astype(F32)
    g2 = lax.dot_general(cotangent, w_out, back_dims, preferred_element_type=F32)
    g2 = (g2 * (1.0 - h2f * h2f)).astype(BF16)
    g1 = lax.dot_general(g2, w_mid, back_dims, preferred_element_type=F32)
    g1 = (g1 * (1.0 - h1f * h1f)).astype(BF16)
    return lax.dot_general(g1, w_in, back_dims, preferred_element_type=F32).astype(BF16)


def on_device(
    state, departures, stencil, bilinear, counts, predictors, w_in, b_in, w_mid, b_mid, w_out, b_out
):
    slots, channels = departures.shape
    columns, feat = state.shape
    npred = predictors.shape[0]
    peers = lax.axis_size("tx")
    rows = lax.axis_size("ty")
    cap = slots // peers
    tile_w = 32
    total_slots = slots * peers * rows
    share = -(-npred * channels // slots)

    live = (jnp.arange(cap, dtype=jnp.int32)[None, :] < counts[:, None]).reshape(slots)
    dy = jnp.where(live[:, None], departures, jnp.zeros_like(departures))
    partial = jnp.dot(predictors, dy.astype(F32), precision=lax.Precision.HIGHEST)
    partial = jnp.pad(partial.reshape(-1), (0, share * slots - npred * channels)).reshape(slots, share)
    high, low = split_pair(partial)
    corner = stencil[:, 0]
    place = jnp.stack([corner // tile_w, corner % tile_w], axis=1).astype(BF16)
    used = 6 + 2 * share
    pad = jnp.zeros((slots, 128 - used), BF16)
    sent = jnp.concatenate([dy, place, bilinear, high, low, pad], axis=1)
    got = exchange(sent.reshape(peers, cap, -1), "tx").reshape(slots, -1)

    got_dy = got[:, :channels]
    extra = got[:, channels:].astype(F32)
    terms = extra[:, 6 : 6 + share] + extra[:, 6 + share : 6 + 2 * share]
    terms = terms.reshape(peers, cap * share).sum(axis=0)
    spread_terms = jnp.broadcast_to(jnp.pad(terms, (0, 128 - cap * share))[None, None], (rows, 1, 128))
    terms = exchange(spread_terms, "ty").sum(axis=(0, 1))[: cap * share]
    terms = terms * (1.0 / math.sqrt(total_slots))
    high, low = split_pair(terms.reshape(cap, share))

    first = (extra[:, 0:1] * tile_w + extra[:, 1:2]).astype(jnp.int32)
    delta = jnp.arange(columns, dtype=jnp.int32)[None, :] - first
    spread = jnp.zeros((slots, columns), F32)
    for k, offset in enumerate((0, 1, tile_w, tile_w + 1)):
        spread = jnp.where(delta == offset, extra[:, 2 + k : 3 + k], spread)
    spread = spread.astype(BF16)
    profile = jnp.dot(spread, state, preferred_element_type=F32).astype(BF16)

    tail = jnp.concatenate([high, low, jnp.zeros((cap, 128 - 2 * share), BF16)], axis=1)
    tail = jnp.broadcast_to(tail[None], (peers, cap, 128))
    back = exchange(jnp.concatenate([profile.reshape(peers, cap, feat), tail], axis=2), "tx")

    h1, h2 = forward(profile, w_in, b_in, w_mid, b_mid)
    dprofile = backward(got_dy, h1, h2, w_in, w_mid, w_out)
    state_grad = lax.dot_general(
        spread, dprofile, (((0,), (0,)), ((), ())), preferred_element_type=F32
    )

    back = back.reshape(slots, -1)
    mine = back[:, :feat]
    bias = back[:, feat : feat + 2 * share].astype(F32)
    bias_grad = (bias[:, :share] + bias[:, share:]).reshape(-1)[: npred * channels]
    bias_grad = bias_grad.reshape(npred, channels)
    h1, h2 = forward(mine, w_in, b_in, w_mid, b_mid)
    radiance = (jnp.dot(h2, w_out, preferred_element_type=F32) + b_out).astype(BF16)
    return (radiance, state_grad, bias_grad)


def solution(mesh):
    both = P(("tx", "ty"), None)
    placed = (both, both, both, both, P(("tx", "ty")), P(None, ("tx", "ty"))) + (P(),) * 6
    return jax.shard_map(
        on_device,
        mesh=mesh,
        in_specs=placed,
        out_specs=(both, both, P()),
        check_vma=False,
    )
```

time: 208 us -> 78.8 us (0.38)
  blocking collectives: 111 us -> 0 us
  starting transfers between devices: 47 us -> 35.8 us
  local copies, waits for them, and re-layouts: 12.7 us -> 6.66 us
  waiting for transfers between devices: 29.7 us -> 26.9 us
  other arithmetic: 1.02 us -> 3.62 us
    psum x1 -> x0, blocking collectives: 111 us -> none  [on_device(): lax.psum(partial_terms, ('tx', 'ty')) * (1.0 / math.sqrt(total_slots))]
    all_to_all x4 -> x3, starting transfers between devices: 47 us -> 35.8 us  [exchange(): return lax.all_to_all(block, axis, split_axis=0, concat_axis=0, tiled=True)]
    gather x5 -> x0, local copies, waits for them, and re-layouts: 4.69 us -> none  [the longest x4 3.14 us: interpolate(): rows = jnp.take(state, stencil[:, k], axis=0)]
    all_to_all x4 -> x3, waiting for transfers between devices: 29.7 us -> 26.9 us  [exchange(): return lax.all_to_all(block, axis, split_axis=0, concat_axis=0, tiled=True)]
    unnamed x24 -> x22, local copies, waits for them, and re-layouts: 5.65 us -> 2.94 us
    all_to_all x4 -> x0, local copies, waits for them, and re-layouts: 2.1 us -> none  [the longest x2 1.37 us: on_device(): lax.all_to_all(computed, 'tx', split_axis=0, concat_axis=0, tiled=True)]
    dot_general x7 -> x9, matrix products: 3.82 us -> 4.42 us  [the longest x1 1.39 us: on_device(): lax.dot_general(spread, dprofile, (((0,), (0,)), ((), ())), preferred_ele...]
  transfers between devices with their start and end apart: 4 -> 3, of which waited for: 3 -> 3; matrix products, arithmetic and copies ran while one was open for 5% -> 4% of each run, Pallas kernels for 0% -> 0%
where the time goes in v1:
time: 78.8 us; the launch traced here: 78.2 us
  starting transfers between devices  35.8 us (45%)
  waiting for transfers between devices  26.9 us (34%)
  local copies, waits for them, and re-layouts  6.66 us (8%)
  matrix products  4.42 us (6%)
  other arithmetic  3.62 us (5%)
  between operations  0.92 us (1%)
    all_to_all x3, starting transfers between devices, exchange(): return lax.all_to_all(block, axis, split_axis=0, concat_axis=0, tiled=True)  35.8 us
    all_to_all x3, waiting for transfers between devices, exchange(): return lax.all_to_all(block, axis, split_axis=0, concat_axis=0, tiled=True)  26.9 us
    unnamed x22, local copies, waits for them, and re-layouts  2.94 us
  transfers between devices with their start and end apart: 3, of which 3 were waited for; matrix products, arithmetic and copies ran while one was open for 4% of the time, Pallas kernels for 0%

profile of v1, /device:TPU:1, one launch (start us, length us, event | category | flops | bytes accessed | tf_op | source)
XLA Modules:
  0.0 78.2 jit_solution(11097989342173844498)
XLA Ops:
  0.6 0.0 copy-start
  0.6 0.0 copy-start.3
  0.7 0.8 fusion.32
  1.4 0.7 fusion.33
  2.1 0.7 iota_compare_fusion
  2.9 0.1 lt.29
  3.0 0.1 copy.24
  3.2 0.0 copy-start.7
  3.2 0.1 copy.25
  3.3 0.5 copy-done.7
  3.9 0.1 copy.26
  4.0 0.0 copy-done.3
  4.0 0.0 copy-start.5
  4.0 0.1 broadcast_select_fusion
  4.1 0.6 copy-done.5
  4.7 0.1 convolution_bitcast_fusion
  4.9 0.2 reshape.60
  5.2 0.2 concatenate.10
  5.3 0.7 reshape.61
  6.1 22.5 %all-to-all-start = ((bf16[96,2,384]{2,1,0:T(2,128)(2,1)}), bf16[96,2,384]{2,1,0:T(2,128)(2,1)S(1)}, u32[]{:S(2)}, u32[]{:S(2)}) async-start(bf16[96,2,384]{2,1,0:T(2,128)(2,1)} %reshape.61), calls=%async_computation | async-start | bytes 294912 | tf_op jit(solution)/shard_map/all_to_all | solution.py:12
  28.6 0.1 pad.14.clone
  28.7 13.6 %all-to-all-done = bf16[96,2,384]{2,1,0:T(2,128)(2,1)S(1)} async-done(((bf16[96,2,384]{2,1,0:T(2,128)(2,1)}), bf16[96,2,384]{2,1,0:T(2,128)(2,1)S(1)}, u32[]{:S(2)}, u32[]{:S(2)}) %all-to-all-start) | async-done | bytes 147488 | tf_op jit(solution)/shard_map/all_to_all | solution.py:12
  42.3 0.1 reshape.62
  42.4 0.2 fusion.29
  42.6 0.4 slice_reduce_fusion.3
  43.0 0.0 copy-start.8
  43.0 0.1 slice_add_fusion.1
  43.1 0.1 reshape.64
  43.2 0.6 broadcast_in_dim.83
  43.8 7.3 %all-to-all-start.1 = ((f32[8,1,128]{2,1,0:T(1,128)}), f32[8,1,128]{2,1,0:T(1,128)S(1)}, u32[]{:S(2)}, u32[]{:S(2)}) async-start(f32[8,1,128]{2,1,0:T(1,128)} %broadcast_in_dim.83), calls=%async_computation.1 | async-start | bytes 8192 | tf_op jit(solution)/shard_map/all_to_all | solution.py:12
  51.1 0.0 copy-done.8
  51.1 0.0 copy-start.1
  51.1 0.0 copy-start.4
  51.1 0.5 convolution_convert_fusion
  51.6 0.4 copy-done.1
  52.0 0.0 copy-done.4
  52.0 0.0 copy-start.6
  52.0 0.2 fusion.6
  52.2 0.0 copy-done
  52.2 0.5 copy-done.6
  52.7 0.0 copy-start.2
  52.7 0.3 fusion.11
  53.0 0.7 copy-done.2
  53.6 0.2 fusion.5
  53.9 1.7 %all-to-all-done.1 = f32[8,1,128]{2,1,0:T(1,128)S(1)} async-done(((f32[8,1,128]{2,1,0:T(1,128)}), f32[8,1,128]{2,1,0:T(1,128)S(1)}, u32[]{:S(2)}, u32[]{:S(2)}) %all-to-all-start.1) | async-done | bytes 4128 | tf_op jit(solution)/shard_map/all_to_all | solution.py:12
  55.6 0.1 mul.28
  55.7 0.1 maximum_maximum_fusion
  55.8 0.7 pad_maximum_fusion
  56.6 5.9 %all-to-all-start.2 = ((bf16[96,2,256]{2,1,0:T(2,128)(2,1)}), bf16[96,2,256]{2,1,0:T(2,128)(2,1)S(1)}, u32[]{:S(2)}, u32[]{:S(2)}) async-start(bf16[96,2,256]{2,1,0:T(2,128)(2,1)} %pad_maximum_fusion), calls=%async_computation.2 | async-start | bytes 196608 | tf_op jit(solution)/shard_map/all_to_all | solution.py:12
  62.5 0.4 fusion.15
  63.0 1.4 %fusion.23 = f32[1024,128]{1,0:T(8,128)} fusion(bf16[192,128]{1,0:T(8,128)(2,1)S(1)} %fusion.15, bf16[192]{0:T(256)(128)(2,1)S(1)} %get-tuple-element.4, bf16[192]{0:T(256)(128)(2,1)S(1)} %get-tuple-element.5, bf16[192]{0:T(256)(128)(2,1)S(1)} %get-tuple-element.6, bf16[192]{0:T(256)(128)(2,1)S(1)} %get-tuple-element.3, s32[192]{0:T(256)S(1)} %fusion.29), kind=kOutput, calls=%fused_computation.34 | convolution fusion | flops 52101120 | bytes 575744 | tf_op jit(solution)/shard_map/dot_general | solution.py:84
  64.4 11.5 %all-to-all-done.2 = bf16[96,2,256]{2,1,0:T(2,128)(2,1)S(1)} async-done(((bf16[96,2,256]{2,1,0:T(2,128)(2,1)}), bf16[96,2,256]{2,1,0:T(2,128)(2,1)S(1)}, u32[]{:S(2)}, u32[]{:S(2)}) %all-to-all-start.2) | async-done | bytes 98336 | tf_op jit(solution)/shard_map/all_to_all | solution.py:12
  76.0 0.2 fusion.4
  76.2 0.1 slice_add_fusion
  76.3 0.2 reshape.66
  76.5 0.0 copy-start.9
  76.5 0.6 reshape.67
  77.1 0.1 copy-done.9
  77.2 1.1 %fusion.14 = bf16[192,256]{1,0:T(8,128)(2,1)} fusion(bf16[512,256]{1,0:T(8,128)(2,1)S(1)} %copy-done.2, bf16[192,512]{1,0:T(8,128)(2,1)S(1)} %fusion.4, bf16[512,512]{1,0:T(8,128)(2,1)S(1)} %copy-done, f32[512]{0:T(512)S(1)} %copy-done.6, f32[256]{0:T(256)S(1)} %copy-done.9), kind=kOutput, calls=%fused_computation.21 | convolution fusion | flops 151289856 | bytes 1084416 | tf_op jit(solution)/shard_map/dot_general | solution.py:94
  (15 shorter events, 0.2 us)
Async XLA Ops:
  0.6 51.6 %copy-start = (bf16[512,512]{1,0:T(8,128)(2,1)S(1)}, bf16[512,512]{1,0:T(8,128)(2,1)}, u32[]{:S(2)}) copy-start(bf16[512,512]{1,0:T(8,128)(2,1)} %param.20) | copy-start | bytes 1572868
  0.6 3.4 %copy-start.3 = (bf16[192,256]{1,0:T(8,128)(2,1)S(1)}, bf16[192,256]{1,0:T(8,128)(2,1)}, u32[]{:S(2)}) copy-start(bf16[192,256]{1,0:T(8,128)(2,1)} %param.13) | copy-start | bytes 294916
  3.2 0.7 copy-start.7
  4.0 0.7 copy-start.5
  6.1 36.3 %all-to-all-start = ((bf16[96,2,384]{2,1,0:T(2,128)(2,1)}), bf16[96,2,384]{2,1,0:T(2,128)(2,1)S(1)}, u32[]{:S(2)}, u32[]{:S(2)}) async-start(bf16[96,2,384]{2,1,0:T(2,128)(2,1)} %reshape.61), calls=%async_computation | async-start | bytes 294912 | tf_op jit(solution)/shard_map/all_to_all | solution.py:12
  43.0 8.1 %copy-start.8 = (bf16[1024,128]{1,0:T(8,128)(2,1)S(1)}, bf16[1024,128]{1,0:T(8,128)(2,1)}, u32[]{:S(2)}) copy-start(bf16[1024,128]{1,0:T(8,128)(2,1)} %param.12) | copy-start | bytes 786436
  43.8 11.8 %all-to-all-start.1 = ((f32[8,1,128]{2,1,0:T(1,128)}), f32[8,1,128]{2,1,0:T(1,128)S(1)}, u32[]{:S(2)}, u32[]{:S(2)}) async-start(f32[8,1,128]{2,1,0:T(1,128)} %broadcast_in_dim.83), calls=%async_computation.1 | async-start | bytes 8192 | tf_op jit(solution)/shard_map/all_to_all | solution.py:12
  51.1 0.9 %copy-start.1 = (bf16[128,512]{1,0:T(8,128)(2,1)S(1)}, bf16[128,512]{1,0:T(8,128)(2,1)}, u32[]{:S(2)}) copy-start(bf16[128,512]{1,0:T(8,128)(2,1)} %param.18) | copy-start | bytes 393220
  51.1 0.9 %copy-start.4 = (f32[512]{0:T(512)S(1)}, f32[512]{0:T(512)}, u32[]{:S(2)}) copy-start(f32[512]{0:T(512)} %param.19) | copy-start | bytes 6148
  52.0 0.7 copy-start.6
  52.7 0.9 %copy-start.2 = (bf16[512,256]{1,0:T(8,128)(2,1)S(1)}, bf16[512,256]{1,0:T(8,128)(2,1)}, u32[]{:S(2)}) copy-start(bf16[512,256]{1,0:T(8,128)(2,1)} %param.22) | copy-start | bytes 786436
  56.6 19.3 %all-to-all-start.2 = ((bf16[96,2,256]{2,1,0:T(2,128)(2,1)}), bf16[96,2,256]{2,1,0:T(2,128)(2,1)S(1)}, u32[]{:S(2)}, u32[]{:S(2)}) async-start(bf16[96,2,256]{2,1,0:T(2,128)(2,1)} %pad_maximum_fusion), calls=%async_computation.2 | async-start | bytes 196608 | tf_op jit(solution)/shard_map/all_to_all | solution.py:12
  76.5 0.7 copy-start.9

commit v2 on v1

v2 whole, which is shorter than its diff:
```python
import functools
import math

import jax
import jax.numpy as jnp
from jax import lax
from jax.experimental import pallas as pl
from jax.experimental.pallas import tpu as pltpu
from jax.sharding import PartitionSpec as P

F32, BF16, I32 = jnp.float32, jnp.bfloat16, jnp.int32
NT = (((1,), (1,)), ((), ()))
TN = (((0,), (0,)), ((), ()))
TILE_W = 32
LANES = 128
GRANT = 40 * 1024 * 1024


def exchange(block, axis):
    return lax.all_to_all(block, axis, split_axis=0, concat_axis=0, tiled=True)


def dot(a, b):
    return jnp.dot(a, b, preferred_element_type=F32)


def dot_dims(a, b, dims):
    return lax.dot_general(a, b, dims, preferred_element_type=F32)


def place(shape, dim):
    return lax.broadcasted_iota(I32, shape, dim)


def identity(rows, columns):
    shape = (rows, columns)
    return (place(shape, 0) == place(shape, 1)).astype(F32).astype(BF16)


def rounded(x):
    return x.astype(BF16).astype(F32)


def pack_kernel(departures, stencil, bilinear, counts, predictors, out):
    slots, channels = departures.shape
    peers = counts.shape[1]
    cap = slots // peers
    npred = predictors.shape[0]
    holds = (place((slots, peers), 0) // cap == place((slots, peers), 1)).astype(F32).astype(BF16)
    counted = jnp.broadcast_to(counts[...].astype(F32), (8, peers)).astype(BF16)
    count_of = dot_dims(holds, counted, NT)[:, 0:1]
    live = (place((slots, 1), 0) % cap).astype(F32) < count_of
    dy = jnp.where(live, departures[...].astype(F32), 0.0).astype(BF16)
    out[:, :channels] = dy

    pred = predictors[...]
    part0 = rounded(pred)
    part1 = rounded(pred - part0)
    part2 = pred - part0 - part1
    thirds = dot(jnp.concatenate([part0, part1, part2], axis=0).astype(BF16), dy)
    partial = thirds[:npred] + thirds[npred : 2 * npred] + thirds[2 * npred :]
    rest = channels - LANES
    upper = jnp.where(
        place((npred, rest), 1) >= slots - LANES, partial[:, LANES:], 0.0
    )
    upper = jnp.concatenate([upper, jnp.zeros((npred, slots - rest), F32)], axis=1)
    lower = partial[:, :slots]
    corner = stencil[0:1, :]
    column = jnp.bitwise_and(corner, TILE_W - 1)
    row = (corner - column) // TILE_W
    rows = [
        bilinear[...].astype(F32),
        row.astype(F32),
        column.astype(F32),
        jnp.zeros((2, slots), F32),
        rounded(lower),
        lower - rounded(lower),
        rounded(upper),
        upper - rounded(upper),
    ]
    rows.append(jnp.zeros((LANES - 8 - 4 * npred, slots), F32))
    extra = jnp.concatenate(rows, axis=0).astype(BF16)
    out[:, channels:] = dot_dims(identity(slots, slots), extra, NT).astype(BF16)


def terms_kernel(got, out):
    slots, width = got.shape
    cap = out.shape[1]
    mine = (place((8, slots), 1) % cap == place((8, slots), 0)).astype(F32).astype(BF16)
    terms = dot(mine, got[:, width - LANES :])
    for peer in range(out.shape[0]):
        out[peer] = terms[:cap]


def spread_of(extra, columns):
    extra = extra.astype(F32)
    corner = (extra[:, 4:5] * TILE_W + extra[:, 5:6]).astype(I32)
    delta = place((extra.shape[0], columns), 1) - corner
    spread = jnp.zeros(delta.shape, F32)
    for k, offset in enumerate((0, 1, TILE_W, TILE_W + 1)):
        spread = jnp.where(delta == offset, extra[:, k : k + 1], spread)
    return spread.astype(BF16)


def profile_kernel(got, state, out):
    width = got.shape[1]
    spread = spread_of(got[:, width - LANES :], state.shape[0])
    out[...] = dot(spread, state[...]).astype(BF16)


def forward(profile, w_in, b_in, w_mid, b_mid):
    h1 = jnp.tanh(dot(profile, w_in[...]) + b_in[...]).astype(BF16)
    h2 = jnp.tanh(dot(h1, w_mid[...]) + b_mid[...]).astype(BF16)
    return h1, h2


def grad_kernel(got, profile, w_in, b_in, w_mid, b_mid, w_out, out):
    width = got.shape[1]
    h1, h2 = forward(profile[...], w_in, b_in, w_mid, b_mid)
    h2, h1 = h2.astype(F32), h1.astype(F32)
    g2 = dot_dims(got[:, : width - LANES], w_out[...], NT)
    g2 = (g2 * (1.0 - h2 * h2)).astype(BF16)
    g1 = dot_dims(g2, w_mid[...], NT)
    g1 = (g1 * (1.0 - h1 * h1)).astype(BF16)
    dprofile = dot_dims(g1, w_in[...], NT).astype(BF16)
    spread = spread_of(got[:, width - LANES :], out.shape[0])
    out[...] = dot_dims(spread, dprofile, TN)


def reply_kernel(scale, npred, profile, terms, out):
    slots, feat = profile.shape
    cap = terms.shape[1]
    total = terms[0]
    for peer in range(1, terms.shape[0]):
        total = total + terms[peer]
    total = jnp.concatenate([total, jnp.zeros((8 - cap, LANES), F32)], axis=0)
    joined = (total + pltpu.roll(total, LANES - npred, 1)) * scale
    high = rounded(joined)
    low = pltpu.roll(joined - high, npred, 1)
    lanes = place((8, LANES), 1)
    is_high = ((lanes >= 8) & (lanes < 8 + npred)) | (
        (lanes >= 8 + 2 * npred) & (lanes < 8 + 3 * npred)
    )
    tail = jnp.where(is_high, high, low)
    which = (place((slots, 8), 0) % cap == place((slots, 8), 1)).astype(F32).astype(BF16)
    out[:, :feat] = profile[...]
    out[:, feat:] = dot(which, tail.astype(BF16)).astype(BF16)


def radiance_kernel(back, w_in, b_in, w_mid, b_mid, w_out, b_out, radiance, bias_grad):
    slots = back.shape[0]
    npred, channels = bias_grad.shape
    feat = w_in.shape[0]
    _, h2 = forward(back[:, :feat], w_in, b_in, w_mid, b_mid)
    radiance[...] = (dot(h2, w_out[...]) + b_out[...]).astype(BF16)
    turned = dot_dims(back[:, feat:], identity(slots, channels), TN)
    at = lambda k: turned[8 + k * npred : 8 + (k + 1) * npred]
    lower, upper = at(0) + at(1), at(2) + at(3)
    bias_grad[:, :LANES] = lower[:, :LANES]
    lanes = place((npred, channels - LANES), 1)
    bias_grad[:, LANES:] = jnp.where(
        lanes < slots - LANES, lower[:, LANES:], upper[:, : channels - LANES]
    )


def call(kernel, out, *args, flops=0, touched=0):
    return pl.pallas_call(
        kernel,
        out_shape=out,
        in_specs=[pl.BlockSpec(memory_space=pltpu.VMEM)] * len(args),
        out_specs=jax.tree.map(lambda _: pl.BlockSpec(memory_space=pltpu.VMEM), out),
        compiler_params=pltpu.CompilerParams(vmem_limit_bytes=GRANT),
        cost_estimate=pl.CostEstimate(flops=flops, bytes_accessed=touched, transcendentals=0),
    )(*args)


def on_device(
    state, departures, stencil, bilinear, counts, predictors, w_in, b_in, w_mid, b_mid, w_out, b_out
):
    slots, channels = departures.shape
    columns, feat = state.shape
    npred = predictors.shape[0]
    peers, rows = lax.axis_size("tx"), lax.axis_size("ty")
    cap = slots // peers
    scale = 1.0 / math.sqrt(slots * peers * rows)
    b_in, b_mid, b_out = b_in[None], b_mid[None], b_out[None]
    shape = jax.ShapeDtypeStruct

    sent = call(
        pack_kernel,
        shape((slots, channels + LANES), BF16),
        departures,
        stencil.T,
        bilinear.T,
        counts[None],
        predictors,
        flops=40_000_000,
        touched=300_000,
    )
    got = exchange(sent.reshape(peers, cap, -1), "tx").reshape(slots, -1)
    terms = call(terms_kernel, shape((rows, cap, LANES), F32), got, flops=1_000_000, touched=200_000)
    terms = exchange(terms, "ty")
    profile = call(
        profile_kernel, shape((slots, feat), BF16), got, state, flops=50_000_000, touched=500_000
    )
    reply = call(
        functools.partial(reply_kernel, scale, npred),
        shape((slots, feat + LANES), BF16),
        profile,
        terms,
        flops=1_000_000,
        touched=200_000,
    )
    back = exchange(reply.reshape(peers, cap, -1), "tx").reshape(slots, -1)
    state_grad = call(
        grad_kernel,
        shape((columns, feat), F32),
        got,
        profile,
        w_in,
        b_in,
        w_mid,
        b_mid,
        w_out,
        flops=400_000_000,
        touched=2_000_000,
    )
    radiance, bias_grad = call(
        radiance_kernel,
        (shape((slots, channels), BF16), shape((npred, channels), F32)),
        back,
        w_in,
        b_in,
        w_mid,
        b_mid,
        w_out,
        b_out,
        flops=200_000_000,
        touched=1_000_000,
    )
    return (radiance, state_grad, bias_grad)


def solution(mesh):
    both = P(("tx", "ty"), None)
    placed = (both, both, both, both, P(("tx", "ty")), P(None, ("tx", "ty"))) + (P(),) * 6
    return jax.shard_map(
        on_device,
        mesh=mesh,
        in_specs=placed,
        out_specs=(both, both, P()),
        check_vma=False,
    )
```

time: 78.8 us -> 75.9 us (0.963)
  blocking collectives: 0 us -> 36.1 us
  starting transfers between devices: 35.8 us -> 13.5 us
  waiting for transfers between devices: 26.9 us -> 14.7 us
  Pallas kernels: 0 us -> 5.32 us
  matrix products: 4.42 us -> 0 us
  other arithmetic: 3.62 us -> 0 us
  local copies, waits for them, and re-layouts: 6.66 us -> 5.13 us
    all_to_all x0 -> x1, blocking collectives: none -> 36.1 us  [exchange(): return lax.all_to_all(block, axis, split_axis=0, concat_axis=0, tiled=True)]
    all_to_all x3 -> x2, starting transfers between devices: 35.8 us -> 13.5 us  [exchange(): return lax.all_to_all(block, axis, split_axis=0, concat_axis=0, tiled=True)]
    all_to_all x3 -> x2, waiting for transfers between devices: 26.9 us -> 14.7 us  [exchange(): return lax.all_to_all(block, axis, split_axis=0, concat_axis=0, tiled=True)]
    pallas_call x0 -> x6, Pallas kernels: none -> 5.32 us  [call(): pl.pallas_call(kernel, out_shape=out, in_specs=[pl.BlockSpec(memory_space...]
    dot_general x9 -> x0, matrix products: 4.42 us -> none  [the longest x1 1.39 us: on_device(): lax.dot_general(spread, dprofile, (((0,), (0,)), ((), ())), preferred_ele...]
    another operation x2 -> x0, other arithmetic: 1.48 us -> none
    unnamed x22 -> x24, local copies, waits for them, and re-layouts: 2.94 us -> 4.28 us
    concatenate x2 -> x0, other arithmetic: 0.82 us -> none  [the longest x1 0.74 us: on_device(): jnp.concatenate([profile.reshape(peers, cap, feat), tail], axis=2)]
  transfers between devices with their start and end apart: 3 -> 2, of which waited for: 3 -> 2; matrix products, arithmetic and copies ran while one was open for 4% -> 0% of each run, Pallas kernels for 0% -> 3%
where the time goes in v2:
time: 75.9 us; the launch traced here: 75.4 us
  blocking collectives  36.1 us (48%)
  waiting for transfers between devices  14.7 us (19%)
  starting transfers between devices  13.5 us (18%)
  Pallas kernels  5.32 us (7%)
  local copies, waits for them, and re-layouts  5.13 us (7%)
    all_to_all x1, blocking collectives, exchange(): return lax.all_to_all(block, axis, split_axis=0, concat_axis=0, tiled=True)  36.1 us
    all_to_all x2, waiting for transfers between devices, exchange(): return lax.all_to_all(block, axis, split_axis=0, concat_axis=0, tiled=True)  14.7 us
    all_to_all x2, starting transfers between devices, exchange(): return lax.all_to_all(block, axis, split_axis=0, concat_axis=0, tiled=True)  13.5 us
    pallas_call x6, Pallas kernels, call(): pl.pallas_call(kernel, out_shape=out, in_specs=[pl.BlockSpec(memory_space...  5.32 us
    unnamed x24, local copies, waits for them, and re-layouts  4.28 us
  transfers between devices with their start and end apart: 2, of which 2 were waited for; matrix products, arithmetic and copies ran while one was open for 0% of the time, Pallas kernels for 3%

profile of v2, /device:TPU:1, one launch (start us, length us, event | category | flops | bytes accessed | tf_op | source)
XLA Modules:
  0.0 75.4 jit_solution(12391059428332797266)
XLA Ops:
  0.6 0.0 copy-start.8
  0.6 0.0 copy-start.11
  0.7 0.7 copy-done.8
  1.3 0.0 copy-done.11
  1.3 0.0 copy-start.4
  1.3 0.9 %copy-done.4 = bf16[192,256]{1,0:T(8,128)(2,1)S(1)} copy-done((bf16[192,256]{1,0:T(8,128)(2,1)S(1)}, bf16[192,256]{1,0:T(8,128)(2,1)}, u32[]{:S(2)}) %copy-start.4) | copy-done | bytes 98328
  2.2 0.0 copy-start.7
  2.2 0.7 copy-done.7
  2.9 0.0 copy-start.9
  2.9 0.7 copy-done.9
  3.6 0.5 shard_map.139
  4.1 0.1 reshape.18
  4.2 36.1 %all_to_all.15 = bf16[96,2,384]{2,1,0:T(2,128)(2,1)S(1)} all-to-all(bf16[96,2,384]{2,1,0:T(2,128)(2,1)S(1)} %reshape.18), channel_id=1, replica_groups=mesh['tx'=96,'ty'=8] {'tx'}, dimensions={0} | all-to-all | bytes 294912 | tf_op jit(solution)/shard_map/all_to_all | solution.py:20
  40.2 0.0 copy-start.3
  40.2 0.1 reshape.19.got
  40.3 0.7 shard_map.141
  41.0 0.0 copy-start
  41.0 7.4 %all-to-all-start.1 = ((f32[8,2,128]{2,1,0:T(2,128)}), f32[8,2,128]{2,1,0:T(2,128)S(1)}, u32[]{:S(2)}, u32[]{:S(2)}) async-start(f32[8,2,128]{2,1,0:T(2,128)} %shard_map.141), calls=%async_computation.1 | async-start | bytes 16384 | tf_op jit(solution)/shard_map/all_to_all | solution.py:20
  48.5 0.0 copy-done.3
  48.5 0.5 shard_map.140.profile
  49.0 0.0 copy-start.1
  49.0 4.1 %all-to-all-done.1.terms = f32[8,2,128]{2,1,0:T(2,128)S(1)} async-done(((f32[8,2,128]{2,1,0:T(2,128)}), f32[8,2,128]{2,1,0:T(2,128)S(1)}, u32[]{:S(2)}, u32[]{:S(2)}) %all-to-all-start.1) | async-done | bytes 8224 | tf_op jit(solution)/shard_map/all_to_all | solution.py:20
  53.1 0.3 shard_map.142
  53.3 0.7 reshape.20
  54.0 0.0 copy-start.2
  54.0 0.0 copy-start.6
  54.0 6.1 %all-to-all-start.2 = ((bf16[96,2,256]{2,1,0:T(2,128)(2,1)}), bf16[96,2,256]{2,1,0:T(2,128)(2,1)S(1)}, u32[]{:S(2)}, u32[]{:S(2)}) async-start(bf16[96,2,256]{2,1,0:T(2,128)(2,1)} %reshape.20), calls=%async_computation.2 | async-start | bytes 196608 | tf_op jit(solution)/shard_map/all_to_all | solution.py:20
  60.1 0.0 copy-start.5
  60.1 0.0 copy-done
  60.1 0.0 copy-done.1
  60.1 0.0 copy-done.2
  60.2 0.0 copy-done.6
  60.2 0.6 copy-done.5
  60.8 2.1 %shard_map.144 = f32[1024,128]{1,0:T(8,128)} custom-call(bf16[192,384]{1,0:T(8,128)(2,1)S(1)} %reshape.19.got, bf16[192,128]{1,0:T(8,128)(2,1)S(1)} %shard_map.140.profile, bf16[128,512]{1,0:T(8,128)(2,1)S(1)} %copy-done.2, f32[1,512]{1,0:T(1,128)S(1)} %bitcast.6, bf16[512,512]{1,0:T(8,128)(2,1)S(1)} %copy-done, f32[1,512]{1,0:T(1,128)S(1)} %bitcast.8, ...), custom_call_target="tpu_custom_call" | custom-call | flops 400000000 | bytes 2000000 | tf_op jit(solution)/shard_map/pallas_call | solution.py:167
  62.9 10.6 %all-to-all-done.2 = bf16[96,2,256]{2,1,0:T(2,128)(2,1)S(1)} async-done(((bf16[96,2,256]{2,1,0:T(2,128)(2,1)}), bf16[96,2,256]{2,1,0:T(2,128)(2,1)S(1)}, u32[]{:S(2)}, u32[]{:S(2)}) %all-to-all-start.2) | async-done | bytes 98336 | tf_op jit(solution)/shard_map/all_to_all | solution.py:20
  73.5 0.0 copy-start.10
  73.5 0.7 copy-done.10
  74.2 1.2 %shard_map.143 = (bf16[192,256]{1,0:T(8,128)(2,1)}, f32[8,256]{1,0:T(8,128)}) custom-call(bf16[192,256]{1,0:T(8,128)(2,1)S(1)} %reshape.21.back, bf16[128,512]{1,0:T(8,128)(2,1)S(1)} %copy-done.2, f32[1,512]{1,0:T(1,128)S(1)} %bitcast.7, bf16[512,512]{1,0:T(8,128)(2,1)S(1)} %copy-done, f32[1,512]{1,0:T(1,128)S(1)} %bitcast.9, ...), custom_call_target="tpu_custom_call" | custom-call | flops 200000000 | bytes 1000000 | tf_op jit(solution)/shard_map/pallas_call | solution.py:167
  (1 shorter events, 0.0 us)
Async XLA Ops:
  0.6 0.7 copy-start.8
  0.6 0.7 copy-start.11
  1.3 0.9 %copy-start.4 = (bf16[192,256]{1,0:T(8,128)(2,1)S(1)}, bf16[192,256]{1,0:T(8,128)(2,1)}, u32[]{:S(2)}) copy-start(bf16[192,256]{1,0:T(8,128)(2,1)} %departures.1) | copy-start | bytes 294916
  2.2 0.7 copy-start.7
  2.9 0.7 copy-start.9
  40.2 8.2 %copy-start.3 = (bf16[1024,128]{1,0:T(8,128)(2,1)S(1)}, bf16[1024,128]{1,0:T(8,128)(2,1)}, u32[]{:S(2)}) copy-start(bf16[1024,128]{1,0:T(8,128)(2,1)} %state.1) | copy-start | bytes 786436
  41.0 19.1 %copy-start = (bf16[512,512]{1,0:T(8,128)(2,1)S(1)}, bf16[512,512]{1,0:T(8,128)(2,1)}, u32[]{:S(2)}) copy-start(bf16[512,512]{1,0:T(8,128)(2,1)} %w_mid.3) | copy-start | bytes 1572868
  41.0 12.0 %all-to-all-start.1 = ((f32[8,2,128]{2,1,0:T(2,128)}), f32[8,2,128]{2,1,0:T(2,128)S(1)}, u32[]{:S(2)}, u32[]{:S(2)}) async-start(f32[8,2,128]{2,1,0:T(2,128)} %shard_map.141), calls=%async_computation.1 | async-start | bytes 16384 | tf_op jit(solution)/shard_map/all_to_all | solution.py:20
  49.0 11.1 %copy-start.1 = (bf16[512,256]{1,0:T(8,128)(2,1)S(1)}, bf16[512,256]{1,0:T(8,128)(2,1)}, u32[]{:S(2)}) copy-start(bf16[512,256]{1,0:T(8,128)(2,1)} %w_out.3) | copy-start | bytes 786436
  54.0 6.1 %copy-start.2 = (bf16[128,512]{1,0:T(8,128)(2,1)S(1)}, bf16[128,512]{1,0:T(8,128)(2,1)}, u32[]{:S(2)}) copy-start(bf16[128,512]{1,0:T(8,128)(2,1)} %w_in.3) | copy-start | bytes 393220
  54.0 6.1 %copy-start.6 = (f32[512]{0:T(512)S(1)}, f32[512]{0:T(512)}, u32[]{:S(2)}) copy-start(f32[512]{0:T(512)} %param.21) | copy-start | bytes 6148
  54.0 19.5 %all-to-all-start.2 = ((bf16[96,2,256]{2,1,0:T(2,128)(2,1)}), bf16[96,2,256]{2,1,0:T(2,128)(2,1)S(1)}, u32[]{:S(2)}, u32[]{:S(2)}) async-start(bf16[96,2,256]{2,1,0:T(2,128)(2,1)} %reshape.20), calls=%async_computation.2 | async-start | bytes 196608 | tf_op jit(solution)/shard_map/all_to_all | solution.py:20
  60.1 0.7 copy-start.5
  73.5 0.7 copy-start.10

commit v3 on v2

v3 whole, which is shorter than its diff:
```python
import functools
import math

import jax
import jax.numpy as jnp
from jax import lax
from jax.experimental import pallas as pl
from jax.experimental.pallas import tpu as pltpu
from jax.sharding import PartitionSpec as P

F32, BF16, I32 = jnp.float32, jnp.bfloat16, jnp.int32
NT = (((1,), (1,)), ((), ()))
TN = (((0,), (0,)), ((), ()))
TILE_W = 32
LANES = 128
GRANT = 40 * 1024 * 1024


def exchange(block, axis):
    return lax.all_to_all(block, axis, split_axis=0, concat_axis=0, tiled=True)


def dot(a, b):
    return jnp.dot(a, b, preferred_element_type=F32)


def dot_dims(a, b, dims):
    return lax.dot_general(a, b, dims, preferred_element_type=F32)


def place(shape, dim):
    return lax.broadcasted_iota(I32, shape, dim)


def identity(rows, columns):
    shape = (rows, columns)
    return (place(shape, 0) == place(shape, 1)).astype(F32).astype(BF16)


def rounded(x):
    return x.astype(BF16).astype(F32)


def pack_kernel(
    departures_hbm, stencil_hbm, bilinear_hbm, counts_hbm, predictors_hbm, out, shared,
    departures, stencil, bilinear, counts, predictors, arrived
):
    pairs = (
        (counts_hbm, counts),
        (departures_hbm, departures),
        (predictors_hbm, predictors),
        (stencil_hbm, stencil),
        (bilinear_hbm, bilinear),
    )
    copies = [
        pltpu.make_async_copy(source, target, arrived.at[k])
        for k, (source, target) in enumerate(pairs)
    ]
    for copy in copies:
        copy.start()
    slots, channels = departures.shape
    peers = counts.shape[1]
    cap = slots // peers
    npred = predictors.shape[0]
    holds = (place((slots, peers), 0) // cap == place((slots, peers), 1)).astype(F32).astype(BF16)
    turn = identity(slots, slots)
    for copy in copies:
        copy.wait()
    counted = jnp.broadcast_to(counts[...].astype(F32), (8, peers)).astype(BF16)
    count_of = dot_dims(holds, counted, NT)[:, 0:1]
    live = (place((slots, 1), 0) % cap).astype(F32) < count_of
    dy = jnp.where(live, departures[...].astype(F32), 0.0).astype(BF16)
    out[:, :channels] = dy

    pred = predictors[...]
    part0 = rounded(pred)
    part1 = rounded(pred - part0)
    part2 = pred - part0 - part1
    thirds = dot(jnp.concatenate([part0, part1, part2], axis=0).astype(BF16), dy)
    partial = thirds[:npred] + thirds[npred : 2 * npred] + thirds[2 * npred :]
    for peer in range(shared.shape[0]):
        shared[peer] = partial

    corner = stencil[0:1, :]
    column = jnp.bitwise_and(corner, TILE_W - 1)
    row = (corner - column) // TILE_W
    rows = [bilinear[...].astype(F32), row.astype(F32), column.astype(F32)]
    rows.append(jnp.zeros((LANES - 6, slots), F32))
    extra = jnp.concatenate(rows, axis=0).astype(BF16)
    out[:, channels:] = dot_dims(turn, extra, NT).astype(BF16)


def terms_kernel(packed, shared, out):
    slots, width = packed.shape
    npred, channels = shared.shape[1:]
    total = shared[0]
    for peer in range(1, shared.shape[0]):
        total = total + shared[peer]
    rest = channels - LANES
    upper = jnp.where(place((npred, rest), 1) >= slots - LANES, total[:, LANES:], 0.0)
    upper = jnp.concatenate([upper, jnp.zeros((npred, slots - rest), F32)], axis=1)
    lower = total[:, :slots]
    rows = [
        jnp.zeros((8, slots), F32),
        rounded(lower),
        lower - rounded(lower),
        rounded(upper),
        upper - rounded(upper),
        jnp.zeros((LANES - 8 - 4 * npred, slots), F32),
    ]
    rows = jnp.concatenate(rows, axis=0).astype(BF16)
    out[:, :channels] = packed[:, :channels]
    extra = dot_dims(identity(slots, slots), rows, NT)
    out[:, channels:] = (packed[:, channels:].astype(F32) + extra).astype(BF16)


def spread_of(extra, columns):
    extra = extra.astype(F32)
    corner = (extra[:, 4:5] * TILE_W + extra[:, 5:6]).astype(I32)
    delta = place((extra.shape[0], columns), 1) - corner
    spread = jnp.zeros(delta.shape, F32)
    for k, offset in enumerate((0, 1, TILE_W, TILE_W + 1)):
        spread = jnp.where(delta == offset, extra[:, k : k + 1], spread)
    return spread.astype(BF16)


def reply_kernel(scale, npred, cap, got, state, out):
    slots, width = got.shape
    feat = state.shape[1]
    extra = got[:, width - LANES :]
    mine = (place((8, slots), 1) % cap == place((8, slots), 0)).astype(F32).astype(BF16)
    total = dot(mine, extra)
    joined = (total + pltpu.roll(total, LANES - npred, 1)) * scale
    high = rounded(joined)
    low = pltpu.roll(joined - high, npred, 1)
    lanes = place((8, LANES), 1)
    is_high = ((lanes >= 8) & (lanes < 8 + npred)) | (
        (lanes >= 8 + 2 * npred) & (lanes < 8 + 3 * npred)
    )
    tail = jnp.where(is_high, high, low).astype(BF16)
    which = (place((slots, 8), 0) % cap == place((slots, 8), 1)).astype(F32).astype(BF16)
    out[:, feat:] = dot(which, tail).astype(BF16)
    spread = spread_of(extra, state.shape[0])
    out[:, :feat] = dot(spread, state[...]).astype(BF16)


def forward(profile, w_in, b_in, w_mid, b_mid):
    h1 = jnp.tanh(dot(profile, w_in[...]) + b_in[...]).astype(BF16)
    h2 = jnp.tanh(dot(h1, w_mid[...]) + b_mid[...]).astype(BF16)
    return h1, h2


def grad_kernel(got, reply, w_in, b_in, w_mid, b_mid, w_out, b_out, out, b_kept):
    width = got.shape[1]
    b_kept[...] = b_out[...]
    h1, h2 = forward(reply[:, : w_in.shape[0]], w_in, b_in, w_mid, b_mid)
    h2, h1 = h2.astype(F32), h1.astype(F32)
    g2 = dot_dims(got[:, : width - LANES], w_out[...], NT)
    g2 = (g2 * (1.0 - h2 * h2)).astype(BF16)
    g1 = dot_dims(g2, w_mid[...], NT)
    g1 = (g1 * (1.0 - h1 * h1)).astype(BF16)
    dprofile = dot_dims(g1, w_in[...], NT).astype(BF16)
    spread = spread_of(got[:, width - LANES :], out.shape[0])
    out[...] = dot_dims(spread, dprofile, TN)


def radiance_kernel(back, w_in, b_in, w_mid, b_mid, w_out, b_out, radiance, bias_grad):
    slots = back.shape[0]
    npred, channels = bias_grad.shape
    feat = w_in.shape[0]
    _, h2 = forward(back[:, :feat], w_in, b_in, w_mid, b_mid)
    radiance[...] = (dot(h2, w_out[...]) + b_out[...]).astype(BF16)
    turned = dot_dims(back[:, feat:], identity(slots, channels), TN)
    at = lambda k: turned[8 + k * npred : 8 + (k + 1) * npred]
    lower, upper = at(0) + at(1), at(2) + at(3)
    bias_grad[:, :LANES] = lower[:, :LANES]
    lanes = place((npred, channels - LANES), 1)
    bias_grad[:, LANES:] = jnp.where(
        lanes < slots - LANES, lower[:, LANES:], upper[:, : channels - LANES]
    )


def call(kernel, out, *args, flops=0, touched=0, space=pltpu.VMEM, scratch=(), grant=GRANT):
    return pl.pallas_call(
        kernel,
        out_shape=out,
        in_specs=[pl.BlockSpec(memory_space=space)] * len(args),
        out_specs=jax.tree.map(lambda _: pl.BlockSpec(memory_space=pltpu.VMEM), out),
        scratch_shapes=scratch,
        compiler_params=pltpu.CompilerParams(vmem_limit_bytes=grant),
        cost_estimate=pl.CostEstimate(flops=flops, bytes_accessed=touched, transcendentals=0),
    )(*args)


def on_device(
    state, departures, stencil, bilinear, counts, predictors, w_in, b_in, w_mid, b_mid, w_out, b_out
):
    slots, channels = departures.shape
    columns, feat = state.shape
    npred = predictors.shape[0]
    peers, rows = lax.axis_size("tx"), lax.axis_size("ty")
    cap = slots // peers
    scale = 1.0 / math.sqrt(slots * peers * rows)
    b_in, b_mid, b_out = b_in[None], b_mid[None], b_out[None]
    shape = jax.ShapeDtypeStruct

    inputs = (departures, stencil.T, bilinear.T, counts[None], predictors)
    packed, shared = call(
        pack_kernel,
        (shape((slots, channels + LANES), BF16), shape((rows, npred, channels), F32)),
        *inputs,
        flops=40_000_000,
        touched=300_000,
        space=pl.ANY,
        scratch=[pltpu.VMEM(a.shape, a.dtype) for a in inputs]
        + [pltpu.SemaphoreType.DMA((len(inputs),))],
        grant=60 * 1024 * 1024,
    )
    shared = exchange(shared, "ty")
    sent = call(
        terms_kernel,
        shape((slots, channels + LANES), BF16),
        packed,
        shared,
        flops=20_000_000,
        touched=300_000,
    )
    got = exchange(sent.reshape(peers, cap, -1), "tx").reshape(slots, -1)
    reply = call(
        functools.partial(reply_kernel, scale, npred, cap),
        shape((slots, feat + LANES), BF16),
        got,
        state,
        flops=50_000_000,
        touched=500_000,
    )
    back = exchange(reply.reshape(peers, cap, -1), "tx").reshape(slots, -1)
    state_grad, b_out = call(
        grad_kernel,
        (shape((columns, feat), F32), shape((1, channels), F32)),
        got,
        reply,
        w_in,
        b_in,
        w_mid,
        b_mid,
        w_out,
        b_out,
        flops=400_000_000,
        touched=2_000_000,
    )
    radiance, bias_grad = call(
        radiance_kernel,
        (shape((slots, channels), BF16), shape((npred, channels), F32)),
        back,
        w_in,
        b_in,
        w_mid,
        b_mid,
        w_out,
        b_out,
        flops=200_000_000,
        touched=1_000_000,
    )
    return (radiance, state_grad, bias_grad)


def solution(mesh):
    both = P(("tx", "ty"), None)
    placed = (both, both, both, both, P(("tx", "ty")), P(None, ("tx", "ty"))) + (P(),) * 6
    return jax.shard_map(
        on_device,
        mesh=mesh,
        in_specs=placed,
        out_specs=(both, both, P()),
        check_vma=False,
    )
```

time: 75.9 us -> 74.3 us (0.979)
  the two profiles are of different devices: /device:TPU:1 before, /device:TPU:8 now
where the time goes in v3:
time: 74.3 us; the launch traced here: 73.9 us
  blocking collectives  47.1 us (63%)
  waiting for transfers between devices  11.4 us (15%)
  starting transfers between devices  6.18 us (8%)
  Pallas kernels  6.12 us (8%)
  local copies, waits for them, and re-layouts  2.43 us (3%)
  between operations  0.75 us (1%)
    all_to_all x2, blocking collectives, exchange(): return lax.all_to_all(block, axis, split_axis=0, concat_axis=0, tiled=True)  47.1 us
    all_to_all x1, waiting for transfers between devices, exchange(): return lax.all_to_all(block, axis, split_axis=0, concat_axis=0, tiled=True)  11.4 us
    all_to_all x1, starting transfers between devices, exchange(): return lax.all_to_all(block, axis, split_axis=0, concat_axis=0, tiled=True)  6.18 us
    pallas_call x5, Pallas kernels, call(): pl.pallas_call(kernel, out_shape=out, in_specs=[pl.BlockSpec(memory_space...  6.12 us
    unnamed x16, local copies, waits for them, and re-layouts  1.58 us
  transfers between devices with their start and end apart: 1, of which 1 were waited for; matrix products, arithmetic and copies ran while one was open for 0% of the time, Pallas kernels for 3%

profile of v3, /device:TPU:8, one launch (start us, length us, event | category | flops | bytes accessed | tf_op | source)
XLA Modules:
  0.0 73.9 jit_solution(11519227858175719095)
XLA Ops:
  0.6 2.0 %shard_map.139 = (bf16[192,384]{1,0:T(8,128)(2,1)}, f32[8,8,256]{2,1,0:T(8,128)}) custom-call(bf16[192,256]{1,0:T(8,128)(2,1)} %departures_hbm.1, s32[4,192]{1,0:T(4,128)} %bitcast.11, bf16[4,192]{1,0:T(4,128)(2,1)} %bitcast.12, s32[1,96]{1,0:T(1,128)} %bitcast.13, f32[8,192]{1,0:T(8,128)} %predictors_hbm.1), custom_call_target="tpu_custom_call" | custom-call | flops 40000000 | bytes 300000 | tf_op jit(solution)/shard_map/pallas_call | solution.py:184
  2.6 9.9 %all_to_all.15.shared = f32[8,8,256]{2,1,0:T(8,128)S(1)} all-to-all(f32[8,8,256]{2,1,0:T(8,128)} %get-tuple-element.10), channel_id=1, replica_groups=mesh['tx'=96,'ty'=8] {'ty'}, dimensions={0} | all-to-all | bytes 131072 | tf_op jit(solution)/shard_map/all_to_all | solution.py:20
  12.6 0.0 copy-start.3
  12.6 0.9 %copy-done.3 = bf16[192,384]{1,0:T(8,128)(2,1)S(1)} copy-done((bf16[192,384]{1,0:T(8,128)(2,1)S(1)}, bf16[192,384]{1,0:T(8,128)(2,1)}, u32[]{:S(2)}) %copy-start.3) | copy-done | bytes 147480
  13.5 0.2 shard_map.140
  13.6 0.1 reshape.18
  13.7 0.0 copy-start.2
  13.7 37.2 %all_to_all.16 = bf16[96,2,384]{2,1,0:T(2,128)(2,1)S(1)} all-to-all(bf16[96,2,384]{2,1,0:T(2,128)(2,1)S(1)} %reshape.18), channel_id=1, replica_groups=mesh['tx'=96,'ty'=8] {'tx'}, dimensions={0} | all-to-all | bytes 294912 | tf_op jit(solution)/shard_map/all_to_all | solution.py:20
  50.9 0.0 copy-start.4
  50.9 0.1 reshape.19.got
  51.0 0.0 copy-done.2
  51.0 0.0 copy-start
  51.0 0.7 shard_map.141.reply
  51.7 0.0 copy-start.1
  51.7 0.7 reshape.20
  52.4 0.0 copy-start.6
  52.4 6.2 %all-to-all-start.2 = ((bf16[96,2,256]{2,1,0:T(2,128)(2,1)}), bf16[96,2,256]{2,1,0:T(2,128)(2,1)S(1)}, u32[]{:S(2)}, u32[]{:S(2)}) async-start(bf16[96,2,256]{2,1,0:T(2,128)(2,1)} %reshape.20), calls=%async_computation.2 | async-start | bytes 196608 | tf_op jit(solution)/shard_map/all_to_all | solution.py:20
  58.6 0.0 copy-start.5
  58.6 0.0 copy-start.7
  58.6 0.0 copy-done.4
  58.6 0.0 copy-done
  58.6 0.0 copy-done.1
  58.6 0.0 copy-done.6
  58.6 0.6 copy-done.5
  59.2 0.0 copy-done.7
  59.3 2.1 %shard_map.142 = (f32[1024,128]{1,0:T(8,128)}, f32[1,256]{1,0:T(1,128)S(1)}) custom-call(bf16[192,384]{1,0:T(8,128)(2,1)S(1)} %reshape.19.got, bf16[192,256]{1,0:T(8,128)(2,1)S(1)} %shard_map.141.reply, bf16[128,512]{1,0:T(8,128)(2,1)S(1)} %copy-done.4, f32[1,512]{1,0:T(1,128)S(1)} %bitcast.6, bf16[512,512]{1,0:T(8,128)(2,1)S(1)} %copy-done, ...), custom_call_target="tpu_custom_call" | custom-call | flops 400000000 | bytes 2000000 | tf_op jit(solution)/shard_map/pallas_call | solution.py:184
  61.4 11.4 %all-to-all-done.2 = bf16[96,2,256]{2,1,0:T(2,128)(2,1)S(1)} async-done(((bf16[96,2,256]{2,1,0:T(2,128)(2,1)}), bf16[96,2,256]{2,1,0:T(2,128)(2,1)S(1)}, u32[]{:S(2)}, u32[]{:S(2)}) %all-to-all-start.2) | async-done | bytes 98336 | tf_op jit(solution)/shard_map/all_to_all | solution.py:20
  72.8 1.2 %shard_map.143 = (bf16[192,256]{1,0:T(8,128)(2,1)}, f32[8,256]{1,0:T(8,128)}) custom-call(bf16[192,256]{1,0:T(8,128)(2,1)S(1)} %reshape.21.back, bf16[128,512]{1,0:T(8,128)(2,1)S(1)} %copy-done.4, f32[1,512]{1,0:T(1,128)S(1)} %bitcast.7, bf16[512,512]{1,0:T(8,128)(2,1)S(1)} %copy-done, f32[1,512]{1,0:T(1,128)S(1)} %bitcast.9, ...), custom_call_target="tpu_custom_call" | custom-call | flops 200000000 | bytes 1000000 | tf_op jit(solution)/shard_map/pallas_call | solution.py:184
  (1 shorter events, 0.0 us)
Async XLA Ops:
  12.6 0.9 %copy-start.3 = (bf16[192,384]{1,0:T(8,128)(2,1)S(1)}, bf16[192,384]{1,0:T(8,128)(2,1)}, u32[]{:S(2)}) copy-start(bf16[192,384]{1,0:T(8,128)(2,1)} %get-tuple-element.9.packed) | copy-start | bytes 442372
  13.7 37.2 %copy-start.2 = (bf16[1024,128]{1,0:T(8,128)(2,1)S(1)}, bf16[1024,128]{1,0:T(8,128)(2,1)}, u32[]{:S(2)}) copy-start(bf16[1024,128]{1,0:T(8,128)(2,1)} %state.1) | copy-start | bytes 786436
  50.9 7.7 %copy-start.4 = (bf16[128,512]{1,0:T(8,128)(2,1)S(1)}, bf16[128,512]{1,0:T(8,128)(2,1)}, u32[]{:S(2)}) copy-start(bf16[128,512]{1,0:T(8,128)(2,1)} %w_in.3) | copy-start | bytes 393220
  51.0 7.6 %copy-start = (bf16[512,512]{1,0:T(8,128)(2,1)S(1)}, bf16[512,512]{1,0:T(8,128)(2,1)}, u32[]{:S(2)}) copy-start(bf16[512,512]{1,0:T(8,128)(2,1)} %w_mid.3) | copy-start | bytes 1572868
  51.7 6.9 %copy-start.1 = (bf16[512,256]{1,0:T(8,128)(2,1)S(1)}, bf16[512,256]{1,0:T(8,128)(2,1)}, u32[]{:S(2)}) copy-start(bf16[512,256]{1,0:T(8,128)(2,1)} %w_out.3) | copy-start | bytes 786436
  52.4 6.3 %copy-start.6 = (f32[512]{0:T(512)S(1)}, f32[512]{0:T(512)}, u32[]{:S(2)}) copy-start(f32[512]{0:T(512)} %param.21) | copy-start | bytes 6148
  52.4 20.3 %all-to-all-start.2 = ((bf16[96,2,256]{2,1,0:T(2,128)(2,1)}), bf16[96,2,256]{2,1,0:T(2,128)(2,1)S(1)}, u32[]{:S(2)}, u32[]{:S(2)}) async-start(bf16[96,2,256]{2,1,0:T(2,128)(2,1)} %reshape.20), calls=%async_computation.2 | async-start | bytes 196608 | tf_op jit(solution)/shard_map/all_to_all | solution.py:20
  58.6 0.7 copy-start.5
  58.6 0.7 copy-start.7

commit v4 on v3

v4 whole, which is shorter than its diff:
```python
import functools
import math

import jax
import jax.numpy as jnp
from jax import lax
from jax.experimental import pallas as pl
from jax.experimental.pallas import tpu as pltpu
from jax.sharding import PartitionSpec as P

F32, BF16, I32 = jnp.float32, jnp.bfloat16, jnp.int32
NT = (((1,), (1,)), ((), ()))
TN = (((0,), (0,)), ((), ()))
TILE_W = 32
LANES = 128
GRANT = 40 * 1024 * 1024
PACK_GRANT = 60 * 1024 * 1024


def exchange(block, axis):
    return lax.all_to_all(block, axis, split_axis=0, concat_axis=0, tiled=True)


def dot(a, b):
    return jnp.dot(a, b, preferred_element_type=F32)


def dot_dims(a, b, dims):
    return lax.dot_general(a, b, dims, preferred_element_type=F32)


def place(shape, dim):
    return lax.broadcasted_iota(I32, shape, dim)


def identity(rows, columns):
    shape = (rows, columns)
    return (place(shape, 0) == place(shape, 1)).astype(F32).astype(BF16)


def rounded(x):
    return x.astype(BF16).astype(F32)


def pack_kernel(
    departures_hbm, stencil_hbm, bilinear_hbm, counts_hbm, predictors_hbm, out, masked,
    departures, stencil, bilinear, counts, predictors, arrived
):
    pairs = (
        (counts_hbm, counts),
        (departures_hbm, departures),
        (predictors_hbm, predictors),
        (stencil_hbm, stencil),
        (bilinear_hbm, bilinear),
    )
    copies = [
        pltpu.make_async_copy(source, target, arrived.at[k])
        for k, (source, target) in enumerate(pairs)
    ]
    for copy in copies:
        copy.start()
    slots, channels = departures.shape
    peers = counts.shape[1]
    cap = slots // peers
    npred = predictors.shape[0]
    holds = (place((slots, peers), 0) // cap == place((slots, peers), 1)).astype(F32).astype(BF16)
    turn = identity(slots, slots)
    for copy in copies:
        copy.wait()
    counted = jnp.broadcast_to(counts[...].astype(F32), (8, peers)).astype(BF16)
    count_of = dot_dims(holds, counted, NT)[:, 0:1]
    live = (place((slots, 1), 0) % cap).astype(F32) < count_of
    dy = jnp.where(live, departures[...].astype(F32), 0.0).astype(BF16)
    masked[...] = dy

    pred = predictors[...]
    part0 = rounded(pred)
    part1 = rounded(pred - part0)
    part2 = pred - part0 - part1
    thirds = dot(jnp.concatenate([part0, part1, part2], axis=0).astype(BF16), dy)
    partial = thirds[:npred] + thirds[npred : 2 * npred] + thirds[2 * npred :]
    slot = place((slots, npred), 0) % (2 * cap) * 2
    which = place((slots, npred), 1)
    partial = partial.astype(BF16)
    for k in range(2):
        chosen = (which == slot + k).astype(F32).astype(BF16)
        out[:, LANES + k * channels : LANES + (k + 1) * channels] = dot(chosen, partial).astype(BF16)

    corner = stencil[0:1, :]
    column = jnp.bitwise_and(corner, TILE_W - 1)
    row = (corner - column) // TILE_W
    rows = [bilinear[...].astype(F32), row.astype(F32), column.astype(F32)]
    rows.append(jnp.zeros((LANES - 6, slots), F32))
    extra = jnp.concatenate(rows, axis=0).astype(BF16)
    out[:, :LANES] = dot_dims(turn, extra, NT).astype(BF16)


def spread_of(extra, columns):
    extra = extra.astype(F32)
    corner = (extra[:, 4:5] * TILE_W + extra[:, 5:6]).astype(I32)
    delta = place((extra.shape[0], columns), 1) - corner
    spread = jnp.zeros(delta.shape, F32)
    for k, offset in enumerate((0, 1, TILE_W, TILE_W + 1)):
        spread = jnp.where(delta == offset, extra[:, k : k + 1], spread)
    return spread.astype(BF16)


def reply_kernel(cap, got, dy, state, out, terms):
    slots = got.shape[0]
    feat = state.shape[1]
    mine = (place((8, slots), 1) % cap == place((8, slots), 0)).astype(F32).astype(BF16)
    terms[...] = dot(mine, got[:, LANES:])
    spread = spread_of(got[:, :LANES], state.shape[0])
    out[:, :feat] = dot(spread, state[...]).astype(BF16)
    out[:, feat:] = dy[...]


def forward(profile, w_in, b_in, w_mid, b_mid):
    h1 = jnp.tanh(dot(profile, w_in[...]) + b_in[...]).astype(BF16)
    h2 = jnp.tanh(dot(h1, w_mid[...]) + b_mid[...]).astype(BF16)
    return h1, h2


def hidden_kernel(reply, w_in, b_in, w_mid, b_mid, b_out, h1, h2, b_kept):
    b_kept[...] = b_out[...]
    h1[...], h2[...] = forward(reply[:, : w_in.shape[0]], w_in, b_in, w_mid, b_mid)


def final_kernel(
    scale, back, got, h1, h2, even, odd, w_in, b_in, w_mid, b_mid, w_out, b_out,
    state_grad, radiance, bias_grad
):
    feat = w_in.shape[0]
    channels = bias_grad.shape[1]
    h2f, h1f = h2[...].astype(F32), h1[...].astype(F32)
    g2 = dot_dims(back[:, feat:], w_out[...], NT)
    g2 = (g2 * (1.0 - h2f * h2f)).astype(BF16)
    g1 = dot_dims(g2, w_mid[...], NT)
    g1 = (g1 * (1.0 - h1f * h1f)).astype(BF16)
    dprofile = dot_dims(g1, w_in[...], NT).astype(BF16)
    spread = spread_of(got[:, :LANES], state_grad.shape[0])
    state_grad[...] = dot_dims(spread, dprofile, TN)

    _, last = forward(back[:, :feat], w_in, b_in, w_mid, b_mid)
    radiance[...] = (dot(last, w_out[...]) + b_out[...]).astype(BF16)

    for k, half in enumerate((even, odd)):
        for j in range(2):
            for e in range(2):
                row = 4 * k + 2 * j + e
                bias_grad[row : row + 1, :] = (
                    half[j : j + 1, e * channels : (e + 1) * channels] * scale
                )


def call(kernel, out, *args, flops=0, touched=0, space=pltpu.VMEM, scratch=(), grant=GRANT):
    return pl.pallas_call(
        kernel,
        out_shape=out,
        in_specs=[pl.BlockSpec(memory_space=space)] * len(args),
        out_specs=jax.tree.map(lambda _: pl.BlockSpec(memory_space=pltpu.VMEM), out),
        scratch_shapes=scratch,
        compiler_params=pltpu.CompilerParams(vmem_limit_bytes=grant),
        cost_estimate=pl.CostEstimate(flops=flops, bytes_accessed=touched, transcendentals=0),
    )(*args)


def on_device(
    state, departures, stencil, bilinear, counts, predictors, w_in, b_in, w_mid, b_mid, w_out, b_out
):
    slots, channels = departures.shape
    columns, feat = state.shape
    npred = predictors.shape[0]
    peers, rows = lax.axis_size("tx"), lax.axis_size("ty")
    cap = slots // peers
    scale = 1.0 / math.sqrt(slots * peers * rows)
    b_in, b_mid, b_out = b_in[None], b_mid[None], b_out[None]
    shape = jax.ShapeDtypeStruct

    inputs = (departures, stencil.T, bilinear.T, counts[None], predictors)
    packed, dy = call(
        pack_kernel,
        (shape((slots, LANES + 2 * channels), BF16), shape((slots, channels), BF16)),
        *inputs,
        flops=40_000_000,
        touched=300_000,
        space=pl.ANY,
        scratch=[pltpu.VMEM(a.shape, a.dtype) for a in inputs]
        + [pltpu.SemaphoreType.DMA((len(inputs),))],
        grant=PACK_GRANT,
    )
    got = exchange(packed.reshape(peers, cap, -1), "tx").reshape(slots, -1)
    reply, terms = call(
        functools.partial(reply_kernel, cap),
        (shape((slots, feat + channels), BF16), shape((8, 2 * channels), F32)),
        got,
        dy,
        state,
        flops=50_000_000,
        touched=500_000,
    )
    back = exchange(reply.reshape(peers, cap, -1), "tx").reshape(slots, -1)
    h1, h2, b_out = call(
        hidden_kernel,
        (shape((slots, w_in.shape[1]), BF16),) * 2 + (shape((1, channels), F32),),
        reply,
        w_in,
        b_in,
        w_mid,
        b_mid,
        b_out,
        flops=130_000_000,
        touched=1_000_000,
    )
    terms = lax.psum(terms[:cap], "ty")
    other = lax.ppermute(terms, "tx", [(a, a ^ 1) for a in range(peers)])
    is_even = lax.axis_index("tx") % 2 == 0
    even = jnp.where(is_even, terms, other)
    odd = jnp.where(is_even, other, terms)
    state_grad, radiance, bias_grad = call(
        functools.partial(final_kernel, scale),
        (
            shape((columns, feat), F32),
            shape((slots, channels), BF16),
            shape((npred, channels), F32),
        ),
        back,
        got,
        h1,
        h2,
        even,
        odd,
        w_in,
        b_in,
        w_mid,
        b_mid,
        w_out,
        b_out,
        flops=400_000_000,
        touched=2_000_000,
    )
    return (radiance, state_grad, bias_grad)


def solution(mesh):
    both = P(("tx", "ty"), None)
    placed = (both, both, both, both, P(("tx", "ty")), P(None, ("tx", "ty"))) + (P(),) * 6
    return jax.shard_map(
        on_device,
        mesh=mesh,
        in_specs=placed,
        out_specs=(both, both, P()),
        check_vma=False,
    )
```

time: 74.3 us -> 74.3 us (level)
  the two profiles are of different devices: /device:TPU:8 before, /device:TPU:1 now
where the time goes in v4:
time: 74.3 us; the launch traced here: 73.1 us
  blocking collectives  51.1 us (69%)
  starting transfers between devices  11.7 us (16%)
  Pallas kernels  5.16 us (7%)
  local copies, waits for them, and re-layouts  4.09 us (6%)
  between operations  0.77 us (1%)
    all_to_all x1, blocking collectives, exchange(): return lax.all_to_all(block, axis, split_axis=0, concat_axis=0, tiled=True)  37.5 us
    psum x1, blocking collectives, on_device(): terms = lax.psum(terms[:cap], 'ty')  13.6 us
    all_to_all x1, starting transfers between devices, exchange(): return lax.all_to_all(block, axis, split_axis=0, concat_axis=0, tiled=True)  8.78 us
    pallas_call x4, Pallas kernels, call(): pl.pallas_call(kernel, out_shape=out, in_specs=[pl.BlockSpec(memory_space...  5.16 us
    ppermute x1, starting transfers between devices, on_device(): other = lax.ppermute(terms, 'tx', [(a, a ^ 1) for a in range(peers)])  2.97 us
    unnamed x16, local copies, waits for them, and re-layouts  2.17 us
  transfers between devices with their start and end apart: 2, of which 1 were waited for; matrix products, arithmetic and copies ran while one was open for 0% of the time, Pallas kernels for 1%

profile of v4, /device:TPU:1, one launch (start us, length us, event | category | flops | bytes accessed | tf_op | source)
XLA Modules:
  0.0 73.1 jit_solution(11663787045370683114)
XLA Ops:
  0.6 2.2 %shard_map.139 = (bf16[192,640]{1,0:T(8,128)(2,1)}, bf16[192,256]{1,0:T(8,128)(2,1)}) custom-call(bf16[192,256]{1,0:T(8,128)(2,1)} %departures_hbm.1, s32[4,192]{1,0:T(4,128)} %bitcast.11, bf16[4,192]{1,0:T(4,128)(2,1)} %bitcast.12, s32[1,96]{1,0:T(1,128)} %bitcast.13, f32[8,192]{1,0:T(8,128)} %predictors_hbm.1), custom_call_target="tpu_custom_call" | custom-call | flops 40000000 | bytes 300000 | tf_op jit(solution)/shard_map/pallas_call | solution.py:157
  2.9 1.0 %reshape.18 = bf16[96,2,640]{2,1,0:T(2,128)(2,1)S(1)} reshape(bf16[192,640]{1,0:T(8,128)(2,1)} %get-tuple-element.13) | data formatting | bytes 491520 | tf_op jit(solution)/shard_map/reshape | solution.py:192
  3.9 37.5 %all_to_all.10 = bf16[96,2,640]{2,1,0:T(2,128)(2,1)S(1)} all-to-all(bf16[96,2,640]{2,1,0:T(2,128)(2,1)S(1)} %reshape.18), channel_id=1, replica_groups=mesh['tx'=96,'ty'=8] {'tx'}, dimensions={0} | all-to-all | bytes 491520 | tf_op jit(solution)/shard_map/all_to_all | solution.py:21
  41.4 0.0 copy-start.2
  41.4 0.0 copy-start.4
  41.5 0.1 reshape.19.got
  41.5 0.8 %copy-done.2 = bf16[1024,128]{1,0:T(8,128)(2,1)S(1)} copy-done((bf16[1024,128]{1,0:T(8,128)(2,1)S(1)}, bf16[1024,128]{1,0:T(8,128)(2,1)}, u32[]{:S(2)}) %copy-start.2) | copy-done | bytes 262168
  42.4 0.0 copy-done.4
  42.4 0.0 copy-start
  42.4 0.5 shard_map.140
  43.0 0.7 reshape.20
  43.7 0.0 copy-start.1
  43.7 8.8 %all-to-all-start.1 = ((bf16[96,2,384]{2,1,0:T(2,128)(2,1)}), bf16[96,2,384]{2,1,0:T(2,128)(2,1)S(1)}, u32[]{:S(2)}, u32[]{:S(2)}) async-start(bf16[96,2,384]{2,1,0:T(2,128)(2,1)} %reshape.20), calls=%async_computation.1 | async-start | bytes 294912 | tf_op jit(solution)/shard_map/all_to_all | solution.py:21
  52.5 13.6 %psum.7 = f32[2,512]{1,0:T(2,128)S(1)} all-reduce(f32[2,512]{1,0:T(2,128)S(1)} %slice.3), channel_id=1, replica_groups=mesh['tx'=96,'ty'=8] {'ty'}, use_global_device_ids=true, to_apply=%region_0.0 | all-reduce | flops 1024 | bytes 8192 | tf_op jit(solution)/shard_map/psum | solution.py:215
  66.1 3.0 %collective-permute-start = (f32[2,512]{1,0:T(2,128)S(1)}, f32[2,512]{1,0:T(2,128)S(1)}, u32[]{:S(2)}, u32[]{:S(2)}) collective-permute-start(f32[2,512]{1,0:T(2,128)S(1)} %psum.7), channel_id=1, source_target_pairs={{0,8},{8,0},{16,24},{24,16},{32,40},{40,32},{48,56},{56,48},{64,72... | collective-permute-start | bytes 12296 | tf_op jit(solution)/shard_map/ppermute | solution.py:216
  69.0 0.0 copy-start.6
  69.0 0.0 copy-start.5
  69.1 0.0 copy-start.7
  69.1 0.0 copy-done
  69.1 0.0 copy-done.1
  69.1 0.6 copy-done.6
  69.7 0.0 copy-done.5
  69.7 0.0 copy-done.7
  69.7 0.4 shard_map.141
  70.1 0.0 copy-start.3
  70.2 0.2 collective-permute-done
  70.4 0.0 all-to-all-done.1
  70.4 0.1 reshape.21.back
  70.5 0.6 copy-done.3
  71.1 2.0 %shard_map.142 = (f32[1024,128]{1,0:T(8,128)}, bf16[192,256]{1,0:T(8,128)(2,1)}, f32[8,256]{1,0:T(8,128)}) custom-call(bf16[192,384]{1,0:T(8,128)(2,1)S(1)} %reshape.21.back, bf16[192,640]{1,0:T(8,128)(2,1)S(1)} %reshape.19.got, bf16[192,512]{1,0:T(8,128)(2,1)S(1)} %get-tuple-element.16.h1, bf16[192,512]{1,0:T(8,128)(2,1)S(1)} %get-tuple-element.17.h2, ...), custom_call_target="tpu_custom_call" | custom-call | flops 400000000 | bytes 2000000 | tf_op jit(solution)/shard_map/pallas_call | solution.py:157
  (2 shorter events, 0.0 us)
Async XLA Ops:
  41.4 1.0 %copy-start.2 = (bf16[1024,128]{1,0:T(8,128)(2,1)S(1)}, bf16[1024,128]{1,0:T(8,128)(2,1)}, u32[]{:S(2)}) copy-start(bf16[1024,128]{1,0:T(8,128)(2,1)} %state.1) | copy-start | bytes 786436
  41.4 1.0 %copy-start.4 = (bf16[192,256]{1,0:T(8,128)(2,1)S(1)}, bf16[192,256]{1,0:T(8,128)(2,1)}, u32[]{:S(2)}) copy-start(bf16[192,256]{1,0:T(8,128)(2,1)} %get-tuple-element.14.dy) | copy-start | bytes 294916
  42.4 26.7 %copy-start = (bf16[512,512]{1,0:T(8,128)(2,1)S(1)}, bf16[512,512]{1,0:T(8,128)(2,1)}, u32[]{:S(2)}) copy-start(bf16[512,512]{1,0:T(8,128)(2,1)} %w_mid.3) | copy-start | bytes 1572868
  43.7 25.4 %copy-start.1 = (bf16[128,512]{1,0:T(8,128)(2,1)S(1)}, bf16[128,512]{1,0:T(8,128)(2,1)}, u32[]{:S(2)}) copy-start(bf16[128,512]{1,0:T(8,128)(2,1)} %w_in.3) | copy-start | bytes 393220
  43.7 26.7 %all-to-all-start.1 = ((bf16[96,2,384]{2,1,0:T(2,128)(2,1)}), bf16[96,2,384]{2,1,0:T(2,128)(2,1)S(1)}, u32[]{:S(2)}, u32[]{:S(2)}) async-start(bf16[96,2,384]{2,1,0:T(2,128)(2,1)} %reshape.20), calls=%async_computation.1 | async-start | bytes 294912 | tf_op jit(solution)/shard_map/all_to_all | solution.py:21
  66.1 4.3 %collective-permute-start = (f32[2,512]{1,0:T(2,128)S(1)}, f32[2,512]{1,0:T(2,128)S(1)}, u32[]{:S(2)}, u32[]{:S(2)}) collective-permute-start(f32[2,512]{1,0:T(2,128)S(1)} %psum.7), channel_id=1, source_target_pairs={{0,8},{8,0},{16,24},{24,16},{32,40},{40,32},{48,56},{56,48},{64,72... | collective-permute-start | bytes 12296 | tf_op jit(solution)/shard_map/ppermute | solution.py:216
  69.0 0.7 copy-start.6
  69.0 0.7 copy-start.5
  69.1 0.7 copy-start.7
  70.1 1.0 %copy-start.3 = (bf16[512,256]{1,0:T(8,128)(2,1)S(1)}, bf16[512,256]{1,0:T(8,128)(2,1)}, u32[]{:S(2)}) copy-start(bf16[512,256]{1,0:T(8,128)(2,1)} %w_out.1) | copy-start | bytes 786436

commit v5 on v4

--- a/solution.py
+++ b/solution.py
@@ -42,8 +42,23 @@
     return x.astype(BF16).astype(F32)
 
 
+def masked_by(departures, counts):
+    slots, peers = departures.shape[0], counts.shape[1]
+    cap = slots // peers
+    holds = (place((slots, peers), 0) // cap == place((slots, peers), 1)).astype(F32).astype(BF16)
+    counted = jnp.broadcast_to(counts[...].astype(F32), (8, peers)).astype(BF16)
+    count_of = dot_dims(holds, counted, NT)[:, 0:1]
+    live = (place((slots, 1), 0) % cap).astype(F32) < count_of
+    return jnp.where(live, departures[...].astype(F32), 0.0).astype(BF16)
+
+
+def keep_kernel(state, departures, counts, state_kept, dy):
+    state_kept[...] = state[...]
+    dy[...] = masked_by(departures, counts)
+
+
 def pack_kernel(
-    departures_hbm, stencil_hbm, bilinear_hbm, counts_hbm, predictors_hbm, out, masked,
+    departures_hbm, stencil_hbm, bilinear_hbm, counts_hbm, predictors_hbm, out,
     departures, stencil, bilinear, counts, predictors, arrived
 ):
     pairs = (
@@ -63,15 +78,10 @@
     peers = counts.shape[1]
     cap = slots // peers
     npred = predictors.shape[0]
-    holds = (place((slots, peers), 0) // cap == place((slots, peers), 1)).astype(F32).astype(BF16)
     turn = identity(slots, slots)
     for copy in copies:
         copy.wait()
-    counted = jnp.broadcast_to(counts[...].astype(F32), (8, peers)).astype(BF16)
-    count_of = dot_dims(holds, counted, NT)[:, 0:1]
-    live = (place((slots, 1), 0) % cap).astype(F32) < count_of
-    dy = jnp.where(live, departures[...].astype(F32), 0.0).astype(BF16)
-    masked[...] = dy
+    dy = masked_by(departures, counts)
 
     pred = predictors[...]
     part0 = rounded(pred)
@@ -84,7 +94,9 @@
     partial = partial.astype(BF16)
     for k in range(2):
         chosen = (which == slot + k).astype(F32).astype(BF16)
-        out[:, LANES + k * channels : LANES + (k + 1) * channels] = dot(chosen, partial).astype(BF16)
+        out[:, :, LANES + k * channels : LANES + (k + 1) * channels] = (
+            dot(chosen, partial).astype(BF16).reshape(peers, cap, channels)
+        )
 
     corner = stencil[0:1, :]
     column = jnp.bitwise_and(corner, TILE_W - 1)
@@ -92,7 +104,7 @@
     rows = [bilinear[...].astype(F32), row.astype(F32), column.astype(F32)]
     rows.append(jnp.zeros((LANES - 6, slots), F32))
     extra = jnp.concatenate(rows, axis=0).astype(BF16)
-    out[:, :LANES] = dot_dims(turn, extra, NT).astype(BF16)
+    out[:, :, :LANES] = dot_dims(turn, extra, NT).astype(BF16).reshape(peers, cap, LANES)
 
 
 def spread_of(extra, columns):
@@ -105,14 +117,17 @@
     return spread.astype(BF16)
 
 
-def reply_kernel(cap, got, dy, state, out, terms):
+def reply_kernel(cap, got, dy, state, out, terms, kept):
     slots = got.shape[0]
     feat = state.shape[1]
     mine = (place((8, slots), 1) % cap == place((8, slots), 0)).astype(F32).astype(BF16)
     terms[...] = dot(mine, got[:, LANES:])
     spread = spread_of(got[:, :LANES], state.shape[0])
-    out[:, :feat] = dot(spread, state[...]).astype(BF16)
-    out[:, feat:] = dy[...]
+    shape = out.shape[:2]
+    profile = dot(spread, state[...]).astype(BF16)
+    kept[...] = profile
+    out[:, :, :feat] = profile.reshape(*shape, feat)
+    out[:, :, feat:] = dy[...].reshape(*shape, dy.shape[1])
 
 
 def forward(profile, w_in, b_in, w_mid, b_mid):
@@ -121,9 +136,9 @@
     return h1, h2
 
 
-def hidden_kernel(reply, w_in, b_in, w_mid, b_mid, b_out, h1, h2, b_kept):
+def hidden_kernel(profile, w_in, b_in, w_mid, b_mid, w_out, b_out, h1, h2, b_kept):
     b_kept[...] = b_out[...]
-    h1[...], h2[...] = forward(reply[:, : w_in.shape[0]], w_in, b_in, w_mid, b_mid)
+    h1[...], h2[...] = forward(profile[...], w_in, b_in, w_mid, b_mid)
 
 
 def final_kernel(
@@ -178,9 +193,9 @@
     shape = jax.ShapeDtypeStruct
 
     inputs = (departures, stencil.T, bilinear.T, counts[None], predictors)
-    packed, dy = call(
+    packed = call(
         pack_kernel,
-        (shape((slots, LANES + 2 * channels), BF16), shape((slots, channels), BF16)),
+        shape((peers, cap, LANES + 2 * channels), BF16),
         *inputs,
         flops=40_000_000,
         touched=300_000,
@@ -189,30 +204,46 @@
         + [pltpu.SemaphoreType.DMA((len(inputs),))],
         grant=PACK_GRANT,
     )
-    got = exchange(packed.reshape(peers, cap, -1), "tx").reshape(slots, -1)
-    reply, terms = call(
+    state, dy = call(
+        keep_kernel,
+        (shape(state.shape, BF16), shape(departures.shape, BF16)),
+        state,
+        departures,
+        counts[None],
+        flops=2_000_000_000,
+        touched=2_000_000,
+    )
+    got = exchange(packed, "tx").reshape(slots, -1)
+    reply, terms, profile = call(
         functools.partial(reply_kernel, cap),
-        (shape((slots, feat + channels), BF16), shape((8, 2 * channels), F32)),
+        (
+            shape((peers, cap, feat + channels), BF16),
+            shape((8, 2 * channels), F32),
+            shape((slots, feat), BF16),
+        ),
         got,
         dy,
         state,
         flops=50_000_000,
         touched=500_000,
     )
-    back = exchange(reply.reshape(peers, cap, -1), "tx").reshape(slots, -1)
+    back = exchange(reply, "tx").reshape(slots, -1)
     h1, h2, b_out = call(
         hidden_kernel,
         (shape((slots, w_in.shape[1]), BF16),) * 2 + (shape((1, channels), F32),),
-        reply,
+        profile,
         w_in,
         b_in,
         w_mid,
         b_mid,
+        w_out,
         b_out,
         flops=130_000_000,
         touched=1_000_000,
     )
-    terms = lax.psum(terms[:cap], "ty")
+    terms = terms[:cap]
+    for step in (1 << k for k in range((rows - 1).bit_length())):
+        terms = terms + lax.ppermute(terms, "ty", [(b, b ^ step) for b in range(rows)])
     other = lax.ppermute(terms, "tx", [(a, a ^ 1) for a in range(peers)])
     is_even = lax.axis_index("tx") % 2 == 0
     even = jnp.where(is_even, terms, other)

time: 74.3 us -> 73.4 us (0.988)
  the two profiles are of different devices: /device:TPU:1 before, /device:TPU:4 now
where the time goes in v5:
time: 73.4 us; the launch traced here: 72.9 us
  starting transfers between devices  38.9 us (53%)
  waiting for transfers between devices  26.2 us (36%)
  Pallas kernels  6.09 us (8%)
  between operations  0.87 us (1%)
  local copies, waits for them, and re-layouts  0.85 us (1%)
    all_to_all x2, starting transfers between devices, exchange(): return lax.all_to_all(block, axis, split_axis=0, concat_axis=0, tiled=True)  28.1 us
    all_to_all x2, waiting for transfers between devices, exchange(): return lax.all_to_all(block, axis, split_axis=0, concat_axis=0, tiled=True)  18.2 us
    ppermute x3, starting transfers between devices, on_device(): lax.ppermute(terms, 'ty', [(b, b ^ step) for b in range(rows)])  7.54 us
    ppermute x3, waiting for transfers between devices, on_device(): lax.ppermute(terms, 'ty', [(b, b ^ step) for b in range(rows)])  6.97 us
    pallas_call x5, Pallas kernels, call(): pl.pallas_call(kernel, out_shape=out, in_specs=[pl.BlockSpec(memory_space...  6.09 us
    ppermute x1, starting transfers between devices, on_device(): other = lax.ppermute(terms, 'tx', [(a, a ^ 1) for a in range(peers)])  3.27 us
  transfers between devices with their start and end apart: 6, of which 4 were waited for; matrix products, arithmetic and copies ran while one was open for 0% of the time, Pallas kernels for 1%

profile of v5, /device:TPU:4, one launch (start us, length us, event | category | flops | bytes accessed | tf_op | source)
XLA Modules:
  0.0 72.9 jit_solution(1512144896830450877)
XLA Ops:
  0.6 2.2 %shard_map.139 = bf16[96,2,640]{2,1,0:T(2,128)(2,1)} custom-call(bf16[192,256]{1,0:T(8,128)(2,1)} %departures.1, s32[4,192]{1,0:T(4,128)} %bitcast.13, bf16[4,192]{1,0:T(4,128)(2,1)} %bitcast.14, s32[1,96]{1,0:T(1,128)} %bitcast.11, f32[8,192]{1,0:T(8,128)} %predictors_hbm.1), custom_call_target="tpu_custom_call" | custom-call | flops 40000000 | bytes 300000 | tf_op jit(solution)/shard_map/pallas_call | solution.py:172
  2.9 0.0 copy-start.3
  2.9 0.0 copy-start.7
  2.9 0.0 copy-start.8
  2.9 22.1 %all-to-all-start = ((bf16[96,2,640]{2,1,0:T(2,128)(2,1)}), bf16[96,2,640]{2,1,0:T(2,128)(2,1)S(1)}, u32[]{:S(2)}, u32[]{:S(2)}) async-start(bf16[96,2,640]{2,1,0:T(2,128)(2,1)} %shard_map.139), calls=%async_computation | async-start | bytes 491520 | tf_op jit(solution)/shard_map/all_to_all | solution.py:21
  25.0 0.0 copy-done.3
  25.1 0.0 copy-done.7
  25.1 0.0 copy-done.8
  25.1 0.2 shard_map.140
  25.3 18.2 %all-to-all-done = bf16[96,2,640]{2,1,0:T(2,128)(2,1)S(1)} async-done(((bf16[96,2,640]{2,1,0:T(2,128)(2,1)}), bf16[96,2,640]{2,1,0:T(2,128)(2,1)S(1)}, u32[]{:S(2)}, u32[]{:S(2)}) %all-to-all-start) | async-done | bytes 245792 | tf_op jit(solution)/shard_map/all_to_all | solution.py:21
  43.5 0.1 reshape.12.got
  43.6 0.0 copy-start
  43.6 0.0 copy-start.2
  43.6 1.2 %shard_map.141 = (bf16[96,2,384]{2,1,0:T(2,128)(2,1)}, f32[8,512]{1,0:T(8,128)S(1)}, bf16[192,128]{1,0:T(8,128)(2,1)S(1)}) custom-call(bf16[192,640]{1,0:T(8,128)(2,1)S(1)} %reshape.12.got, bf16[192,256]{1,0:T(8,128)(2,1)S(1)} %get-tuple-element.14.dy, bf16[1024,128]{1,0:T(8,128)(2,1)S(1)} %get-tuple-element.15.state), custom_call_target="tpu_custom_call" | custom-call | flops 50000000 | bytes 500000 | tf_op jit(solution)/shard_map/pallas_call | solution.py:172
  44.8 0.0 copy-start.1
  44.8 2.0 %collective-permute-start = (f32[2,512]{1,0:T(2,128)S(1)}, f32[2,512]{1,0:T(2,128)S(1)}, u32[]{:S(2)}, u32[]{:S(2)}) collective-permute-start(f32[2,512]{1,0:T(2,128)S(1)} %slice.3), channel_id=1, source_target_pairs={{0,1},{1,0},{2,3},{3,2},{4,5},{5,4},{6,7},{7,6},{8,9},{9,8},{10,11... | collective-permute-start | bytes 12296 | tf_op jit(solution)/shard_map/ppermute | solution.py:246
  46.9 6.0 %all-to-all-start.1 = ((bf16[96,2,384]{2,1,0:T(2,128)(2,1)}), bf16[96,2,384]{2,1,0:T(2,128)(2,1)S(1)}, u32[]{:S(2)}, u32[]{:S(2)}) async-start(bf16[96,2,384]{2,1,0:T(2,128)(2,1)} %get-tuple-element.16), calls=%async_computation.1 | async-start | bytes 294912 | tf_op jit(solution)/shard_map/all_to_all | solution.py:21
  52.8 0.0 collective-permute-done
  52.8 3.1 %collective-permute-start.1 = (f32[2,512]{1,0:T(2,128)S(1)}, f32[2,512]{1,0:T(2,128)S(1)}, u32[]{:S(2)}, u32[]{:S(2)}) collective-permute-start(f32[2,512]{1,0:T(2,128)S(1)} %slice_add_fusion), channel_id=1, source_target_pairs={{0,2},{1,3},{2,0},{3,1},{4,6},{5,7},{6,4},{7,5},{8,10},{9,11},{10,... | collective-permute-start | bytes 12296 | tf_op jit(solution)/shard_map/ppermute | solution.py:246
  56.0 2.4 %collective-permute-done.1 = f32[2,512]{1,0:T(2,128)S(1)} collective-permute-done((f32[2,512]{1,0:T(2,128)S(1)}, f32[2,512]{1,0:T(2,128)S(1)}, u32[]{:S(2)}, u32[]{:S(2)}) %collective-permute-start.1) | collective-permute-done | bytes 4128 | tf_op jit(solution)/shard_map/ppermute | solution.py:246
  58.4 2.4 %collective-permute-start.2 = (f32[2,512]{1,0:T(2,128)S(1)}, f32[2,512]{1,0:T(2,128)S(1)}, u32[]{:S(2)}, u32[]{:S(2)}) collective-permute-start(f32[2,512]{1,0:T(2,128)S(1)} %add.15), channel_id=1, source_target_pairs={{0,4},{1,5},{2,6},{3,7},{4,0},{5,1},{6,2},{7,3},{8,12},{9,13},{10,... | collective-permute-start | bytes 12296 | tf_op jit(solution)/shard_map/ppermute | solution.py:246
  60.8 4.6 %collective-permute-done.2 = f32[2,512]{1,0:T(2,128)S(1)} collective-permute-done((f32[2,512]{1,0:T(2,128)S(1)}, f32[2,512]{1,0:T(2,128)S(1)}, u32[]{:S(2)}, u32[]{:S(2)}) %collective-permute-start.2) | collective-permute-done | bytes 4128 | tf_op jit(solution)/shard_map/ppermute | solution.py:246
  65.3 3.3 %collective-permute-start.3 = (f32[2,512]{1,0:T(2,128)S(1)}, f32[2,512]{1,0:T(2,128)S(1)}, u32[]{:S(2)}, u32[]{:S(2)}) collective-permute-start(f32[2,512]{1,0:T(2,128)S(1)} %add.16), channel_id=1, source_target_pairs={{0,8},{8,0},{16,24},{24,16},{32,40},{40,32},{48,56},{56,48},{64,72... | collective-permute-start | bytes 12296 | tf_op jit(solution)/shard_map/ppermute | solution.py:247
  68.6 0.0 copy-start.5
  68.6 0.0 copy-start.4
  68.6 0.0 copy-start.6
  68.7 0.0 copy-done
  68.7 0.0 copy-done.2
  68.7 0.0 copy-done.1
  68.7 0.6 copy-done.5
  69.3 0.0 copy-done.4
  69.3 0.0 copy-done.6
  69.3 0.4 shard_map.142
  69.7 1.1 %collective-permute-done.3 = f32[2,512]{1,0:T(2,128)S(1)} collective-permute-done((f32[2,512]{1,0:T(2,128)S(1)}, f32[2,512]{1,0:T(2,128)S(1)}, u32[]{:S(2)}, u32[]{:S(2)}) %collective-permute-start.3) | collective-permute-done | bytes 4128 | tf_op jit(solution)/shard_map/ppermute | solution.py:247
  70.8 0.0 all-to-all-done.1
  70.9 0.1 reshape.13.back
  70.9 2.0 %shard_map.143 = (f32[1024,128]{1,0:T(8,128)}, bf16[192,256]{1,0:T(8,128)(2,1)}, f32[8,256]{1,0:T(8,128)}) custom-call(bf16[192,384]{1,0:T(8,128)(2,1)S(1)} %reshape.13.back, bf16[192,640]{1,0:T(8,128)(2,1)S(1)} %reshape.12.got, bf16[192,512]{1,0:T(8,128)(2,1)S(1)} %get-tuple-element.18.h1, bf16[192,512]{1,0:T(8,128)(2,1)S(1)} %get-tuple-element.19.h2, ...), custom_call_target="tpu_custom_call" | custom-call | flops 400000000 | bytes 2000000 | tf_op jit(solution)/shard_map/pallas_call | solution.py:172
  (5 shorter events, 0.0 us)
Async XLA Ops:
  2.9 22.2 %copy-start.3 = (bf16[192,256]{1,0:T(8,128)(2,1)S(1)}, bf16[192,256]{1,0:T(8,128)(2,1)}, u32[]{:S(2)}) copy-start(bf16[192,256]{1,0:T(8,128)(2,1)} %departures.1) | copy-start | bytes 294916
  2.9 22.2 %copy-start.7 = (s32[96]{0:T(128)S(1)}, s32[96]{0:T(128)}, u32[]{:S(2)}) copy-start(s32[96]{0:T(128)} %param.16) | copy-start | bytes 1156
  2.9 22.2 %copy-start.8 = (bf16[1024,128]{1,0:T(8,128)(2,1)S(1)}, bf16[1024,128]{1,0:T(8,128)(2,1)}, u32[]{:S(2)}) copy-start(bf16[1024,128]{1,0:T(8,128)(2,1)} %state.1) | copy-start | bytes 786436
  2.9 40.6 %all-to-all-start = ((bf16[96,2,640]{2,1,0:T(2,128)(2,1)}), bf16[96,2,640]{2,1,0:T(2,128)(2,1)S(1)}, u32[]{:S(2)}, u32[]{:S(2)}) async-start(bf16[96,2,640]{2,1,0:T(2,128)(2,1)} %shard_map.139), calls=%async_computation | async-start | bytes 491520 | tf_op jit(solution)/shard_map/all_to_all | solution.py:21
  43.6 25.1 %copy-start = (bf16[512,512]{1,0:T(8,128)(2,1)S(1)}, bf16[512,512]{1,0:T(8,128)(2,1)}, u32[]{:S(2)}) copy-start(bf16[512,512]{1,0:T(8,128)(2,1)} %w_mid.3) | copy-start | bytes 1572868
  43.6 25.1 %copy-start.2 = (bf16[128,512]{1,0:T(8,128)(2,1)S(1)}, bf16[128,512]{1,0:T(8,128)(2,1)}, u32[]{:S(2)}) copy-start(bf16[128,512]{1,0:T(8,128)(2,1)} %w_in.3) | copy-start | bytes 393220
  44.8 23.9 %copy-start.1 = (bf16[512,256]{1,0:T(8,128)(2,1)S(1)}, bf16[512,256]{1,0:T(8,128)(2,1)}, u32[]{:S(2)}) copy-start(bf16[512,256]{1,0:T(8,128)(2,1)} %w_out.3) | copy-start | bytes 786436
  44.8 8.0 %collective-permute-start = (f32[2,512]{1,0:T(2,128)S(1)}, f32[2,512]{1,0:T(2,128)S(1)}, u32[]{:S(2)}, u32[]{:S(2)}) collective-permute-start(f32[2,512]{1,0:T(2,128)S(1)} %slice.3), channel_id=1, source_target_pairs={{0,1},{1,0},{2,3},{3,2},{4,5},{5,4},{6,7},{7,6},{8,9},{9,8},{10,11... | collective-permute-start | bytes 12296 | tf_op jit(solution)/shard_map/ppermute | solution.py:246
  46.9 24.0 %all-to-all-start.1 = ((bf16[96,2,384]{2,1,0:T(2,128)(2,1)}), bf16[96,2,384]{2,1,0:T(2,128)(2,1)S(1)}, u32[]{:S(2)}, u32[]{:S(2)}) async-start(bf16[96,2,384]{2,1,0:T(2,128)(2,1)} %get-tuple-element.16), calls=%async_computation.1 | async-start | bytes 294912 | tf_op jit(solution)/shard_map/all_to_all | solution.py:21
  52.8 5.5 %collective-permute-start.1 = (f32[2,512]{1,0:T(2,128)S(1)}, f32[2,512]{1,0:T(2,128)S(1)}, u32[]{:S(2)}, u32[]{:S(2)}) collective-permute-start(f32[2,512]{1,0:T(2,128)S(1)} %slice_add_fusion), channel_id=1, source_target_pairs={{0,2},{1,3},{2,0},{3,1},{4,6},{5,7},{6,4},{7,5},{8,10},{9,11},{10,... | collective-permute-start | bytes 12296 | tf_op jit(solution)/shard_map/ppermute | solution.py:246
  58.4 7.0 %collective-permute-start.2 = (f32[2,512]{1,0:T(2,128)S(1)}, f32[2,512]{1,0:T(2,128)S(1)}, u32[]{:S(2)}, u32[]{:S(2)}) collective-permute-start(f32[2,512]{1,0:T(2,128)S(1)} %add.15), channel_id=1, source_target_pairs={{0,4},{1,5},{2,6},{3,7},{4,0},{5,1},{6,2},{7,3},{8,12},{9,13},{10,... | collective-permute-start | bytes 12296 | tf_op jit(solution)/shard_map/ppermute | solution.py:246
  65.3 5.5 %collective-permute-start.3 = (f32[2,512]{1,0:T(2,128)S(1)}, f32[2,512]{1,0:T(2,128)S(1)}, u32[]{:S(2)}, u32[]{:S(2)}) collective-permute-start(f32[2,512]{1,0:T(2,128)S(1)} %add.16), channel_id=1, source_target_pairs={{0,8},{8,0},{16,24},{24,16},{32,40},{40,32},{48,56},{56,48},{64,72... | collective-permute-start | bytes 12296 | tf_op jit(solution)/shard_map/ppermute | solution.py:247
  68.6 0.7 copy-start.5
  68.6 0.7 copy-start.4
  68.6 0.7 copy-start.6

commit v6 on v3

v6 whole, which is shorter than its diff:
```python
import functools
import math

import jax
import jax.numpy as jnp
from jax import lax
from jax.experimental import pallas as pl
from jax.experimental.pallas import tpu as pltpu
from jax.sharding import PartitionSpec as P

F32, BF16, I32 = jnp.float32, jnp.bfloat16, jnp.int32
NT = (((1,), (1,)), ((), ()))
TN = (((0,), (0,)), ((), ()))
TILE_W = 32
LANES = 128
GRANT = 40 * 1024 * 1024
PACK_GRANT = 60 * 1024 * 1024


def exchange(block, axis):
    return lax.all_to_all(block, axis, split_axis=0, concat_axis=0, tiled=True)


def dot(a, b):
    return jnp.dot(a, b, preferred_element_type=F32)


def dot_dims(a, b, dims):
    return lax.dot_general(a, b, dims, preferred_element_type=F32)


def place(shape, dim):
    return lax.broadcasted_iota(I32, shape, dim)


def identity(rows, columns):
    shape = (rows, columns)
    return (place(shape, 0) == place(shape, 1)).astype(F32).astype(BF16)


def rounded(x):
    return x.astype(BF16).astype(F32)


def masked_by(departures, counts):
    slots, peers = departures.shape[0], counts.shape[1]
    cap = slots // peers
    holds = (place((slots, peers), 0) // cap == place((slots, peers), 1)).astype(F32).astype(BF16)
    counted = jnp.broadcast_to(counts[...].astype(F32), (8, peers)).astype(BF16)
    count_of = dot_dims(holds, counted, NT)[:, 0:1]
    live = (place((slots, 1), 0) % cap).astype(F32) < count_of
    return jnp.where(live, departures[...].astype(F32), 0.0).astype(BF16)


def keep_kernel(state, state_kept):
    state_kept[...] = state[...]


def pack_kernel(
    departures_hbm, stencil_hbm, bilinear_hbm, counts_hbm, predictors_hbm, out,
    departures, stencil, bilinear, counts, predictors, arrived
):
    pairs = (
        (counts_hbm, counts),
        (departures_hbm, departures),
        (predictors_hbm, predictors),
        (stencil_hbm, stencil),
        (bilinear_hbm, bilinear),
    )
    copies = [
        pltpu.make_async_copy(source, target, arrived.at[k])
        for k, (source, target) in enumerate(pairs)
    ]
    for copy in copies:
        copy.start()
    slots, channels = departures.shape
    peers = counts.shape[1]
    cap = slots // peers
    npred = predictors.shape[0]
    turn = identity(slots, slots)
    for copy in copies:
        copy.wait()
    dy = masked_by(departures, counts)
    out[:, :, :channels] = dy.reshape(peers, cap, channels)

    pred = predictors[...]
    part0 = rounded(pred)
    part1 = rounded(pred - part0)
    part2 = pred - part0 - part1
    thirds = dot(jnp.concatenate([part0, part1, part2], axis=0).astype(BF16), dy)
    partial = thirds[:npred] + thirds[npred : 2 * npred] + thirds[2 * npred :]
    rest = channels - LANES
    upper = jnp.where(place((npred, rest), 1) >= slots - LANES, partial[:, LANES:], 0.0)
    upper = jnp.concatenate([upper, jnp.zeros((npred, slots - rest), F32)], axis=1)
    lower = partial[:, :slots]
    corner = stencil[0:1, :]
    column = jnp.bitwise_and(corner, TILE_W - 1)
    row = (corner - column) // TILE_W
    rows = [
        bilinear[...].astype(F32),
        row.astype(F32),
        column.astype(F32),
        jnp.zeros((2, slots), F32),
        rounded(lower),
        lower - rounded(lower),
        rounded(upper),
        upper - rounded(upper),
        jnp.zeros((LANES - 8 - 4 * npred, slots), F32),
    ]
    extra = dot_dims(turn, jnp.concatenate(rows, axis=0).astype(BF16), NT).astype(BF16)
    out[:, :, channels:] = extra.reshape(peers, cap, LANES)


def spread_of(extra, columns):
    extra = extra.astype(F32)
    corner = (extra[:, 4:5] * TILE_W + extra[:, 5:6]).astype(I32)
    delta = place((extra.shape[0], columns), 1) - corner
    spread = jnp.zeros(delta.shape, F32)
    for k, offset in enumerate((0, 1, TILE_W, TILE_W + 1)):
        spread = jnp.where(delta == offset, extra[:, k : k + 1], spread)
    return spread.astype(BF16)


def reply_kernel(npred, got, state, out, kept):
    slots, width = got.shape
    peers, cap = out.shape[:2]
    feat = state.shape[1]
    extra = got[:, width - LANES :]
    mine = (place((8, slots), 1) % cap == place((8, slots), 0)).astype(F32).astype(BF16)
    total = dot(mine, extra)
    joined = total + pltpu.roll(total, LANES - npred, 1)
    high = rounded(joined)
    low = pltpu.roll(joined - high, npred, 1)
    lanes = place((8, LANES), 1)
    is_high = ((lanes >= 8) & (lanes < 8 + npred)) | (
        (lanes >= 8 + 2 * npred) & (lanes < 8 + 3 * npred)
    )
    tail = jnp.where(is_high, high, low).astype(BF16)
    for peer in range(peers):
        out[peer, :, feat:] = tail[:cap]
    spread = spread_of(extra, state.shape[0])
    profile = dot(spread, state[...]).astype(BF16)
    kept[...] = profile
    out[:, :, :feat] = profile.reshape(peers, cap, feat)


def forward(profile, w_in, b_in, w_mid, b_mid):
    h1 = jnp.tanh(dot(profile, w_in[...]) + b_in[...]).astype(BF16)
    h2 = jnp.tanh(dot(h1, w_mid[...]) + b_mid[...]).astype(BF16)
    return h1, h2


def grad_kernel(got, profile, w_in, b_in, w_mid, b_mid, w_out, b_out, out, b_kept):
    width = got.shape[1]
    b_kept[...] = b_out[...]
    h1, h2 = forward(profile[...], w_in, b_in, w_mid, b_mid)
    h2, h1 = h2.astype(F32), h1.astype(F32)
    g2 = dot_dims(got[:, : width - LANES], w_out[...], NT)
    g2 = (g2 * (1.0 - h2 * h2)).astype(BF16)
    g1 = dot_dims(g2, w_mid[...], NT)
    g1 = (g1 * (1.0 - h1 * h1)).astype(BF16)
    dprofile = dot_dims(g1, w_in[...], NT).astype(BF16)
    spread = spread_of(got[:, width - LANES :], out.shape[0])
    out[...] = dot_dims(spread, dprofile, TN)


def bias_kernel(scale, back, out):
    slots, width = back.shape
    npred, channels = out.shape[1:]
    turned = dot_dims(back[:, width - LANES :], identity(slots, channels), TN)
    at = lambda k: turned[8 + k * npred : 8 + (k + 1) * npred]
    lower, upper = (at(0) + at(1)) * scale, (at(2) + at(3)) * scale
    lanes = place((npred, channels - LANES), 1)
    second = jnp.where(lanes < slots - LANES, lower[:, LANES:], upper[:, : channels - LANES])
    for peer in range(out.shape[0]):
        out[peer, :, :LANES] = lower[:, :LANES]
        out[peer, :, LANES:] = second


def radiance_kernel(back, w_in, b_in, w_mid, b_mid, w_out, b_out, radiance):
    _, h2 = forward(back[:, : w_in.shape[0]], w_in, b_in, w_mid, b_mid)
    radiance[...] = (dot(h2, w_out[...]) + b_out[...]).astype(BF16)


def sum_kernel(shared, out):
    total = shared[0]
    for peer in range(1, shared.shape[0]):
        total = total + shared[peer]
    out[...] = total


def call(kernel, out, *args, flops=0, touched=0, space=pltpu.VMEM, scratch=(), grant=GRANT):
    return pl.pallas_call(
        kernel,
        out_shape=out,
        in_specs=[pl.BlockSpec(memory_space=space)] * len(args),
        out_specs=jax.tree.map(lambda _: pl.BlockSpec(memory_space=pltpu.VMEM), out),
        scratch_shapes=scratch,
        compiler_params=pltpu.CompilerParams(vmem_limit_bytes=grant),
        cost_estimate=pl.CostEstimate(flops=flops, bytes_accessed=touched, transcendentals=0),
    )(*args)


def on_device(
    state, departures, stencil, bilinear, counts, predictors, w_in, b_in, w_mid, b_mid, w_out, b_out
):
    slots, channels = departures.shape
    columns, feat = state.shape
    npred = predictors.shape[0]
    peers, rows = lax.axis_size("tx"), lax.axis_size("ty")
    cap = slots // peers
    scale = 1.0 / math.sqrt(slots * peers * rows)
    b_in, b_mid, b_out = b_in[None], b_mid[None], b_out[None]
    shape = jax.ShapeDtypeStruct

    inputs = (departures, stencil.T, bilinear.T, counts[None], predictors)
    packed = call(
        pack_kernel,
        shape((peers, cap, channels + LANES), BF16),
        *inputs,
        flops=40_000_000,
        touched=300_000,
        space=pl.ANY,
        scratch=[pltpu.VMEM(a.shape, a.dtype) for a in inputs]
        + [pltpu.SemaphoreType.DMA((len(inputs),))],
        grant=PACK_GRANT,
    )
    state = call(
        keep_kernel, shape(state.shape, BF16), state, flops=2_000_000_000, touched=2_000_000
    )
    got = exchange(packed, "tx").reshape(slots, -1)
    reply, profile = call(
        functools.partial(reply_kernel, npred),
        (shape((peers, cap, feat + LANES), BF16), shape((slots, feat), BF16)),
        got,
        state,
        flops=50_000_000,
        touched=500_000,
    )
    back = exchange(reply, "tx").reshape(slots, -1)
    state_grad, b_out = call(
        grad_kernel,
        (shape((columns, feat), F32), shape((1, channels), F32)),
        got,
        profile,
        w_in,
        b_in,
        w_mid,
        b_mid,
        w_out,
        b_out,
        flops=400_000_000,
        touched=2_000_000,
    )
    shared = call(
        functools.partial(bias_kernel, scale),
        shape((rows, npred, channels), F32),
        back,
        flops=10_000_000,
        touched=200_000,
    )
    shared = exchange(shared, "ty")
    radiance = call(
        radiance_kernel,
        shape((slots, channels), BF16),
        back,
        w_in,
        b_in,
        w_mid,
        b_mid,
        w_out,
        b_out,
        flops=2_000_000_000,
        touched=2_000_000,
    )
    bias_grad = call(
        sum_kernel, shape((npred, channels), F32), shared, flops=20_000, touched=70_000
    )
    return (radiance, state_grad, bias_grad)


def solution(mesh):
    both = P(("tx", "ty"), None)
    placed = (both, both, both, both, P(("tx", "ty")), P(None, ("tx", "ty"))) + (P(),) * 6
    return jax.shard_map(
        on_device,
        mesh=mesh,
        in_specs=placed,
        out_specs=(both, both, P()),
        check_vma=False,
    )
```

time: 74.3 us -> 75 us (level)
  the two profiles are of different devices: /device:TPU:8 before, /device:TPU:1 now
where the time goes in v6:
time: 75 us; the launch traced here: 74.7 us
  starting transfers between devices  37.1 us (49%)
  waiting for transfers between devices  27.9 us (37%)
  Pallas kernels  8.12 us (11%)
  local copies, waits for them, and re-layouts  0.77 us (1%)
  between operations  0.76 us (1%)
    all_to_all x3, starting transfers between devices, exchange(): return lax.all_to_all(block, axis, split_axis=0, concat_axis=0, tiled=True)  37.1 us
    all_to_all x3, waiting for transfers between devices, exchange(): return lax.all_to_all(block, axis, split_axis=0, concat_axis=0, tiled=True)  27.9 us
    pallas_call x7, Pallas kernels, call(): pl.pallas_call(kernel, out_shape=out, in_specs=[pl.BlockSpec(memory_space...  8.12 us
  transfers between devices with their start and end apart: 3, of which 3 were waited for; matrix products, arithmetic and copies ran while one was open for 0% of the time, Pallas kernels for 4%

profile of v6, /device:TPU:1, one launch (start us, length us, event | category | flops | bytes accessed | tf_op | source)
XLA Modules:
  0.0 74.7 jit_solution(13782137170760859692)
XLA Ops:
  0.6 0.0 copy-start.1
  0.6 2.2 %shard_map.139 = bf16[96,2,384]{2,1,0:T(2,128)(2,1)} custom-call(bf16[192,256]{1,0:T(8,128)(2,1)} %departures_hbm.1, s32[4,192]{1,0:T(4,128)} %bitcast.11, bf16[4,192]{1,0:T(4,128)(2,1)} %bitcast.12, s32[1,96]{1,0:T(1,128)} %bitcast.13, f32[8,192]{1,0:T(8,128)} %predictors_hbm.1), custom_call_target="tpu_custom_call" | custom-call | flops 40000000 | bytes 300000 | tf_op jit(solution)/shard_map/pallas_call | solution.py:193
  2.8 22.6 %all-to-all-start = ((bf16[96,2,384]{2,1,0:T(2,128)(2,1)}), bf16[96,2,384]{2,1,0:T(2,128)(2,1)S(1)}, u32[]{:S(2)}, u32[]{:S(2)}) async-start(bf16[96,2,384]{2,1,0:T(2,128)(2,1)} %shard_map.139), calls=%async_computation | async-start | bytes 294912 | tf_op jit(solution)/shard_map/all_to_all | solution.py:21
  25.4 0.0 copy-done.1
  25.4 0.0 copy-start.3
  25.4 0.0 copy-start
  25.5 13.7 %all-to-all-done = bf16[96,2,384]{2,1,0:T(2,128)(2,1)S(1)} async-done(((bf16[96,2,384]{2,1,0:T(2,128)(2,1)}), bf16[96,2,384]{2,1,0:T(2,128)(2,1)S(1)}, u32[]{:S(2)}, u32[]{:S(2)}) %all-to-all-start) | async-done | bytes 147488 | tf_op jit(solution)/shard_map/all_to_all | solution.py:21
  39.1 0.1 reshape.12.got
  39.2 0.0 copy-start.2
  39.2 1.2 %shard_map.141 = (bf16[96,2,256]{2,1,0:T(2,128)(2,1)}, bf16[192,128]{1,0:T(8,128)(2,1)S(1)}) custom-call(bf16[192,384]{1,0:T(8,128)(2,1)S(1)} %reshape.12.got, bf16[1024,128]{1,0:T(8,128)(2,1)S(1)} %shard_map.140.state), custom_call_target="tpu_custom_call" | custom-call | flops 50000000 | bytes 500000 | tf_op jit(solution)/shard_map/pallas_call | solution.py:193
  40.4 0.0 copy-start.5
  40.4 6.7 %all-to-all-start.1 = ((bf16[96,2,256]{2,1,0:T(2,128)(2,1)}), bf16[96,2,256]{2,1,0:T(2,128)(2,1)S(1)}, u32[]{:S(2)}, u32[]{:S(2)}) async-start(bf16[96,2,256]{2,1,0:T(2,128)(2,1)} %get-tuple-element.7), calls=%async_computation.1 | async-start | bytes 196608 | tf_op jit(solution)/shard_map/all_to_all | solution.py:21
  47.1 0.0 copy-start.4
  47.1 0.0 copy-start.6
  47.1 0.0 copy-done.3
  47.1 0.0 copy-done
  47.1 0.0 copy-done.2
  47.2 0.0 copy-done.5
  47.2 0.6 copy-done.4
  47.8 0.0 copy-done.6
  47.8 2.1 %shard_map.142 = (f32[1024,128]{1,0:T(8,128)}, f32[1,256]{1,0:T(1,128)S(1)}) custom-call(bf16[192,384]{1,0:T(8,128)(2,1)S(1)} %reshape.12.got, bf16[192,128]{1,0:T(8,128)(2,1)S(1)} %get-tuple-element.8.profile, bf16[128,512]{1,0:T(8,128)(2,1)S(1)} %copy-done.3, f32[1,512]{1,0:T(1,128)S(1)} %bitcast.6, bf16[512,512]{1,0:T(8,128)(2,1)S(1)} %copy-done, ...), custom_call_target="tpu_custom_call" | custom-call | flops 400000000 | bytes 2000000 | tf_op jit(solution)/shard_map/pallas_call | solution.py:193
  49.9 10.6 %all-to-all-done.1 = bf16[96,2,256]{2,1,0:T(2,128)(2,1)S(1)} async-done(((bf16[96,2,256]{2,1,0:T(2,128)(2,1)}), bf16[96,2,256]{2,1,0:T(2,128)(2,1)S(1)}, u32[]{:S(2)}, u32[]{:S(2)}) %all-to-all-start.1) | async-done | bytes 98336 | tf_op jit(solution)/shard_map/all_to_all | solution.py:21
  60.6 0.8 %shard_map.144 = f32[8,8,256]{2,1,0:T(8,128)} custom-call(bf16[192,256]{1,0:T(8,128)(2,1)S(1)} %reshape.13.back), custom_call_target="tpu_custom_call" | custom-call | flops 10000000 | bytes 200000 | tf_op jit(solution)/shard_map/pallas_call | solution.py:193
  61.4 7.9 %all-to-all-start.2 = ((f32[8,8,256]{2,1,0:T(8,128)}), f32[8,8,256]{2,1,0:T(8,128)S(1)}, u32[]{:S(2)}, u32[]{:S(2)}) async-start(f32[8,8,256]{2,1,0:T(8,128)} %shard_map.144), calls=%async_computation.2 | async-start | bytes 131072 | tf_op jit(solution)/shard_map/all_to_all | solution.py:21
  69.2 1.2 %shard_map.143 = bf16[192,256]{1,0:T(8,128)(2,1)} custom-call(bf16[192,256]{1,0:T(8,128)(2,1)S(1)} %reshape.13.back, bf16[128,512]{1,0:T(8,128)(2,1)S(1)} %copy-done.3, f32[1,512]{1,0:T(1,128)S(1)} %bitcast.7, bf16[512,512]{1,0:T(8,128)(2,1)S(1)} %copy-done, f32[1,512]{1,0:T(1,128)S(1)} %bitcast.9, bf16[512,256]{1,0:T(8,128)(2,1)S(1)} %copy-done.2, ...), custom_call_target="tpu_custom_call" | custom-call | flops 2000000000 | bytes 2000000 | tf_op jit(solution)/shard_map/pallas_call | solution.py:193
  70.4 3.6 %all-to-all-done.2.shared = f32[8,8,256]{2,1,0:T(8,128)S(1)} async-done(((f32[8,8,256]{2,1,0:T(8,128)}), f32[8,8,256]{2,1,0:T(8,128)S(1)}, u32[]{:S(2)}, u32[]{:S(2)}) %all-to-all-start.2) | async-done | bytes 65568 | tf_op jit(solution)/shard_map/all_to_all | solution.py:21
  74.1 0.6 shard_map.145
  (2 shorter events, 0.1 us)
Async XLA Ops:
  0.6 24.8 %copy-start.1 = (bf16[1024,128]{1,0:T(8,128)(2,1)S(1)}, bf16[1024,128]{1,0:T(8,128)(2,1)}, u32[]{:S(2)}) copy-start(bf16[1024,128]{1,0:T(8,128)(2,1)} %state.1) | copy-start | bytes 786436
  2.8 36.3 %all-to-all-start = ((bf16[96,2,384]{2,1,0:T(2,128)(2,1)}), bf16[96,2,384]{2,1,0:T(2,128)(2,1)S(1)}, u32[]{:S(2)}, u32[]{:S(2)}) async-start(bf16[96,2,384]{2,1,0:T(2,128)(2,1)} %shard_map.139), calls=%async_computation | async-start | bytes 294912 | tf_op jit(solution)/shard_map/all_to_all | solution.py:21
  25.4 21.7 %copy-start.3 = (bf16[128,512]{1,0:T(8,128)(2,1)S(1)}, bf16[128,512]{1,0:T(8,128)(2,1)}, u32[]{:S(2)}) copy-start(bf16[128,512]{1,0:T(8,128)(2,1)} %w_in.3) | copy-start | bytes 393220
  25.4 21.7 %copy-start = (bf16[512,512]{1,0:T(8,128)(2,1)S(1)}, bf16[512,512]{1,0:T(8,128)(2,1)}, u32[]{:S(2)}) copy-start(bf16[512,512]{1,0:T(8,128)(2,1)} %w_mid.3) | copy-start | bytes 1572868
  39.2 8.0 %copy-start.2 = (bf16[512,256]{1,0:T(8,128)(2,1)S(1)}, bf16[512,256]{1,0:T(8,128)(2,1)}, u32[]{:S(2)}) copy-start(bf16[512,256]{1,0:T(8,128)(2,1)} %w_out.3) | copy-start | bytes 786436
  40.4 6.7 %copy-start.5 = (f32[512]{0:T(512)S(1)}, f32[512]{0:T(512)}, u32[]{:S(2)}) copy-start(f32[512]{0:T(512)} %param.21) | copy-start | bytes 6148
  40.4 20.1 %all-to-all-start.1 = ((bf16[96,2,256]{2,1,0:T(2,128)(2,1)}), bf16[96,2,256]{2,1,0:T(2,128)(2,1)S(1)}, u32[]{:S(2)}, u32[]{:S(2)}) async-start(bf16[96,2,256]{2,1,0:T(2,128)(2,1)} %get-tuple-element.7), calls=%async_computation.1 | async-start | bytes 196608 | tf_op jit(solution)/shard_map/all_to_all | solution.py:21
  47.1 0.7 copy-start.4
  47.1 0.7 copy-start.6
  61.4 12.7 %all-to-all-start.2 = ((f32[8,8,256]{2,1,0:T(8,128)}), f32[8,8,256]{2,1,0:T(8,128)S(1)}, u32[]{:S(2)}, u32[]{:S(2)}) async-start(f32[8,8,256]{2,1,0:T(8,128)} %shard_map.144), calls=%async_computation.2 | async-start | bytes 131072 | tf_op jit(solution)/shard_map/all_to_all | solution.py:21

commit v7 on v5

--- a/solution.py
+++ b/solution.py
@@ -136,25 +136,38 @@
     return h1, h2
 
 
-def hidden_kernel(profile, w_in, b_in, w_mid, b_mid, w_out, b_out, h1, h2, b_kept):
+def hidden_kernel(
+    got, profile, w_in, b_in, w_mid, b_mid, w_out, b_out, slope1, slope2, spread, b_kept
+):
+    slots = got.shape[0]
     b_kept[...] = b_out[...]
-    h1[...], h2[...] = forward(profile[...], w_in, b_in, w_mid, b_mid)
+    h1, h2 = forward(profile[...], w_in, b_in, w_mid, b_mid)
+    h1, h2 = h1.astype(F32), h2.astype(F32)
+    slope1[...] = 1.0 - h1 * h1
+    slope2[...] = 1.0 - h2 * h2
+    extra = dot_dims(got[:, :LANES], identity(slots, slots), TN)
+    corner = (extra[4:5] * TILE_W + extra[5:6]).astype(I32)
+    delta = place(spread.shape, 0) - corner
+    turned = jnp.zeros(spread.shape, F32)
+    for k, offset in enumerate((0, 1, TILE_W, TILE_W + 1)):
+        turned = jnp.where(delta == offset, extra[k : k + 1], turned)
+    spread[...] = turned.astype(BF16)
 
 
 def final_kernel(
-    scale, back, got, h1, h2, even, odd, w_in, b_in, w_mid, b_mid, w_out, b_out,
-    state_grad, radiance, bias_grad
+    scale, back, spread, slope1, slope2, even, odd, w_in, b_in, w_mid, b_mid, w_out, b_out,
+    state_grad, radiance, bias_grad, grad, sent
 ):
     feat = w_in.shape[0]
     channels = bias_grad.shape[1]
-    h2f, h1f = h2[...].astype(F32), h1[...].astype(F32)
     g2 = dot_dims(back[:, feat:], w_out[...], NT)
-    g2 = (g2 * (1.0 - h2f * h2f)).astype(BF16)
+    g2 = (g2 * slope2[...]).astype(BF16)
     g1 = dot_dims(g2, w_mid[...], NT)
-    g1 = (g1 * (1.0 - h1f * h1f)).astype(BF16)
+    g1 = (g1 * slope1[...]).astype(BF16)
     dprofile = dot_dims(g1, w_in[...], NT).astype(BF16)
-    spread = spread_of(got[:, :LANES], state_grad.shape[0])
-    state_grad[...] = dot_dims(spread, dprofile, TN)
+    grad[...] = dot(spread[...], dprofile)
+    copy = pltpu.make_async_copy(grad, state_grad, sent)
+    copy.start()
 
     _, last = forward(back[:, :feat], w_in, b_in, w_mid, b_mid)
     radiance[...] = (dot(last, w_out[...]) + b_out[...]).astype(BF16)
@@ -166,14 +179,17 @@
                 bias_grad[row : row + 1, :] = (
                     half[j : j + 1, e * channels : (e + 1) * channels] * scale
                 )
-
-
-def call(kernel, out, *args, flops=0, touched=0, space=pltpu.VMEM, scratch=(), grant=GRANT):
+    copy.wait()
+
+
+def call(
+    kernel, out, *args, flops=0, touched=0, space=pltpu.VMEM, scratch=(), grant=GRANT, places=None
+):
     return pl.pallas_call(
         kernel,
         out_shape=out,
         in_specs=[pl.BlockSpec(memory_space=space)] * len(args),
-        out_specs=jax.tree.map(lambda _: pl.BlockSpec(memory_space=pltpu.VMEM), out),
+        out_specs=places or jax.tree.map(lambda _: pl.BlockSpec(memory_space=pltpu.VMEM), out),
         scratch_shapes=scratch,
         compiler_params=pltpu.CompilerParams(vmem_limit_bytes=grant),
         cost_estimate=pl.CostEstimate(flops=flops, bytes_accessed=touched, transcendentals=0),
@@ -228,9 +244,16 @@
         touched=500_000,
     )
     back = exchange(reply, "tx").reshape(slots, -1)
-    h1, h2, b_out = call(
+    hid = w_in.shape[1]
+    slope1, slope2, spread, b_out = call(
         hidden_kernel,
-        (shape((slots, w_in.shape[1]), BF16),) * 2 + (shape((1, channels), F32),),
+        (
+            shape((slots, hid), F32),
+            shape((slots, hid), F32),
+            shape((columns, slots), BF16),
+            shape((1, channels), F32),
+        ),
+        got,
         profile,
         w_in,
         b_in,
@@ -241,9 +264,7 @@
         flops=130_000_000,
         touched=1_000_000,
     )
-    terms = terms[:cap]
-    for step in (1 << k for k in range((rows - 1).bit_length())):
-        terms = terms + lax.ppermute(terms, "ty", [(b, b ^ step) for b in range(rows)])
+    terms = lax.all_gather(terms, "ty").sum(axis=0)[:cap]
     other = lax.ppermute(terms, "tx", [(a, a ^ 1) for a in range(peers)])
     is_even = lax.axis_index("tx") % 2 == 0
     even = jnp.where(is_even, terms, other)
@@ -256,9 +277,9 @@
             shape((npred, channels), F32),
         ),
         back,
-        got,
-        h1,
-        h2,
+        spread,
+        slope1,
+        slope2,
         even,
         odd,
         w_in,
@@ -269,6 +290,12 @@
         b_out,
         flops=400_000_000,
         touched=2_000_000,
+        scratch=[pltpu.VMEM((columns, feat), F32), pltpu.SemaphoreType.DMA],
+        places=(
+            pl.BlockSpec(memory_space=pl.ANY),
+            pl.BlockSpec(memory_space=pltpu.VMEM),
+            pl.BlockSpec(memory_space=pltpu.VMEM),
+        ),
     )
     return (radiance, state_grad, bias_grad)
 

time: 73.4 us -> 73.1 us (level)
  the two profiles are of different devices: /device:TPU:4 before, /device:TPU:1 now
where the time goes in v7:
time: 73.1 us; the launch traced here: 72.7 us
  starting transfers between devices  34.3 us (47%)
  waiting for transfers between devices  14.9 us (20%)
  blocking collectives  14.6 us (20%)
  Pallas kernels  7.08 us (10%)
  local copies, waits for them, and re-layouts  0.85 us (1%)
  between operations  0.85 us (1%)
    all_to_all x2, starting transfers between devices, exchange(): return lax.all_to_all(block, axis, split_axis=0, concat_axis=0, tiled=True)  31.4 us
    all_to_all x2, waiting for transfers between devices, exchange(): return lax.all_to_all(block, axis, split_axis=0, concat_axis=0, tiled=True)  14.9 us
    all_gather x1, blocking collectives, on_device(): terms = lax.all_gather(terms, 'ty').sum(axis=0)[:cap]  14.6 us
    pallas_call x5, Pallas kernels, call(): pl.pallas_call(kernel, out_shape=out, in_specs=[pl.BlockSpec(memory_space...  7.08 us
    ppermute x1, starting transfers between devices, on_device(): other = lax.ppermute(terms, 'tx', [(a, a ^ 1) for a in range(peers)])  2.98 us
  transfers between devices with their start and end apart: 3, of which 1 were waited for; matrix products, arithmetic and copies ran while one was open for 0% of the time, Pallas kernels for 2%

profile of v7, /device:TPU:1, one launch (start us, length us, event | category | flops | bytes accessed | tf_op | source)
XLA Modules:
  0.0 72.7 jit_solution(6443674144801581688)
XLA Ops:
  0.6 2.2 %shard_map.139 = bf16[96,2,640]{2,1,0:T(2,128)(2,1)} custom-call(bf16[192,256]{1,0:T(8,128)(2,1)} %departures.1, s32[4,192]{1,0:T(4,128)} %bitcast.15, bf16[4,192]{1,0:T(4,128)(2,1)} %bitcast.16, s32[1,96]{1,0:T(1,128)} %bitcast.13, f32[8,192]{1,0:T(8,128)} %predictors_hbm.1), custom_call_target="tpu_custom_call" | custom-call | flops 40000000 | bytes 300000 | tf_op jit(solution)/shard_map/pallas_call | solution.py:188
  2.9 0.0 copy-start.3
  2.9 0.0 copy-start.7
  2.9 0.0 copy-start.8
  2.9 22.7 %all-to-all-start = ((bf16[96,2,640]{2,1,0:T(2,128)(2,1)}), bf16[96,2,640]{2,1,0:T(2,128)(2,1)S(1)}, u32[]{:S(2)}, u32[]{:S(2)}) async-start(bf16[96,2,640]{2,1,0:T(2,128)(2,1)} %shard_map.139), calls=%async_computation | async-start | bytes 491520 | tf_op jit(solution)/shard_map/all_to_all | solution.py:21
  25.6 0.0 copy-done.3
  25.6 0.0 copy-done.7
  25.6 0.0 copy-done.8
  25.6 0.2 shard_map.140
  25.9 14.9 %all-to-all-done = bf16[96,2,640]{2,1,0:T(2,128)(2,1)S(1)} async-done(((bf16[96,2,640]{2,1,0:T(2,128)(2,1)}), bf16[96,2,640]{2,1,0:T(2,128)(2,1)S(1)}, u32[]{:S(2)}, u32[]{:S(2)}) %all-to-all-start) | async-done | bytes 245792 | tf_op jit(solution)/shard_map/all_to_all | solution.py:21
  40.8 0.1 reshape.12.got
  40.9 0.0 copy-start
  40.9 1.2 %shard_map.141 = (bf16[96,2,384]{2,1,0:T(2,128)(2,1)}, f32[8,512]{1,0:T(8,128)S(1)}, bf16[192,128]{1,0:T(8,128)(2,1)S(1)}) custom-call(bf16[192,640]{1,0:T(8,128)(2,1)S(1)} %reshape.12.got, bf16[192,256]{1,0:T(8,128)(2,1)S(1)} %get-tuple-element.15.dy, bf16[1024,128]{1,0:T(8,128)(2,1)S(1)} %get-tuple-element.16.state), custom_call_target="tpu_custom_call" | custom-call | flops 50000000 | bytes 500000 | tf_op jit(solution)/shard_map/pallas_call | solution.py:188
  42.1 0.0 copy-start.1
  42.1 8.7 %all-to-all-start.1 = ((bf16[96,2,384]{2,1,0:T(2,128)(2,1)}), bf16[96,2,384]{2,1,0:T(2,128)(2,1)S(1)}, u32[]{:S(2)}, u32[]{:S(2)}) async-start(bf16[96,2,384]{2,1,0:T(2,128)(2,1)} %get-tuple-element.17), calls=%async_computation.1 | async-start | bytes 294912 | tf_op jit(solution)/shard_map/all_to_all | solution.py:21
  50.8 0.0 copy-start.2
  50.8 14.6 %all-gather = f32[64,512]{1,0:T(8,128)S(1)} all-gather(f32[8,512]{1,0:T(8,128)S(1)} %get-tuple-element.22), channel_id=2, replica_groups=mesh['tx'=96,'ty'=8] {'ty'}, dimensions={0}, use_global_device_ids=true | all-gather | bytes 147456 | tf_op jit(solution)/shard_map/all_gather | solution.py:267
  65.5 3.0 %collective-permute-start = (f32[2,512]{1,0:T(2,128)S(1)}, f32[2,512]{1,0:T(2,128)S(1)}, u32[]{:S(2)}, u32[]{:S(2)}) collective-permute-start(f32[2,512]{1,0:T(2,128)S(1)} %slice.4), channel_id=1, source_target_pairs={{0,8},{8,0},{16,24},{24,16},{32,40},{40,32},{48,56},{56,48},{64,72... | collective-permute-start | bytes 12296 | tf_op jit(solution)/shard_map/ppermute | solution.py:268
  68.5 0.0 copy-start.5
  68.5 0.0 copy-start.4
  68.5 0.0 copy-start.6
  68.5 0.0 copy-done
  68.5 0.0 copy-done.1
  68.5 0.0 copy-done.2
  68.5 0.6 copy-done.5
  69.2 0.0 copy-done.4
  69.2 0.0 copy-done.6
  69.2 1.0 %shard_map.142 = (f32[192,512]{1,0:T(8,128)S(1)}, f32[192,512]{1,0:T(8,128)S(1)}, bf16[1024,192]{1,0:T(8,128)(2,1)S(1)}, f32[1,256]{1,0:T(1,128)S(1)}) custom-call(bf16[192,640]{1,0:T(8,128)(2,1)S(1)} %reshape.12.got, bf16[192,128]{1,0:T(8,128)(2,1)S(1)} %get-tuple-element.18.profile, bf16[128,512]{1,0:T(8,128)(2,1)S(1)} %copy-done.2, f32[1,512]{1,0:T(1,128)S(1)} %bitcast.8, ...), custom_call_target="tpu_custom_call" | custom-call | flops 130000000 | bytes 1000000 | tf_op jit(solution)/shard_map/pallas_call | solution.py:188
  70.2 0.0 collective-permute-done
  70.2 0.0 all-to-all-done.1
  70.2 0.1 reshape.13.back
  70.3 2.5 %shard_map.143 = (f32[1024,128]{1,0:T(8,128)}, bf16[192,256]{1,0:T(8,128)(2,1)}, f32[8,256]{1,0:T(8,128)}) custom-call(bf16[192,384]{1,0:T(8,128)(2,1)S(1)} %reshape.13.back, bf16[1024,192]{1,0:T(8,128)(2,1)S(1)} %get-tuple-element.19.spread, f32[192,512]{1,0:T(8,128)S(1)} %get-tuple-element.20.slope1, f32[192,512]{1,0:T(8,128)S(1)} %get-tuple-element.21.slope2, ...), custom_call_target="tpu_custom_call" | custom-call | flops 400000000 | bytes 2000000 | tf_op jit(solution)/shard_map/pallas_call | solution.py:188
  (3 shorter events, 0.0 us)
Async XLA Ops:
  2.9 22.7 %copy-start.3 = (bf16[192,256]{1,0:T(8,128)(2,1)S(1)}, bf16[192,256]{1,0:T(8,128)(2,1)}, u32[]{:S(2)}) copy-start(bf16[192,256]{1,0:T(8,128)(2,1)} %departures.1) | copy-start | bytes 294916
  2.9 22.7 %copy-start.7 = (s32[96]{0:T(128)S(1)}, s32[96]{0:T(128)}, u32[]{:S(2)}) copy-start(s32[96]{0:T(128)} %param.16) | copy-start | bytes 1156
  2.9 22.7 %copy-start.8 = (bf16[1024,128]{1,0:T(8,128)(2,1)S(1)}, bf16[1024,128]{1,0:T(8,128)(2,1)}, u32[]{:S(2)}) copy-start(bf16[1024,128]{1,0:T(8,128)(2,1)} %state.1) | copy-start | bytes 786436
  2.9 37.9 %all-to-all-start = ((bf16[96,2,640]{2,1,0:T(2,128)(2,1)}), bf16[96,2,640]{2,1,0:T(2,128)(2,1)S(1)}, u32[]{:S(2)}, u32[]{:S(2)}) async-start(bf16[96,2,640]{2,1,0:T(2,128)(2,1)} %shard_map.139), calls=%async_computation | async-start | bytes 491520 | tf_op jit(solution)/shard_map/all_to_all | solution.py:21
  40.9 27.6 %copy-start = (bf16[512,512]{1,0:T(8,128)(2,1)S(1)}, bf16[512,512]{1,0:T(8,128)(2,1)}, u32[]{:S(2)}) copy-start(bf16[512,512]{1,0:T(8,128)(2,1)} %w_mid.3) | copy-start | bytes 1572868
  42.1 26.4 %copy-start.1 = (bf16[512,256]{1,0:T(8,128)(2,1)S(1)}, bf16[512,256]{1,0:T(8,128)(2,1)}, u32[]{:S(2)}) copy-start(bf16[512,256]{1,0:T(8,128)(2,1)} %w_out.3) | copy-start | bytes 786436
  42.1 28.1 %all-to-all-start.1 = ((bf16[96,2,384]{2,1,0:T(2,128)(2,1)}), bf16[96,2,384]{2,1,0:T(2,128)(2,1)S(1)}, u32[]{:S(2)}, u32[]{:S(2)}) async-start(bf16[96,2,384]{2,1,0:T(2,128)(2,1)} %get-tuple-element.17), calls=%async_computation.1 | async-start | bytes 294912 | tf_op jit(solution)/shard_map/all_to_all | solution.py:21
  50.8 17.7 %copy-start.2 = (bf16[128,512]{1,0:T(8,128)(2,1)S(1)}, bf16[128,512]{1,0:T(8,128)(2,1)}, u32[]{:S(2)}) copy-start(bf16[128,512]{1,0:T(8,128)(2,1)} %w_in.3) | copy-start | bytes 393220
  65.5 4.7 %collective-permute-start = (f32[2,512]{1,0:T(2,128)S(1)}, f32[2,512]{1,0:T(2,128)S(1)}, u32[]{:S(2)}, u32[]{:S(2)}) collective-permute-start(f32[2,512]{1,0:T(2,128)S(1)} %slice.4), channel_id=1, source_target_pairs={{0,8},{8,0},{16,24},{24,16},{32,40},{40,32},{48,56},{56,48},{64,72... | collective-permute-start | bytes 12296 | tf_op jit(solution)/shard_map/ppermute | solution.py:268
  68.5 0.7 copy-start.5
  68.5 0.7 copy-start.4
  68.5 0.7 copy-start.6

commit v8 on v5

--- a/solution.py
+++ b/solution.py
@@ -52,8 +52,11 @@
     return jnp.where(live, departures[...].astype(F32), 0.0).astype(BF16)
 
 
-def keep_kernel(state, departures, counts, state_kept, dy):
+def keep_kernel(state, departures, counts, b_in, b_mid, b_out, state_kept, dy, in_kept, mid_kept, out_kept):
     state_kept[...] = state[...]
+    in_kept[...] = b_in[...]
+    mid_kept[...] = b_mid[...]
+    out_kept[...] = b_out[...]
     dy[...] = masked_by(departures, counts)
 
 
@@ -136,8 +139,8 @@
     return h1, h2
 
 
-def hidden_kernel(profile, w_in, b_in, w_mid, b_mid, w_out, b_out, h1, h2, b_kept):
-    b_kept[...] = b_out[...]
+def hidden_kernel(profile, w_in, b_in, w_mid, b_mid, w_out, h1, h2):
+    del w_out
     h1[...], h2[...] = forward(profile[...], w_in, b_in, w_mid, b_mid)
 
 
@@ -204,12 +207,16 @@
         + [pltpu.SemaphoreType.DMA((len(inputs),))],
         grant=PACK_GRANT,
     )
-    state, dy = call(
+    state, dy, b_in, b_mid, b_out = call(
         keep_kernel,
-        (shape(state.shape, BF16), shape(departures.shape, BF16)),
+        (shape(state.shape, BF16), shape(departures.shape, BF16))
+        + tuple(shape(b.shape, F32) for b in (b_in, b_mid, b_out)),
         state,
         departures,
         counts[None],
+        b_in,
+        b_mid,
+        b_out,
         flops=2_000_000_000,
         touched=2_000_000,
     )
@@ -228,22 +235,19 @@
         touched=500_000,
     )
     back = exchange(reply, "tx").reshape(slots, -1)
-    h1, h2, b_out = call(
+    h1, h2 = call(
         hidden_kernel,
-        (shape((slots, w_in.shape[1]), BF16),) * 2 + (shape((1, channels), F32),),
+        (shape((slots, w_in.shape[1]), BF16),) * 2,
         profile,
         w_in,
         b_in,
         w_mid,
         b_mid,
         w_out,
-        b_out,
         flops=130_000_000,
         touched=1_000_000,
     )
-    terms = terms[:cap]
-    for step in (1 << k for k in range((rows - 1).bit_length())):
-        terms = terms + lax.ppermute(terms, "ty", [(b, b ^ step) for b in range(rows)])
+    terms = lax.psum(terms[:cap], "ty")
     other = lax.ppermute(terms, "tx", [(a, a ^ 1) for a in range(peers)])
     is_even = lax.axis_index("tx") % 2 == 0
     even = jnp.where(is_even, terms, other)

time: 73.4 us -> 72.8 us (level)
  the two profiles are of different devices: /device:TPU:4 before, /device:TPU:8 now
where the time goes in v8:
time: 72.8 us; the launch traced here: 72.4 us
  starting transfers between devices  31.5 us (43%)
  waiting for transfers between devices  19 us (26%)
  blocking collectives  14.1 us (19%)
  Pallas kernels  6.1 us (8%)
  local copies, waits for them, and re-layouts  0.85 us (1%)
  between operations  0.83 us (1%)
    all_to_all x2, starting transfers between devices, exchange(): return lax.all_to_all(block, axis, split_axis=0, concat_axis=0, tiled=True)  28.1 us
    all_to_all x2, waiting for transfers between devices, exchange(): return lax.all_to_all(block, axis, split_axis=0, concat_axis=0, tiled=True)  17.3 us
    psum x1, blocking collectives, on_device(): terms = lax.psum(terms[:cap], 'ty')  14.1 us
    pallas_call x5, Pallas kernels, call(): pl.pallas_call(kernel, out_shape=out, in_specs=[pl.BlockSpec(memory_space...  6.1 us
    ppermute x1, starting transfers between devices, on_device(): other = lax.ppermute(terms, 'tx', [(a, a ^ 1) for a in range(peers)])  3.36 us
    ppermute x1, waiting for transfers between devices, on_device(): other = lax.ppermute(terms, 'tx', [(a, a ^ 1) for a in range(peers)])  1.69 us
  transfers between devices with their start and end apart: 3, of which 2 were waited for; matrix products, arithmetic and copies ran while one was open for 0% of the time, Pallas kernels for 1%

profile of v8, /device:TPU:8, one launch (start us, length us, event | category | flops | bytes accessed | tf_op | source)
XLA Modules:
  0.0 72.4 jit_solution(5403458891819979962)
XLA Ops:
  0.6 2.2 %shard_map.139 = bf16[96,2,640]{2,1,0:T(2,128)(2,1)} custom-call(bf16[192,256]{1,0:T(8,128)(2,1)} %departures.1, s32[4,192]{1,0:T(4,128)} %bitcast.11, bf16[4,192]{1,0:T(4,128)(2,1)} %bitcast.12, s32[1,96]{1,0:T(1,128)} %bitcast.6, f32[8,192]{1,0:T(8,128)} %predictors_hbm.1), custom_call_target="tpu_custom_call" | custom-call | flops 40000000 | bytes 300000 | tf_op jit(solution)/shard_map/pallas_call | solution.py:175
  2.9 0.0 copy-start.3
  2.9 0.0 copy-start.5
  2.9 0.0 copy-start.7
  2.9 21.9 %all-to-all-start = ((bf16[96,2,640]{2,1,0:T(2,128)(2,1)}), bf16[96,2,640]{2,1,0:T(2,128)(2,1)S(1)}, u32[]{:S(2)}, u32[]{:S(2)}) async-start(bf16[96,2,640]{2,1,0:T(2,128)(2,1)} %shard_map.139), calls=%async_computation | async-start | bytes 491520 | tf_op jit(solution)/shard_map/all_to_all | solution.py:21
  24.8 0.0 copy-start.6
  24.8 0.0 copy-start.4
  24.9 0.0 copy-start.8
  24.9 0.0 copy-done.3
  24.9 0.0 copy-done.5
  24.9 0.0 copy-done.7
  24.9 0.6 copy-done.6
  25.5 0.0 copy-done.4
  25.5 0.0 copy-done.8
  25.5 0.2 shard_map.140
  25.8 17.3 %all-to-all-done = bf16[96,2,640]{2,1,0:T(2,128)(2,1)S(1)} async-done(((bf16[96,2,640]{2,1,0:T(2,128)(2,1)}), bf16[96,2,640]{2,1,0:T(2,128)(2,1)S(1)}, u32[]{:S(2)}, u32[]{:S(2)}) %all-to-all-start) | async-done | bytes 245792 | tf_op jit(solution)/shard_map/all_to_all | solution.py:21
  43.1 0.1 reshape.12.got
  43.2 0.0 copy-start
  43.2 0.0 copy-start.2
  43.2 1.2 %shard_map.141 = (bf16[96,2,384]{2,1,0:T(2,128)(2,1)}, f32[8,512]{1,0:T(8,128)S(1)}, bf16[192,128]{1,0:T(8,128)(2,1)S(1)}) custom-call(bf16[192,640]{1,0:T(8,128)(2,1)S(1)} %reshape.12.got, bf16[192,256]{1,0:T(8,128)(2,1)S(1)} %get-tuple-element.16.dy, bf16[1024,128]{1,0:T(8,128)(2,1)S(1)} %get-tuple-element.17.state), custom_call_target="tpu_custom_call" | custom-call | flops 50000000 | bytes 500000 | tf_op jit(solution)/shard_map/pallas_call | solution.py:175
  44.4 0.0 copy-start.1
  44.4 6.2 %all-to-all-start.1 = ((bf16[96,2,384]{2,1,0:T(2,128)(2,1)}), bf16[96,2,384]{2,1,0:T(2,128)(2,1)S(1)}, u32[]{:S(2)}, u32[]{:S(2)}) async-start(bf16[96,2,384]{2,1,0:T(2,128)(2,1)} %get-tuple-element.18), calls=%async_computation.1 | async-start | bytes 294912 | tf_op jit(solution)/shard_map/all_to_all | solution.py:21
  50.7 14.1 %psum.7 = f32[2,512]{1,0:T(2,128)S(1)} all-reduce(f32[2,512]{1,0:T(2,128)S(1)} %slice.3), channel_id=1, replica_groups=mesh['tx'=96,'ty'=8] {'ty'}, use_global_device_ids=true, to_apply=%region_0.0 | all-reduce | flops 1024 | bytes 8192 | tf_op jit(solution)/shard_map/psum | solution.py:250
  64.8 3.4 %collective-permute-start = (f32[2,512]{1,0:T(2,128)S(1)}, f32[2,512]{1,0:T(2,128)S(1)}, u32[]{:S(2)}, u32[]{:S(2)}) collective-permute-start(f32[2,512]{1,0:T(2,128)S(1)} %psum.7), channel_id=1, source_target_pairs={{0,8},{8,0},{16,24},{24,16},{32,40},{40,32},{48,56},{56,48},{64,72... | collective-permute-start | bytes 12296 | tf_op jit(solution)/shard_map/ppermute | solution.py:251
  68.2 0.0 copy-done
  68.2 0.0 copy-done.2
  68.2 0.0 copy-done.1
  68.2 0.4 shard_map.142
  68.6 1.7 %collective-permute-done = f32[2,512]{1,0:T(2,128)S(1)} collective-permute-done((f32[2,512]{1,0:T(2,128)S(1)}, f32[2,512]{1,0:T(2,128)S(1)}, u32[]{:S(2)}, u32[]{:S(2)}) %collective-permute-start) | collective-permute-done | bytes 4128 | tf_op jit(solution)/shard_map/ppermute | solution.py:251
  70.3 0.0 all-to-all-done.1
  70.3 0.1 reshape.13.back
  70.4 2.0 %shard_map.143 = (f32[1024,128]{1,0:T(8,128)}, bf16[192,256]{1,0:T(8,128)(2,1)}, f32[8,256]{1,0:T(8,128)}) custom-call(bf16[192,384]{1,0:T(8,128)(2,1)S(1)} %reshape.13.back, bf16[192,640]{1,0:T(8,128)(2,1)S(1)} %reshape.12.got, bf16[192,512]{1,0:T(8,128)(2,1)S(1)} %get-tuple-element.22.h1, bf16[192,512]{1,0:T(8,128)(2,1)S(1)} %get-tuple-element.23.h2, ...), custom_call_target="tpu_custom_call" | custom-call | flops 400000000 | bytes 2000000 | tf_op jit(solution)/shard_map/pallas_call | solution.py:175
  (2 shorter events, 0.0 us)
Async XLA Ops:
  2.9 22.0 %copy-start.3 = (bf16[192,256]{1,0:T(8,128)(2,1)S(1)}, bf16[192,256]{1,0:T(8,128)(2,1)}, u32[]{:S(2)}) copy-start(bf16[192,256]{1,0:T(8,128)(2,1)} %departures.1) | copy-start | bytes 294916
  2.9 22.0 %copy-start.5 = (bf16[1024,128]{1,0:T(8,128)(2,1)S(1)}, bf16[1024,128]{1,0:T(8,128)(2,1)}, u32[]{:S(2)}) copy-start(bf16[1024,128]{1,0:T(8,128)(2,1)} %state.1) | copy-start | bytes 786436
  2.9 22.0 %copy-start.7 = (f32[512]{0:T(512)S(1)}, f32[512]{0:T(512)}, u32[]{:S(2)}) copy-start(f32[512]{0:T(512)} %param.21) | copy-start | bytes 6148
  2.9 40.2 %all-to-all-start = ((bf16[96,2,640]{2,1,0:T(2,128)(2,1)}), bf16[96,2,640]{2,1,0:T(2,128)(2,1)S(1)}, u32[]{:S(2)}, u32[]{:S(2)}) async-start(bf16[96,2,640]{2,1,0:T(2,128)(2,1)} %shard_map.139), calls=%async_computation | async-start | bytes 491520 | tf_op jit(solution)/shard_map/all_to_all | solution.py:21
  24.8 0.7 copy-start.6
  24.8 0.7 copy-start.4
  24.9 0.7 copy-start.8
  43.2 25.0 %copy-start = (bf16[512,512]{1,0:T(8,128)(2,1)S(1)}, bf16[512,512]{1,0:T(8,128)(2,1)}, u32[]{:S(2)}) copy-start(bf16[512,512]{1,0:T(8,128)(2,1)} %w_mid.3) | copy-start | bytes 1572868
  43.2 25.0 %copy-start.2 = (bf16[128,512]{1,0:T(8,128)(2,1)S(1)}, bf16[128,512]{1,0:T(8,128)(2,1)}, u32[]{:S(2)}) copy-start(bf16[128,512]{1,0:T(8,128)(2,1)} %w_in.3) | copy-start | bytes 393220
  44.4 23.8 %copy-start.1 = (bf16[512,256]{1,0:T(8,128)(2,1)S(1)}, bf16[512,256]{1,0:T(8,128)(2,1)}, u32[]{:S(2)}) copy-start(bf16[512,256]{1,0:T(8,128)(2,1)} %w_out.3) | copy-start | bytes 786436
  44.4 25.9 %all-to-all-start.1 = ((bf16[96,2,384]{2,1,0:T(2,128)(2,1)}), bf16[96,2,384]{2,1,0:T(2,128)(2,1)S(1)}, u32[]{:S(2)}, u32[]{:S(2)}) async-start(bf16[96,2,384]{2,1,0:T(2,128)(2,1)} %get-tuple-element.18), calls=%async_computation.1 | async-start | bytes 294912 | tf_op jit(solution)/shard_map/all_to_all | solution.py:21
  64.8 5.5 %collective-permute-start = (f32[2,512]{1,0:T(2,128)S(1)}, f32[2,512]{1,0:T(2,128)S(1)}, u32[]{:S(2)}, u32[]{:S(2)}) collective-permute-start(f32[2,512]{1,0:T(2,128)S(1)} %psum.7), channel_id=1, source_target_pairs={{0,8},{8,0},{16,24},{24,16},{32,40},{40,32},{48,56},{56,48},{64,72... | collective-permute-start | bytes 12296 | tf_op jit(solution)/shard_map/ppermute | solution.py:251

commit v9 on v8

--- a/solution.py
+++ b/solution.py
@@ -145,11 +145,9 @@
 
 
 def final_kernel(
-    scale, back, got, h1, h2, even, odd, w_in, b_in, w_mid, b_mid, w_out, b_out,
-    state_grad, radiance, bias_grad
+    back, got, h1, h2, w_in, b_in, w_mid, b_mid, w_out, b_out, state_grad, radiance, one
 ):
     feat = w_in.shape[0]
-    channels = bias_grad.shape[1]
     h2f, h1f = h2[...].astype(F32), h1[...].astype(F32)
     g2 = dot_dims(back[:, feat:], w_out[...], NT)
     g2 = (g2 * (1.0 - h2f * h2f)).astype(BF16)
@@ -161,7 +159,12 @@
 
     _, last = forward(back[:, :feat], w_in, b_in, w_mid, b_mid)
     radiance[...] = (dot(last, w_out[...]) + b_out[...]).astype(BF16)
-
+    one[...] = jnp.ones(one.shape, F32)
+
+
+def bias_kernel(scale, one, even, odd, bias_grad):
+    channels = bias_grad.shape[1]
+    scale = one[0:1, 0:1] * scale
     for k, half in enumerate((even, odd)):
         for j in range(2):
             for e in range(2):
@@ -248,31 +251,35 @@
         touched=1_000_000,
     )
     terms = lax.psum(terms[:cap], "ty")
+    terms, back = lax.optimization_barrier((terms, back))
     other = lax.ppermute(terms, "tx", [(a, a ^ 1) for a in range(peers)])
     is_even = lax.axis_index("tx") % 2 == 0
     even = jnp.where(is_even, terms, other)
     odd = jnp.where(is_even, other, terms)
-    state_grad, radiance, bias_grad = call(
-        functools.partial(final_kernel, scale),
-        (
-            shape((columns, feat), F32),
-            shape((slots, channels), BF16),
-            shape((npred, channels), F32),
-        ),
+    state_grad, radiance, one = call(
+        final_kernel,
+        (shape((columns, feat), F32), shape((slots, channels), BF16), shape((8, LANES), F32)),
         back,
         got,
         h1,
         h2,
-        even,
-        odd,
         w_in,
         b_in,
         w_mid,
         b_mid,
         w_out,
         b_out,
-        flops=400_000_000,
+        flops=3_000_000_000,
         touched=2_000_000,
+    )
+    bias_grad = call(
+        functools.partial(bias_kernel, scale),
+        shape((npred, channels), F32),
+        one,
+        even,
+        odd,
+        flops=2_000,
+        touched=20_000,
     )
     return (radiance, state_grad, bias_grad)
 

time: 72.8 us -> 72.8 us (level)
  the two profiles are of different devices: /device:TPU:8 before, /device:TPU:4 now
where the time goes in v9:
time: 72.8 us; the launch traced here: 72.4 us
  starting transfers between devices  30.8 us (42%)
  waiting for transfers between devices  22.6 us (31%)
  blocking collectives  10.6 us (15%)
  Pallas kernels  6.78 us (9%)
  local copies, waits for them, and re-layouts  0.85 us (1%)
  between operations  0.82 us (1%)
    all_to_all x2, starting transfers between devices, exchange(): return lax.all_to_all(block, axis, split_axis=0, concat_axis=0, tiled=True)  28.2 us
    all_to_all x2, waiting for transfers between devices, exchange(): return lax.all_to_all(block, axis, split_axis=0, concat_axis=0, tiled=True)  21.7 us
    psum x1, blocking collectives, on_device(): terms = lax.psum(terms[:cap], 'ty')  10.6 us
    pallas_call x6, Pallas kernels, call(): pl.pallas_call(kernel, out_shape=out, in_specs=[pl.BlockSpec(memory_space...  6.78 us
    ppermute x1, starting transfers between devices, on_device(): other = lax.ppermute(terms, 'tx', [(a, a ^ 1) for a in range(peers)])  2.61 us
  transfers between devices with their start and end apart: 3, of which 3 were waited for; matrix products, arithmetic and copies ran while one was open for 0% of the time, Pallas kernels for 4%

profile of v9, /device:TPU:4, one launch (start us, length us, event | category | flops | bytes accessed | tf_op | source)
XLA Modules:
  0.0 72.4 jit_solution(11501437338416341396)
XLA Ops:
  0.6 2.2 %shard_map.139 = bf16[96,2,640]{2,1,0:T(2,128)(2,1)} custom-call(bf16[192,256]{1,0:T(8,128)(2,1)} %departures.1, s32[4,192]{1,0:T(4,128)} %bitcast.11, bf16[4,192]{1,0:T(4,128)(2,1)} %bitcast.12, s32[1,96]{1,0:T(1,128)} %bitcast.6, f32[8,192]{1,0:T(8,128)} %predictors_hbm.1), custom_call_target="tpu_custom_call" | custom-call | flops 40000000 | bytes 300000 | tf_op jit(solution)/shard_map/pallas_call | solution.py:178
  2.9 0.0 copy-start.3
  2.9 0.0 copy-start.5
  2.9 0.0 copy-start.7
  2.9 22.1 %all-to-all-start = ((bf16[96,2,640]{2,1,0:T(2,128)(2,1)}), bf16[96,2,640]{2,1,0:T(2,128)(2,1)S(1)}, u32[]{:S(2)}, u32[]{:S(2)}) async-start(bf16[96,2,640]{2,1,0:T(2,128)(2,1)} %shard_map.139), calls=%async_computation | async-start | bytes 491520 | tf_op jit(solution)/shard_map/all_to_all | solution.py:21
  25.0 0.0 copy-start.6
  25.1 0.0 copy-start.4
  25.1 0.0 copy-start.8
  25.1 0.0 copy-done.3
  25.1 0.0 copy-done.5
  25.1 0.0 copy-done.7
  25.1 0.6 copy-done.6
  25.7 0.0 copy-done.4
  25.7 0.0 copy-done.8
  25.8 0.2 shard_map.140
  26.0 17.5 %all-to-all-done = bf16[96,2,640]{2,1,0:T(2,128)(2,1)S(1)} async-done(((bf16[96,2,640]{2,1,0:T(2,128)(2,1)}), bf16[96,2,640]{2,1,0:T(2,128)(2,1)S(1)}, u32[]{:S(2)}, u32[]{:S(2)}) %all-to-all-start) | async-done | bytes 245792 | tf_op jit(solution)/shard_map/all_to_all | solution.py:21
  43.5 0.1 reshape.12.got
  43.6 0.0 copy-start
  43.6 0.0 copy-start.2
  43.6 1.2 %shard_map.141 = (bf16[96,2,384]{2,1,0:T(2,128)(2,1)}, f32[8,512]{1,0:T(8,128)S(1)}, bf16[192,128]{1,0:T(8,128)(2,1)S(1)}) custom-call(bf16[192,640]{1,0:T(8,128)(2,1)S(1)} %reshape.12.got, bf16[192,256]{1,0:T(8,128)(2,1)S(1)} %get-tuple-element.18.dy, bf16[1024,128]{1,0:T(8,128)(2,1)S(1)} %get-tuple-element.19.state), custom_call_target="tpu_custom_call" | custom-call | flops 50000000 | bytes 500000 | tf_op jit(solution)/shard_map/pallas_call | solution.py:178
  44.8 0.0 copy-start.1
  44.8 6.1 %all-to-all-start.1 = ((bf16[96,2,384]{2,1,0:T(2,128)(2,1)}), bf16[96,2,384]{2,1,0:T(2,128)(2,1)S(1)}, u32[]{:S(2)}, u32[]{:S(2)}) async-start(bf16[96,2,384]{2,1,0:T(2,128)(2,1)} %get-tuple-element.21), calls=%async_computation.1 | async-start | bytes 294912 | tf_op jit(solution)/shard_map/all_to_all | solution.py:21
  50.9 10.6 %psum.7 = f32[2,512]{1,0:T(2,128)S(1)} all-reduce(f32[2,512]{1,0:T(2,128)S(1)} %slice.3), channel_id=1, replica_groups=mesh['tx'=96,'ty'=8] {'ty'}, use_global_device_ids=true, to_apply=%region_0.0 | all-reduce | flops 1024 | bytes 8192 | tf_op jit(solution)/shard_map/psum | solution.py:253
  61.5 0.0 copy-done
  61.5 0.0 copy-done.2
  61.5 0.0 copy-done.1
  61.5 0.4 shard_map.142
  62.0 4.3 %all-to-all-done.1 = bf16[96,2,384]{2,1,0:T(2,128)(2,1)S(1)} async-done(((bf16[96,2,384]{2,1,0:T(2,128)(2,1)}), bf16[96,2,384]{2,1,0:T(2,128)(2,1)S(1)}, u32[]{:S(2)}, u32[]{:S(2)}) %all-to-all-start.1) | async-done | bytes 147488 | tf_op jit(solution)/shard_map/all_to_all | solution.py:21
  66.2 0.1 reshape.13.back
  66.3 2.6 %collective-permute-start = (f32[2,512]{1,0:T(2,128)S(1)}, f32[2,512]{1,0:T(2,128)S(1)}, u32[]{:S(2)}, u32[]{:S(2)}) collective-permute-start(f32[2,512]{1,0:T(2,128)S(1)} %psum.7), channel_id=1, source_target_pairs={{0,8},{8,0},{16,24},{24,16},{32,40},{40,32},{48,56},{56,48},{64,72... | collective-permute-start | bytes 12296 | tf_op jit(solution)/shard_map/ppermute | solution.py:255
  68.9 2.0 %shard_map.143 = (f32[1024,128]{1,0:T(8,128)}, bf16[192,256]{1,0:T(8,128)(2,1)}, f32[8,128]{1,0:T(8,128)S(1)}) custom-call(bf16[192,384]{1,0:T(8,128)(2,1)S(1)} %reshape.13.back, bf16[192,640]{1,0:T(8,128)(2,1)S(1)} %reshape.12.got, bf16[192,512]{1,0:T(8,128)(2,1)S(1)} %get-tuple-element.26.h1, bf16[192,512]{1,0:T(8,128)(2,1)S(1)} %get-tuple-element.27.h2, ...), custom_call_target="tpu_custom_call" | custom-call | flops 3000000000 | bytes 2000000 | tf_op jit(solution)/shard_map/pallas_call | solution.py:178
  70.9 0.8 %collective-permute-done = f32[2,512]{1,0:T(2,128)S(1)} collective-permute-done((f32[2,512]{1,0:T(2,128)S(1)}, f32[2,512]{1,0:T(2,128)S(1)}, u32[]{:S(2)}, u32[]{:S(2)}) %collective-permute-start) | collective-permute-done | bytes 4128 | tf_op jit(solution)/shard_map/ppermute | solution.py:255
  71.8 0.7 shard_map.144
  (2 shorter events, 0.0 us)
Async XLA Ops:
  2.9 22.2 %copy-start.3 = (bf16[192,256]{1,0:T(8,128)(2,1)S(1)}, bf16[192,256]{1,0:T(8,128)(2,1)}, u32[]{:S(2)}) copy-start(bf16[192,256]{1,0:T(8,128)(2,1)} %departures.1) | copy-start | bytes 294916
  2.9 22.2 %copy-start.5 = (bf16[1024,128]{1,0:T(8,128)(2,1)S(1)}, bf16[1024,128]{1,0:T(8,128)(2,1)}, u32[]{:S(2)}) copy-start(bf16[1024,128]{1,0:T(8,128)(2,1)} %state.1) | copy-start | bytes 786436
  2.9 22.2 %copy-start.7 = (f32[512]{0:T(512)S(1)}, f32[512]{0:T(512)}, u32[]{:S(2)}) copy-start(f32[512]{0:T(512)} %param.21) | copy-start | bytes 6148
  2.9 40.6 %all-to-all-start = ((bf16[96,2,640]{2,1,0:T(2,128)(2,1)}), bf16[96,2,640]{2,1,0:T(2,128)(2,1)S(1)}, u32[]{:S(2)}, u32[]{:S(2)}) async-start(bf16[96,2,640]{2,1,0:T(2,128)(2,1)} %shard_map.139), calls=%async_computation | async-start | bytes 491520 | tf_op jit(solution)/shard_map/all_to_all | solution.py:21
  25.0 0.7 copy-start.6
  25.1 0.7 copy-start.4
  25.1 0.7 copy-start.8
  43.6 18.0 %copy-start = (bf16[512,512]{1,0:T(8,128)(2,1)S(1)}, bf16[512,512]{1,0:T(8,128)(2,1)}, u32[]{:S(2)}) copy-start(bf16[512,512]{1,0:T(8,128)(2,1)} %w_mid.3) | copy-start | bytes 1572868
  43.6 18.0 %copy-start.2 = (bf16[128,512]{1,0:T(8,128)(2,1)S(1)}, bf16[128,512]{1,0:T(8,128)(2,1)}, u32[]{:S(2)}) copy-start(bf16[128,512]{1,0:T(8,128)(2,1)} %w_in.3) | copy-start | bytes 393220
  44.8 16.7 %copy-start.1 = (bf16[512,256]{1,0:T(8,128)(2,1)S(1)}, bf16[512,256]{1,0:T(8,128)(2,1)}, u32[]{:S(2)}) copy-start(bf16[512,256]{1,0:T(8,128)(2,1)} %w_out.3) | copy-start | bytes 786436
  44.8 21.4 %all-to-all-start.1 = ((bf16[96,2,384]{2,1,0:T(2,128)(2,1)}), bf16[96,2,384]{2,1,0:T(2,128)(2,1)S(1)}, u32[]{:S(2)}, u32[]{:S(2)}) async-start(bf16[96,2,384]{2,1,0:T(2,128)(2,1)} %get-tuple-element.21), calls=%async_computation.1 | async-start | bytes 294912 | tf_op jit(solution)/shard_map/all_to_all | solution.py:21
  66.3 5.5 %collective-permute-start = (f32[2,512]{1,0:T(2,128)S(1)}, f32[2,512]{1,0:T(2,128)S(1)}, u32[]{:S(2)}, u32[]{:S(2)}) collective-permute-start(f32[2,512]{1,0:T(2,128)S(1)} %psum.7), channel_id=1, source_target_pairs={{0,8},{8,0},{16,24},{24,16},{32,40},{40,32},{48,56},{56,48},{64,72... | collective-permute-start | bytes 12296 | tf_op jit(solution)/shard_map/ppermute | solution.py:255

commit v10 on v8

--- a/solution.py
+++ b/solution.py
@@ -60,9 +60,9 @@
     dy[...] = masked_by(departures, counts)
 
 
-def pack_kernel(
-    departures_hbm, stencil_hbm, bilinear_hbm, counts_hbm, predictors_hbm, out,
-    departures, stencil, bilinear, counts, predictors, arrived
+def partial_kernel(
+    departures_hbm, counts_hbm, predictors_hbm, stencil_hbm, bilinear_hbm, own, other, meta,
+    departures, counts, predictors, stencil, bilinear, arrived
 ):
     pairs = (
         (counts_hbm, counts),
@@ -77,37 +77,45 @@
     ]
     for copy in copies:
         copy.start()
-    slots, channels = departures.shape
-    peers = counts.shape[1]
-    cap = slots // peers
-    npred = predictors.shape[0]
-    turn = identity(slots, slots)
     for copy in copies:
         copy.wait()
+    npred = predictors.shape[0]
     dy = masked_by(departures, counts)
-
     pred = predictors[...]
     part0 = rounded(pred)
     part1 = rounded(pred - part0)
     part2 = pred - part0 - part1
     thirds = dot(jnp.concatenate([part0, part1, part2], axis=0).astype(BF16), dy)
     partial = thirds[:npred] + thirds[npred : 2 * npred] + thirds[2 * npred :]
-    slot = place((slots, npred), 0) % (2 * cap) * 2
-    which = place((slots, npred), 1)
-    partial = partial.astype(BF16)
-    for k in range(2):
-        chosen = (which == slot + k).astype(F32).astype(BF16)
-        out[:, :, LANES + k * channels : LANES + (k + 1) * channels] = (
-            dot(chosen, partial).astype(BF16).reshape(peers, cap, channels)
-        )
-
+    half = npred // 2
+    first = lax.axis_index("ty") % 2 == 0
+    own[...] = jnp.where(first, partial[:half], partial[half:])
+    other[...] = jnp.where(first, partial[half:], partial[:half])
+    slots = departures.shape[0]
     corner = stencil[0:1, :]
     column = jnp.bitwise_and(corner, TILE_W - 1)
     row = (corner - column) // TILE_W
     rows = [bilinear[...].astype(F32), row.astype(F32), column.astype(F32)]
     rows.append(jnp.zeros((LANES - 6, slots), F32))
     extra = jnp.concatenate(rows, axis=0).astype(BF16)
-    out[:, :, :LANES] = dot_dims(turn, extra, NT).astype(BF16).reshape(peers, cap, LANES)
+    extra = dot_dims(identity(slots, slots), extra, NT).astype(BF16)
+    meta[...] = extra
+
+
+def pack_kernel(meta, own, given, out):
+    peers, cap = out.shape[:2]
+    slots = peers * cap
+    half, channels = own.shape
+    joined = own[...] + given[...]
+    joined = jnp.concatenate([joined, jnp.zeros((8 - half, channels), F32)], axis=0).astype(BF16)
+    slot = place((slots, 8), 0) % cap * 2
+    which = place((slots, 8), 1)
+    for k in range(2):
+        chosen = (which == slot + k).astype(F32).astype(BF16)
+        out[:, :, LANES + k * channels : LANES + (k + 1) * channels] = (
+            dot(chosen, joined).astype(BF16).reshape(peers, cap, channels)
+        )
+    out[:, :, :LANES] = meta[...].reshape(peers, cap, LANES)
 
 
 def spread_of(extra, columns):
@@ -145,7 +153,7 @@
 
 
 def final_kernel(
-    scale, back, got, h1, h2, even, odd, w_in, b_in, w_mid, b_mid, w_out, b_out,
+    scale, back, got, h1, h2, terms, w_in, b_in, w_mid, b_mid, w_out, b_out,
     state_grad, radiance, bias_grad
 ):
     feat = w_in.shape[0]
@@ -162,13 +170,12 @@
     _, last = forward(back[:, :feat], w_in, b_in, w_mid, b_mid)
     radiance[...] = (dot(last, w_out[...]) + b_out[...]).astype(BF16)
 
-    for k, half in enumerate((even, odd)):
-        for j in range(2):
-            for e in range(2):
-                row = 4 * k + 2 * j + e
-                bias_grad[row : row + 1, :] = (
-                    half[j : j + 1, e * channels : (e + 1) * channels] * scale
-                )
+    for j in range(terms.shape[0]):
+        for e in range(2):
+            row = 2 * j + e
+            bias_grad[row : row + 1, :] = (
+                terms[j : j + 1, e * channels : (e + 1) * channels] * scale
+            )
 
 
 def call(kernel, out, *args, flops=0, touched=0, space=pltpu.VMEM, scratch=(), grant=GRANT):
@@ -195,17 +202,27 @@
     b_in, b_mid, b_out = b_in[None], b_mid[None], b_out[None]
     shape = jax.ShapeDtypeStruct
 
-    inputs = (departures, stencil.T, bilinear.T, counts[None], predictors)
-    packed = call(
-        pack_kernel,
-        shape((peers, cap, LANES + 2 * channels), BF16),
+    inputs = (departures, counts[None], predictors, stencil.T, bilinear.T)
+    own, other, meta = call(
+        partial_kernel,
+        (shape((npred // 2, channels), F32),) * 2 + (shape((slots, LANES), BF16),),
         *inputs,
-        flops=40_000_000,
-        touched=300_000,
+        flops=20_000_000,
+        touched=200_000,
         space=pl.ANY,
         scratch=[pltpu.VMEM(a.shape, a.dtype) for a in inputs]
         + [pltpu.SemaphoreType.DMA((len(inputs),))],
         grant=PACK_GRANT,
+    )
+    given = lax.ppermute(other, "ty", [(b, b ^ 1) for b in range(rows)])
+    packed = call(
+        pack_kernel,
+        shape((peers, cap, LANES + 2 * channels), BF16),
+        meta,
+        own,
+        given,
+        flops=20_000_000,
+        touched=300_000,
     )
     state, dy, b_in, b_mid, b_out = call(
         keep_kernel,
@@ -247,11 +264,11 @@
         flops=130_000_000,
         touched=1_000_000,
     )
-    terms = lax.psum(terms[:cap], "ty")
-    other = lax.ppermute(terms, "tx", [(a, a ^ 1) for a in range(peers)])
-    is_even = lax.axis_index("tx") % 2 == 0
-    even = jnp.where(is_even, terms, other)
-    odd = jnp.where(is_even, other, terms)
+    terms = terms[:cap]
+    first = lax.axis_index("ty") % 2 == 0
+    even = jnp.where(first, terms, 0.0)
+    odd = jnp.where(first, 0.0, terms)
+    terms = lax.psum(jnp.concatenate([even, odd], axis=0), "ty")
     state_grad, radiance, bias_grad = call(
         functools.partial(final_kernel, scale),
         (
@@ -263,8 +280,7 @@
         got,
         h1,
         h2,
-        even,
-        odd,
+        terms,
         w_in,
         b_in,
         w_mid,

time: 72.8 us -> 73.8 us (1.014)
  the two profiles are of different devices: /device:TPU:8 before, /device:TPU:4 now
where the time goes in v10:
time: 73.8 us; the launch traced here: 73.4 us
  starting transfers between devices  30.2 us (41%)
  waiting for transfers between devices  23.2 us (31%)
  blocking collectives  10.9 us (15%)
  Pallas kernels  6.68 us (9%)
  local copies, waits for them, and re-layouts  1.64 us (2%)
  between operations  0.82 us (1%)
    all_to_all x2, starting transfers between devices, exchange(): return lax.all_to_all(block, axis, split_axis=0, concat_axis=0, tiled=True)  28.2 us
    all_to_all x2, waiting for transfers between devices, exchange(): return lax.all_to_all(block, axis, split_axis=0, concat_axis=0, tiled=True)  21.8 us
    psum x1, blocking collectives, on_device(): terms = lax.psum(jnp.concatenate([even, odd], axis=0), 'ty')  10.9 us
    pallas_call x6, Pallas kernels, call(): pl.pallas_call(kernel, out_shape=out, in_specs=[pl.BlockSpec(memory_space...  6.68 us
    ppermute x1, starting transfers between devices, on_device(): given = lax.ppermute(other, 'ty', [(b, b ^ 1) for b in range(rows)])  1.92 us
    unnamed x22, local copies, waits for them, and re-layouts  1.49 us
  transfers between devices with their start and end apart: 3, of which 3 were waited for; matrix products, arithmetic and copies ran while one was open for 0% of the time, Pallas kernels for 1%

profile of v10, /device:TPU:4, one launch (start us, length us, event | category | flops | bytes accessed | tf_op | source)
XLA Modules:
  0.0 73.4 jit_solution(12002936568416717631)
XLA Ops:
  0.6 1.9 %shard_map.139 = (f32[4,256]{1,0:T(4,128)}, f32[4,256]{1,0:T(4,128)}, bf16[192,128]{1,0:T(8,128)(2,1)}) custom-call(bf16[192,256]{1,0:T(8,128)(2,1)} %departures.1, s32[1,96]{1,0:T(1,128)} %bitcast.6, f32[8,192]{1,0:T(8,128)} %predictors_hbm.1, s32[4,192]{1,0:T(4,128)} %bitcast.11, bf16[4,192]{1,0:T(4,128)(2,1)} %bitcast.12), custom_call_target="tpu_custom_call" | custom-call | flops 20000000 | bytes 200000 | tf_op jit(solution)/shard_map/pallas_call | solution.py:182
  2.6 0.0 copy-start.5
  2.6 1.9 %collective-permute-start = (f32[4,256]{1,0:T(4,128)}, f32[4,256]{1,0:T(4,128)S(1)}, u32[]{:S(2)}, u32[]{:S(2)}) collective-permute-start(f32[4,256]{1,0:T(4,128)} %get-tuple-element.21), channel_id=1, source_target_pairs={{0,1},{1,0},{2,3},{3,2},{4,5},{5,4},{6,7},{7,6},{8,9},{9,8},{10,11... | collective-permute-start | bytes 12296 | tf_op jit(solution)/shard_map/ppermute | solution.py:217
  4.5 1.3 %collective-permute-done.given = f32[4,256]{1,0:T(4,128)S(1)} collective-permute-done((f32[4,256]{1,0:T(4,128)}, f32[4,256]{1,0:T(4,128)S(1)}, u32[]{:S(2)}, u32[]{:S(2)}) %collective-permute-start) | collective-permute-done | bytes 4128 | tf_op jit(solution)/shard_map/ppermute | solution.py:217
  5.9 0.0 copy-done.5
  5.9 0.0 copy-start.4
  5.9 0.8 %copy-done.4 = bf16[192,128]{1,0:T(8,128)(2,1)S(1)} copy-done((bf16[192,128]{1,0:T(8,128)(2,1)S(1)}, bf16[192,128]{1,0:T(8,128)(2,1)}, u32[]{:S(2)}) %copy-start.4) | copy-done | bytes 49176
  6.7 0.9 %shard_map.140 = bf16[96,2,640]{2,1,0:T(2,128)(2,1)} custom-call(bf16[192,128]{1,0:T(8,128)(2,1)S(1)} %copy-done.4, f32[4,256]{1,0:T(4,128)S(1)} %copy-done.5, f32[4,256]{1,0:T(4,128)S(1)} %collective-permute-done.given), custom_call_target="tpu_custom_call" | custom-call | flops 20000000 | bytes 300000 | tf_op jit(solution)/shard_map/pallas_call | solution.py:182
  7.5 0.0 copy-start.3
  7.6 0.0 copy-start.7
  7.6 0.0 copy-start.9
  7.6 22.1 %all-to-all-start = ((bf16[96,2,640]{2,1,0:T(2,128)(2,1)}), bf16[96,2,640]{2,1,0:T(2,128)(2,1)S(1)}, u32[]{:S(2)}, u32[]{:S(2)}) async-start(bf16[96,2,640]{2,1,0:T(2,128)(2,1)} %shard_map.140), calls=%async_computation | async-start | bytes 491520 | tf_op jit(solution)/shard_map/all_to_all | solution.py:21
  29.7 0.0 copy-start.8
  29.7 0.0 copy-start.6
  29.7 0.0 copy-start.10
  29.7 0.0 copy-done.3
  29.7 0.0 copy-done.7
  29.7 0.0 copy-done.9
  29.8 0.6 copy-done.8
  30.4 0.0 copy-done.6
  30.4 0.0 copy-done.10
  30.4 0.2 shard_map.141
  30.6 17.8 %all-to-all-done = bf16[96,2,640]{2,1,0:T(2,128)(2,1)S(1)} async-done(((bf16[96,2,640]{2,1,0:T(2,128)(2,1)}), bf16[96,2,640]{2,1,0:T(2,128)(2,1)S(1)}, u32[]{:S(2)}, u32[]{:S(2)}) %all-to-all-start) | async-done | bytes 245792 | tf_op jit(solution)/shard_map/all_to_all | solution.py:21
  48.4 0.1 reshape.12.got
  48.5 0.0 copy-start
  48.5 0.0 copy-start.2
  48.5 1.2 %shard_map.142 = (bf16[96,2,384]{2,1,0:T(2,128)(2,1)}, f32[8,512]{1,0:T(8,128)S(1)}, bf16[192,128]{1,0:T(8,128)(2,1)S(1)}) custom-call(bf16[192,640]{1,0:T(8,128)(2,1)S(1)} %reshape.12.got, bf16[192,256]{1,0:T(8,128)(2,1)S(1)} %get-tuple-element.22.dy, bf16[1024,128]{1,0:T(8,128)(2,1)S(1)} %get-tuple-element.23.state), custom_call_target="tpu_custom_call" | custom-call | flops 50000000 | bytes 500000 | tf_op jit(solution)/shard_map/pallas_call | solution.py:182
  49.7 0.0 copy-start.1
  49.7 6.1 %all-to-all-start.1 = ((bf16[96,2,384]{2,1,0:T(2,128)(2,1)}), bf16[96,2,384]{2,1,0:T(2,128)(2,1)S(1)}, u32[]{:S(2)}, u32[]{:S(2)}) async-start(bf16[96,2,384]{2,1,0:T(2,128)(2,1)} %get-tuple-element.24), calls=%async_computation.1 | async-start | bytes 294912 | tf_op jit(solution)/shard_map/all_to_all | solution.py:21
  55.9 10.9 %psum.7.terms = f32[4,512]{1,0:T(4,128)S(1)} all-reduce(f32[4,512]{1,0:T(4,128)S(1)} %pad_maximum_fusion), channel_id=1, replica_groups=mesh['tx'=96,'ty'=8] {'ty'}, use_global_device_ids=true, to_apply=%region_0.1 | all-reduce | flops 2048 | bytes 16384 | tf_op jit(solution)/shard_map/psum | solution.py:271
  66.8 0.0 copy-done
  66.8 0.0 copy-done.2
  66.8 0.0 copy-done.1
  66.8 0.4 shard_map.143
  67.2 4.1 %all-to-all-done.1 = bf16[96,2,384]{2,1,0:T(2,128)(2,1)S(1)} async-done(((bf16[96,2,384]{2,1,0:T(2,128)(2,1)}), bf16[96,2,384]{2,1,0:T(2,128)(2,1)S(1)}, u32[]{:S(2)}, u32[]{:S(2)}) %all-to-all-start.1) | async-done | bytes 147488 | tf_op jit(solution)/shard_map/all_to_all | solution.py:21
  71.3 0.1 reshape.13.back
  71.3 2.0 %shard_map.144 = (f32[1024,128]{1,0:T(8,128)}, bf16[192,256]{1,0:T(8,128)(2,1)}, f32[8,256]{1,0:T(8,128)}) custom-call(bf16[192,384]{1,0:T(8,128)(2,1)S(1)} %reshape.13.back, bf16[192,640]{1,0:T(8,128)(2,1)S(1)} %reshape.12.got, bf16[192,512]{1,0:T(8,128)(2,1)S(1)} %get-tuple-element.28.h1, bf16[192,512]{1,0:T(8,128)(2,1)S(1)} %get-tuple-element.29.h2, ...), custom_call_target="tpu_custom_call" | custom-call | flops 400000000 | bytes 2000000 | tf_op jit(solution)/shard_map/pallas_call | solution.py:182
  (2 shorter events, 0.0 us)
Async XLA Ops:
  2.6 3.3 %copy-start.5 = (f32[4,256]{1,0:T(4,128)S(1)}, f32[4,256]{1,0:T(4,128)}, u32[]{:S(2)}) copy-start(f32[4,256]{1,0:T(4,128)} %get-tuple-element.20.own) | copy-start | bytes 12292
  2.6 3.3 %collective-permute-start = (f32[4,256]{1,0:T(4,128)}, f32[4,256]{1,0:T(4,128)S(1)}, u32[]{:S(2)}, u32[]{:S(2)}) collective-permute-start(f32[4,256]{1,0:T(4,128)} %get-tuple-element.21), channel_id=1, source_target_pairs={{0,1},{1,0},{2,3},{3,2},{4,5},{5,4},{6,7},{7,6},{8,9},{9,8},{10,11... | collective-permute-start | bytes 12296 | tf_op jit(solution)/shard_map/ppermute | solution.py:217
  5.9 0.8 %copy-start.4 = (bf16[192,128]{1,0:T(8,128)(2,1)S(1)}, bf16[192,128]{1,0:T(8,128)(2,1)}, u32[]{:S(2)}) copy-start(bf16[192,128]{1,0:T(8,128)(2,1)} %get-tuple-element.19.meta) | copy-start | bytes 147460
  7.5 22.2 %copy-start.3 = (bf16[192,256]{1,0:T(8,128)(2,1)S(1)}, bf16[192,256]{1,0:T(8,128)(2,1)}, u32[]{:S(2)}) copy-start(bf16[192,256]{1,0:T(8,128)(2,1)} %departures.1) | copy-start | bytes 294916
  7.6 22.2 %copy-start.7 = (bf16[1024,128]{1,0:T(8,128)(2,1)S(1)}, bf16[1024,128]{1,0:T(8,128)(2,1)}, u32[]{:S(2)}) copy-start(bf16[1024,128]{1,0:T(8,128)(2,1)} %state.1) | copy-start | bytes 786436
  7.6 22.2 %copy-start.9 = (f32[512]{0:T(512)S(1)}, f32[512]{0:T(512)}, u32[]{:S(2)}) copy-start(f32[512]{0:T(512)} %param.21) | copy-start | bytes 6148
  7.6 40.8 %all-to-all-start = ((bf16[96,2,640]{2,1,0:T(2,128)(2,1)}), bf16[96,2,640]{2,1,0:T(2,128)(2,1)S(1)}, u32[]{:S(2)}, u32[]{:S(2)}) async-start(bf16[96,2,640]{2,1,0:T(2,128)(2,1)} %shard_map.140), calls=%async_computation | async-start | bytes 491520 | tf_op jit(solution)/shard_map/all_to_all | solution.py:21
  29.7 0.7 copy-start.8
  29.7 0.7 copy-start.6
  29.7 0.7 copy-start.10
  48.5 18.3 %copy-start = (bf16[512,512]{1,0:T(8,128)(2,1)S(1)}, bf16[512,512]{1,0:T(8,128)(2,1)}, u32[]{:S(2)}) copy-start(bf16[512,512]{1,0:T(8,128)(2,1)} %w_mid.3) | copy-start | bytes 1572868
  48.5 18.3 %copy-start.2 = (bf16[128,512]{1,0:T(8,128)(2,1)S(1)}, bf16[128,512]{1,0:T(8,128)(2,1)}, u32[]{:S(2)}) copy-start(bf16[128,512]{1,0:T(8,128)(2,1)} %w_in.3) | copy-start | bytes 393220
  49.7 17.1 %copy-start.1 = (bf16[512,256]{1,0:T(8,128)(2,1)S(1)}, bf16[512,256]{1,0:T(8,128)(2,1)}, u32[]{:S(2)}) copy-start(bf16[512,256]{1,0:T(8,128)(2,1)} %w_out.3) | copy-start | bytes 786436
  49.7 21.5 %all-to-all-start.1 = ((bf16[96,2,384]{2,1,0:T(2,128)(2,1)}), bf16[96,2,384]{2,1,0:T(2,128)(2,1)S(1)}, u32[]{:S(2)}, u32[]{:S(2)}) async-start(bf16[96,2,384]{2,1,0:T(2,128)(2,1)} %get-tuple-element.24), calls=%async_computation.1 | async-start | bytes 294912 | tf_op jit(solution)/shard_map/all_to_all | solution.py:21

commit v11 on v8

--- a/solution.py
+++ b/solution.py
@@ -247,7 +247,7 @@
         flops=130_000_000,
         touched=1_000_000,
     )
-    terms = lax.psum(terms[:cap], "ty")
+    terms = lax.all_gather(terms[:cap], "ty").sum(axis=0)
     other = lax.ppermute(terms, "tx", [(a, a ^ 1) for a in range(peers)])
     is_even = lax.axis_index("tx") % 2 == 0
     even = jnp.where(is_even, terms, other)

time: 72.8 us -> 72.2 us (level)
  the two profiles are of different devices: /device:TPU:8 before, /device:TPU:1 now
where the time goes in v11:
time: 72.2 us; the launch traced here: 71.9 us
  starting transfers between devices  34.3 us (48%)
  waiting for transfers between devices  15.2 us (21%)
  blocking collectives  14.5 us (20%)
  Pallas kernels  6.09 us (8%)
  local copies, waits for them, and re-layouts  0.86 us (1%)
  between operations  0.83 us (1%)
    all_to_all x2, starting transfers between devices, exchange(): return lax.all_to_all(block, axis, split_axis=0, concat_axis=0, tiled=True)  31.4 us
    all_gather x1, blocking collectives, on_device(): terms = lax.all_gather(terms[:cap], 'ty').sum(axis=0)  14.5 us
    all_to_all x2, waiting for transfers between devices, exchange(): return lax.all_to_all(block, axis, split_axis=0, concat_axis=0, tiled=True)  14.2 us
    pallas_call x5, Pallas kernels, call(): pl.pallas_call(kernel, out_shape=out, in_specs=[pl.BlockSpec(memory_space...  6.09 us
    ppermute x1, starting transfers between devices, on_device(): other = lax.ppermute(terms, 'tx', [(a, a ^ 1) for a in range(peers)])  2.98 us
  transfers between devices with their start and end apart: 3, of which 2 were waited for; matrix products, arithmetic and copies ran while one was open for 0% of the time, Pallas kernels for 1%

profile of v11, /device:TPU:1, one launch (start us, length us, event | category | flops | bytes accessed | tf_op | source)
XLA Modules:
  0.0 71.9 jit_solution(16324972073485080730)
XLA Ops:
  0.6 2.2 %shard_map.139 = bf16[96,2,640]{2,1,0:T(2,128)(2,1)} custom-call(bf16[192,256]{1,0:T(8,128)(2,1)} %departures.1, s32[4,192]{1,0:T(4,128)} %bitcast.13, bf16[4,192]{1,0:T(4,128)(2,1)} %bitcast.14, s32[1,96]{1,0:T(1,128)} %bitcast.8, f32[8,192]{1,0:T(8,128)} %predictors_hbm.1), custom_call_target="tpu_custom_call" | custom-call | flops 40000000 | bytes 300000 | tf_op jit(solution)/shard_map/pallas_call | solution.py:175
  2.9 0.0 copy-start.3
  2.9 0.0 copy-start.5
  2.9 22.7 %all-to-all-start = ((bf16[96,2,640]{2,1,0:T(2,128)(2,1)}), bf16[96,2,640]{2,1,0:T(2,128)(2,1)S(1)}, u32[]{:S(2)}, u32[]{:S(2)}) async-start(bf16[96,2,640]{2,1,0:T(2,128)(2,1)} %shard_map.139), calls=%async_computation | async-start | bytes 491520 | tf_op jit(solution)/shard_map/all_to_all | solution.py:21
  25.6 0.0 copy-start.7
  25.6 0.0 copy-start.6
  25.6 0.0 copy-start.4
  25.6 0.0 copy-start.8
  25.6 0.0 copy-done.3
  25.7 0.0 copy-done.5
  25.7 0.6 copy-done.7
  26.3 0.0 copy-done.6
  26.3 0.0 copy-done.4
  26.3 0.0 copy-done.8
  26.3 0.2 shard_map.140
  26.6 14.2 %all-to-all-done = bf16[96,2,640]{2,1,0:T(2,128)(2,1)S(1)} async-done(((bf16[96,2,640]{2,1,0:T(2,128)(2,1)}), bf16[96,2,640]{2,1,0:T(2,128)(2,1)S(1)}, u32[]{:S(2)}, u32[]{:S(2)}) %all-to-all-start) | async-done | bytes 245792 | tf_op jit(solution)/shard_map/all_to_all | solution.py:21
  40.8 0.1 reshape.12.got
  40.9 0.0 copy-start
  40.9 0.0 copy-start.2
  40.9 1.2 %shard_map.141 = (bf16[96,2,384]{2,1,0:T(2,128)(2,1)}, f32[8,512]{1,0:T(8,128)S(1)}, bf16[192,128]{1,0:T(8,128)(2,1)S(1)}) custom-call(bf16[192,640]{1,0:T(8,128)(2,1)S(1)} %reshape.12.got, bf16[192,256]{1,0:T(8,128)(2,1)S(1)} %get-tuple-element.16.dy, bf16[1024,128]{1,0:T(8,128)(2,1)S(1)} %get-tuple-element.17.state), custom_call_target="tpu_custom_call" | custom-call | flops 50000000 | bytes 500000 | tf_op jit(solution)/shard_map/pallas_call | solution.py:175
  42.1 0.0 copy-start.1
  42.1 8.7 %all-to-all-start.1 = ((bf16[96,2,384]{2,1,0:T(2,128)(2,1)}), bf16[96,2,384]{2,1,0:T(2,128)(2,1)S(1)}, u32[]{:S(2)}, u32[]{:S(2)}) async-start(bf16[96,2,384]{2,1,0:T(2,128)(2,1)} %get-tuple-element.18), calls=%async_computation.1 | async-start | bytes 294912 | tf_op jit(solution)/shard_map/all_to_all | solution.py:21
  50.8 14.5 %all-gather.1 = f32[8,2,512]{2,1,0:T(2,128)S(1)} all-gather(f32[1,2,512]{2,1,0:T(2,128)S(1)} %slice_bitcast_fusion), channel_id=2, replica_groups=mesh['tx'=96,'ty'=8] {'ty'}, dimensions={0}, use_global_device_ids=true | all-gather | bytes 36864 | tf_op jit(solution)/shard_map/all_gather | solution.py:250
  65.4 3.0 %collective-permute-start = (f32[2,512]{1,0:T(2,128)S(1)}, f32[2,512]{1,0:T(2,128)S(1)}, u32[]{:S(2)}, u32[]{:S(2)}) collective-permute-start(f32[2,512]{1,0:T(2,128)S(1)} %reduce_sum.9), channel_id=1, source_target_pairs={{0,8},{8,0},{16,24},{24,16},{32,40},{40,32},{48,56},{56,48},{64,72... | collective-permute-start | bytes 12296 | tf_op jit(solution)/shard_map/ppermute | solution.py:251
  68.4 0.0 copy-done
  68.4 0.0 copy-done.2
  68.4 0.0 copy-done.1
  68.4 0.4 shard_map.142
  68.8 0.9 %collective-permute-done = f32[2,512]{1,0:T(2,128)S(1)} collective-permute-done((f32[2,512]{1,0:T(2,128)S(1)}, f32[2,512]{1,0:T(2,128)S(1)}, u32[]{:S(2)}, u32[]{:S(2)}) %collective-permute-start) | collective-permute-done | bytes 4128 | tf_op jit(solution)/shard_map/ppermute | solution.py:251
  69.7 0.0 all-to-all-done.1
  69.8 0.1 reshape.13.back
  69.8 2.0 %shard_map.143 = (f32[1024,128]{1,0:T(8,128)}, bf16[192,256]{1,0:T(8,128)(2,1)}, f32[8,256]{1,0:T(8,128)}) custom-call(bf16[192,384]{1,0:T(8,128)(2,1)S(1)} %reshape.13.back, bf16[192,640]{1,0:T(8,128)(2,1)S(1)} %reshape.12.got, bf16[192,512]{1,0:T(8,128)(2,1)S(1)} %get-tuple-element.22.h1, bf16[192,512]{1,0:T(8,128)(2,1)S(1)} %get-tuple-element.23.h2, ...), custom_call_target="tpu_custom_call" | custom-call | flops 400000000 | bytes 2000000 | tf_op jit(solution)/shard_map/pallas_call | solution.py:175
  (3 shorter events, 0.0 us)
Async XLA Ops:
  2.9 22.8 %copy-start.3 = (bf16[192,256]{1,0:T(8,128)(2,1)S(1)}, bf16[192,256]{1,0:T(8,128)(2,1)}, u32[]{:S(2)}) copy-start(bf16[192,256]{1,0:T(8,128)(2,1)} %departures.1) | copy-start | bytes 294916
  2.9 22.8 %copy-start.5 = (bf16[1024,128]{1,0:T(8,128)(2,1)S(1)}, bf16[1024,128]{1,0:T(8,128)(2,1)}, u32[]{:S(2)}) copy-start(bf16[1024,128]{1,0:T(8,128)(2,1)} %state.1) | copy-start | bytes 786436
  2.9 37.9 %all-to-all-start = ((bf16[96,2,640]{2,1,0:T(2,128)(2,1)}), bf16[96,2,640]{2,1,0:T(2,128)(2,1)S(1)}, u32[]{:S(2)}, u32[]{:S(2)}) async-start(bf16[96,2,640]{2,1,0:T(2,128)(2,1)} %shard_map.139), calls=%async_computation | async-start | bytes 491520 | tf_op jit(solution)/shard_map/all_to_all | solution.py:21
  25.6 0.7 copy-start.7
  25.6 0.7 copy-start.6
  25.6 0.7 copy-start.4
  25.6 0.7 copy-start.8
  40.9 27.5 %copy-start = (bf16[512,512]{1,0:T(8,128)(2,1)S(1)}, bf16[512,512]{1,0:T(8,128)(2,1)}, u32[]{:S(2)}) copy-start(bf16[512,512]{1,0:T(8,128)(2,1)} %w_mid.3) | copy-start | bytes 1572868
  40.9 27.5 %copy-start.2 = (bf16[128,512]{1,0:T(8,128)(2,1)S(1)}, bf16[128,512]{1,0:T(8,128)(2,1)}, u32[]{:S(2)}) copy-start(bf16[128,512]{1,0:T(8,128)(2,1)} %w_in.3) | copy-start | bytes 393220
  42.1 26.3 %copy-start.1 = (bf16[512,256]{1,0:T(8,128)(2,1)S(1)}, bf16[512,256]{1,0:T(8,128)(2,1)}, u32[]{:S(2)}) copy-start(bf16[512,256]{1,0:T(8,128)(2,1)} %w_out.3) | copy-start | bytes 786436
  42.1 27.6 %all-to-all-start.1 = ((bf16[96,2,384]{2,1,0:T(2,128)(2,1)}), bf16[96,2,384]{2,1,0:T(2,128)(2,1)S(1)}, u32[]{:S(2)}, u32[]{:S(2)}) async-start(bf16[96,2,384]{2,1,0:T(2,128)(2,1)} %get-tuple-element.18), calls=%async_computation.1 | async-start | bytes 294912 | tf_op jit(solution)/shard_map/all_to_all | solution.py:21
  65.4 4.4 %collective-permute-start = (f32[2,512]{1,0:T(2,128)S(1)}, f32[2,512]{1,0:T(2,128)S(1)}, u32[]{:S(2)}, u32[]{:S(2)}) collective-permute-start(f32[2,512]{1,0:T(2,128)S(1)} %reduce_sum.9), channel_id=1, source_target_pairs={{0,8},{8,0},{16,24},{24,16},{32,40},{40,32},{48,56},{56,48},{64,72... | collective-permute-start | bytes 12296 | tf_op jit(solution)/shard_map/ppermute | solution.py:251

commit v12 on v9

--- a/solution.py
+++ b/solution.py
@@ -250,7 +250,7 @@
         flops=130_000_000,
         touched=1_000_000,
     )
-    terms = lax.psum(terms[:cap], "ty")
+    terms = lax.all_gather(terms[:cap], "ty").sum(axis=0)
     terms, back = lax.optimization_barrier((terms, back))
     other = lax.ppermute(terms, "tx", [(a, a ^ 1) for a in range(peers)])
     is_even = lax.axis_index("tx") % 2 == 0

time: 72.8 us -> 72.8 us (level)
  the two profiles are of different devices: /device:TPU:4 before, /device:TPU:1 now
where the time goes in v12:
time: 72.8 us; the launch traced here: 71.6 us
  starting transfers between devices  34.3 us (47%)
  blocking collectives  14.5 us (20%)
  waiting for transfers between devices  14.3 us (20%)
  Pallas kernels  6.78 us (9%)
  local copies, waits for them, and re-layouts  0.85 us (1%)
  between operations  0.83 us (1%)
    all_to_all x2, starting transfers between devices, exchange(): return lax.all_to_all(block, axis, split_axis=0, concat_axis=0, tiled=True)  31.4 us
    all_gather x1, blocking collectives, on_device(): terms = lax.all_gather(terms[:cap], 'ty').sum(axis=0)  14.5 us
    all_to_all x2, waiting for transfers between devices, exchange(): return lax.all_to_all(block, axis, split_axis=0, concat_axis=0, tiled=True)  14.3 us
    pallas_call x6, Pallas kernels, call(): pl.pallas_call(kernel, out_shape=out, in_specs=[pl.BlockSpec(memory_space...  6.78 us
    ppermute x1, starting transfers between devices, on_device(): other = lax.ppermute(terms, 'tx', [(a, a ^ 1) for a in range(peers)])  2.98 us
  transfers between devices with their start and end apart: 3, of which 1 were waited for; matrix products, arithmetic and copies ran while one was open for 0% of the time, Pallas kernels for 4%

profile of v12, /device:TPU:1, one launch (start us, length us, event | category | flops | bytes accessed | tf_op | source)
XLA Modules:
  0.0 71.6 jit_solution(1496308095023809473)
XLA Ops:
  0.6 2.2 %shard_map.139 = bf16[96,2,640]{2,1,0:T(2,128)(2,1)} custom-call(bf16[192,256]{1,0:T(8,128)(2,1)} %departures.1, s32[4,192]{1,0:T(4,128)} %bitcast.13, bf16[4,192]{1,0:T(4,128)(2,1)} %bitcast.14, s32[1,96]{1,0:T(1,128)} %bitcast.8, f32[8,192]{1,0:T(8,128)} %predictors_hbm.1), custom_call_target="tpu_custom_call" | custom-call | flops 40000000 | bytes 300000 | tf_op jit(solution)/shard_map/pallas_call | solution.py:178
  2.9 0.0 copy-start.3
  2.9 0.0 copy-start.5
  2.9 0.0 copy-start.7
  2.9 22.7 %all-to-all-start = ((bf16[96,2,640]{2,1,0:T(2,128)(2,1)}), bf16[96,2,640]{2,1,0:T(2,128)(2,1)S(1)}, u32[]{:S(2)}, u32[]{:S(2)}) async-start(bf16[96,2,640]{2,1,0:T(2,128)(2,1)} %shard_map.139), calls=%async_computation | async-start | bytes 491520 | tf_op jit(solution)/shard_map/all_to_all | solution.py:21
  25.6 0.0 copy-start.6
  25.6 0.0 copy-start.4
  25.6 0.0 copy-start.8
  25.6 0.0 copy-done.3
  25.6 0.0 copy-done.5
  25.7 0.0 copy-done.7
  25.7 0.6 copy-done.6
  26.3 0.0 copy-done.4
  26.3 0.0 copy-done.8
  26.3 0.2 shard_map.140
  26.5 14.3 %all-to-all-done = bf16[96,2,640]{2,1,0:T(2,128)(2,1)S(1)} async-done(((bf16[96,2,640]{2,1,0:T(2,128)(2,1)}), bf16[96,2,640]{2,1,0:T(2,128)(2,1)S(1)}, u32[]{:S(2)}, u32[]{:S(2)}) %all-to-all-start) | async-done | bytes 245792 | tf_op jit(solution)/shard_map/all_to_all | solution.py:21
  40.8 0.1 reshape.12.got
  40.9 0.0 copy-start
  40.9 1.2 %shard_map.141 = (bf16[96,2,384]{2,1,0:T(2,128)(2,1)}, f32[8,512]{1,0:T(8,128)S(1)}, bf16[192,128]{1,0:T(8,128)(2,1)S(1)}) custom-call(bf16[192,640]{1,0:T(8,128)(2,1)S(1)} %reshape.12.got, bf16[192,256]{1,0:T(8,128)(2,1)S(1)} %get-tuple-element.18.dy, bf16[1024,128]{1,0:T(8,128)(2,1)S(1)} %get-tuple-element.19.state), custom_call_target="tpu_custom_call" | custom-call | flops 50000000 | bytes 500000 | tf_op jit(solution)/shard_map/pallas_call | solution.py:178
  42.1 0.0 copy-start.1
  42.1 0.0 copy-start.2
  42.1 8.7 %all-to-all-start.1 = ((bf16[96,2,384]{2,1,0:T(2,128)(2,1)}), bf16[96,2,384]{2,1,0:T(2,128)(2,1)S(1)}, u32[]{:S(2)}, u32[]{:S(2)}) async-start(bf16[96,2,384]{2,1,0:T(2,128)(2,1)} %get-tuple-element.21), calls=%async_computation.1 | async-start | bytes 294912 | tf_op jit(solution)/shard_map/all_to_all | solution.py:21
  50.8 14.5 %all-gather.1 = f32[8,2,512]{2,1,0:T(2,128)S(1)} all-gather(f32[1,2,512]{2,1,0:T(2,128)S(1)} %slice_bitcast_fusion), channel_id=2, replica_groups=mesh['tx'=96,'ty'=8] {'ty'}, dimensions={0}, use_global_device_ids=true | all-gather | bytes 36864 | tf_op jit(solution)/shard_map/all_gather | solution.py:253
  65.4 0.0 copy-done
  65.4 0.0 copy-done.1
  65.4 0.0 copy-done.2
  65.4 0.4 shard_map.142
  65.8 0.0 all-to-all-done.1
  65.8 0.1 reshape.13.back
  65.9 3.0 %collective-permute-start = (f32[2,512]{1,0:T(2,128)S(1)}, f32[2,512]{1,0:T(2,128)S(1)}, u32[]{:S(2)}, u32[]{:S(2)}) collective-permute-start(f32[2,512]{1,0:T(2,128)S(1)} %reduce_sum.9), channel_id=1, source_target_pairs={{0,8},{8,0},{16,24},{24,16},{32,40},{40,32},{48,56},{56,48},{64,72... | collective-permute-start | bytes 12296 | tf_op jit(solution)/shard_map/ppermute | solution.py:255
  68.9 2.0 %shard_map.143 = (f32[1024,128]{1,0:T(8,128)}, bf16[192,256]{1,0:T(8,128)(2,1)}, f32[8,128]{1,0:T(8,128)S(1)}) custom-call(bf16[192,384]{1,0:T(8,128)(2,1)S(1)} %reshape.13.back, bf16[192,640]{1,0:T(8,128)(2,1)S(1)} %reshape.12.got, bf16[192,512]{1,0:T(8,128)(2,1)S(1)} %get-tuple-element.26.h1, bf16[192,512]{1,0:T(8,128)(2,1)S(1)} %get-tuple-element.27.h2, ...), custom_call_target="tpu_custom_call" | custom-call | flops 3000000000 | bytes 2000000 | tf_op jit(solution)/shard_map/pallas_call | solution.py:178
  70.9 0.0 collective-permute-done
  71.0 0.7 shard_map.144
  (3 shorter events, 0.0 us)
Async XLA Ops:
  2.9 22.8 %copy-start.3 = (bf16[192,256]{1,0:T(8,128)(2,1)S(1)}, bf16[192,256]{1,0:T(8,128)(2,1)}, u32[]{:S(2)}) copy-start(bf16[192,256]{1,0:T(8,128)(2,1)} %departures.1) | copy-start | bytes 294916
  2.9 22.8 %copy-start.5 = (bf16[1024,128]{1,0:T(8,128)(2,1)S(1)}, bf16[1024,128]{1,0:T(8,128)(2,1)}, u32[]{:S(2)}) copy-start(bf16[1024,128]{1,0:T(8,128)(2,1)} %state.1) | copy-start | bytes 786436
  2.9 22.8 %copy-start.7 = (f32[512]{0:T(512)S(1)}, f32[512]{0:T(512)}, u32[]{:S(2)}) copy-start(f32[512]{0:T(512)} %param.21) | copy-start | bytes 6148
  2.9 37.9 %all-to-all-start = ((bf16[96,2,640]{2,1,0:T(2,128)(2,1)}), bf16[96,2,640]{2,1,0:T(2,128)(2,1)S(1)}, u32[]{:S(2)}, u32[]{:S(2)}) async-start(bf16[96,2,640]{2,1,0:T(2,128)(2,1)} %shard_map.139), calls=%async_computation | async-start | bytes 491520 | tf_op jit(solution)/shard_map/all_to_all | solution.py:21
  25.6 0.7 copy-start.6
  25.6 0.7 copy-start.4
  25.6 0.7 copy-start.8
  40.9 24.5 %copy-start = (bf16[512,512]{1,0:T(8,128)(2,1)S(1)}, bf16[512,512]{1,0:T(8,128)(2,1)}, u32[]{:S(2)}) copy-start(bf16[512,512]{1,0:T(8,128)(2,1)} %w_mid.3) | copy-start | bytes 1572868
  42.1 23.3 %copy-start.1 = (bf16[512,256]{1,0:T(8,128)(2,1)S(1)}, bf16[512,256]{1,0:T(8,128)(2,1)}, u32[]{:S(2)}) copy-start(bf16[512,256]{1,0:T(8,128)(2,1)} %w_out.3) | copy-start | bytes 786436
  42.1 23.3 %copy-start.2 = (bf16[128,512]{1,0:T(8,128)(2,1)S(1)}, bf16[128,512]{1,0:T(8,128)(2,1)}, u32[]{:S(2)}) copy-start(bf16[128,512]{1,0:T(8,128)(2,1)} %w_in.3) | copy-start | bytes 393220
  42.1 23.7 %all-to-all-start.1 = ((bf16[96,2,384]{2,1,0:T(2,128)(2,1)}), bf16[96,2,384]{2,1,0:T(2,128)(2,1)S(1)}, u32[]{:S(2)}, u32[]{:S(2)}) async-start(bf16[96,2,384]{2,1,0:T(2,128)(2,1)} %get-tuple-element.21), calls=%async_computation.1 | async-start | bytes 294912 | tf_op jit(solution)/shard_map/all_to_all | solution.py:21
  65.9 5.0 %collective-permute-start = (f32[2,512]{1,0:T(2,128)S(1)}, f32[2,512]{1,0:T(2,128)S(1)}, u32[]{:S(2)}, u32[]{:S(2)}) collective-permute-start(f32[2,512]{1,0:T(2,128)S(1)} %reduce_sum.9), channel_id=1, source_target_pairs={{0,8},{8,0},{16,24},{24,16},{32,40},{40,32},{48,56},{56,48},{64,72... | collective-permute-start | bytes 12296 | tf_op jit(solution)/shard_map/ppermute | solution.py:255
